TPU v7x, 512 devices: a whole 4x4x16 slice. The times are simulated.
512 devices in a mesh: row: 32 (over x, y, core), col: 16 (over z).
Axes of the slice: x: 4, y: 4, z: 16, core: 2. Of those that a mesh axis runs over, the one named last changes fastest.
Arguments:
- vectors: float32 [2, 128, 128, 8192], P(None, 'row', None, 'col'), may hold values from -120 to 120
- potential: int32 [4, 128, 128], replicated, may hold values from 0 to 4095
Outputs:
- renewed: float32 [2, 128, 128, 8192], P(None, 'row', None, 'col')
- growth: float32 [8192], P('col')
All inputs are finite; a program needn't handle non-finite values.
Results may differ from a plain program's by a relative error of at most 0.00016.
Values sent between devices are 32-bit elements; how exact they have to be, the bound alone decides.
No kernel may reach another device: no remote copies, remote signals or barrier semaphores. Data moves between devices by JAX's collectives and lax.ppermute only.
A program may use at most 64 MiB of HBM per device.

v0:
```python
import jax
import jax.numpy as jnp
from jax import lax
from jax.sharding import PartitionSpec as P

PANEL = 128
PANELS = 2
LEVELS = 4096


energy = 0.25
disorder = 16.5
tiny = 1e-06
highest = lax.Precision.HIGHEST


def with_halo(block, sides, width):
    for axis, dim in sides:
        count = lax.axis_size(axis)
        forward = [(i, i + 1) for i in range(count - 1)]
        forward.append((count - 1, 0))
        backward = [(target, source) for source, target in forward]
        low = lax.ppermute(
            lax.slice_in_dim(block, block.shape[dim] - width, None, axis=dim), axis, forward
        )
        high = lax.ppermute(lax.slice_in_dim(block, 0, width, axis=dim), axis, backward)
        block = jnp.concatenate([low, block, high], axis=dim)
    return block


def broadcast(array, axis, root):
    mine = lax.axis_index(axis) == root
    return lax.psum(jnp.where(mine, array, jnp.zeros_like(array)), axis)


def site_values(codes):
    return disorder * ((codes.astype(jnp.float32) + 0.5) / LEVELS - 0.5)


def contract(left, right):
    return lax.dot_general(
        left, right, (((0,), (0,)), ((), ())), precision=highest, preferred_element_type=jnp.float32
    )


def advance(padded, earlier, values):
    center = padded[1:-1]
    beside = padded[2:] + padded[:-2] + jnp.roll(center, 1, axis=1) + jnp.roll(center, -1, axis=1)
    return (energy - values[:, :, None]) * center - beside - earlier


def on_device(vectors, potential):
    depth = potential.shape[0]
    local_rows = vectors.shape[1]
    row_index = lax.axis_index("row")
    values_all = site_values(potential)
    own_values = lax.dynamic_slice_in_dim(values_all, row_index * local_rows, local_rows, 1)
    current = vectors[0]
    previous = vectors[1]
    for step in range(depth):
        padded = with_halo(current, (("row", 0),), 1)
        fresh = advance(padded, previous, own_values[step])
        previous = current
        current = fresh
    stacked = jnp.stack([current, previous])
    columns = stacked.shape[-1]
    matrix = stacked.reshape(-1, columns)
    total_rows = matrix.shape[0] * lax.axis_size("row")
    squares = lax.psum(jnp.sum(matrix * matrix, 0), "row")
    scale = jnp.sqrt(squares / total_rows + tiny)
    growth = jnp.log(scale)
    matrix = matrix / scale
    col_index = lax.axis_index("col")
    local_cols = jnp.arange(columns)
    for panel in range(PANELS):
        raw = matrix[:, :PANEL]
        gram = lax.psum(contract(raw, raw), "row") / total_rows
        lower = jnp.linalg.cholesky(gram)
        basis = lax.linalg.triangular_solve(
            lower, raw, left_side=False, lower=True, transpose_a=True
        )
        basis = broadcast(basis, "col", panel)
        coeffs = lax.psum(contract(basis, matrix), "row") / total_rows
        update = matrix - jnp.dot(
            basis, coeffs, precision=highest, preferred_element_type=jnp.float32
        )
        keep = (local_cols < PANEL) & (col_index <= panel)
        matrix = jnp.where(keep[None, :], matrix, update)
        matrix = matrix.at[:, :PANEL].set(jnp.where(col_index == panel, basis, matrix[:, :PANEL]))
    return (matrix.reshape(stacked.shape), growth)


def solution(mesh):
    return jax.shard_map(
        on_device,
        mesh=mesh,
        in_specs=(P(None, "row", None, "col"), P()),
        out_specs=(P(None, "row", None, "col"), P("col")),
        check_vma=False,
    )
```

profile of v0, /device:TPU:1, one launch (start us, length us, event | category | flops | bytes accessed | tf_op | source)
XLA Modules:
  0.0 1002.0 jit_solution(246488487386533440)
XLA Ops:
  7.2 1.8 slice_bitcast_fusion.2
  9.0 8.8 collective-permute-start
  17.8 1.9 collective-permute-start.1
  19.7 1.3 slice_bitcast_fusion
  21.0 1.5 fusion.59
  22.5 0.7 fusion.40
  23.4 2.0 fusion.22
  25.4 7.5 collective-permute-start.2
  32.9 1.9 collective-permute-start.3
  34.8 0.2 fusion.56
  35.1 3.0 collective-permute-done.3
  38.1 0.4 fusion.17
  38.5 7.7 collective-permute-start.4
  46.2 1.9 collective-permute-start.5
  48.2 0.2 fusion.53
  48.4 3.0 collective-permute-done.5
  51.5 0.3 fusion.12
  51.8 7.7 collective-permute-start.6
  59.6 1.9 collective-permute-start.7
  61.5 0.2 fusion.50
  61.8 3.0 collective-permute-done.7
  64.8 0.3 fusion.7
  65.1 0.3 multiply_reduce_fusion
  65.4 1.8 copy.16
  67.2 67.8 %psum.49 = f32[512]{0:T(512)S(1)} all-reduce(f32[512]{0:T(512)S(1)} %get-tuple-element.32), channel_id=1, replica_groups=mesh['row'=32,'col'=16] {'row'}, use_global_device_ids=true, to_apply=%region_1.2 | all-reduce | flops 512 | bytes 4096 | tf_op jit(solution)/shard_map/psum | solution.py:69
  135.1 0.6 log_multiply_fusion
  135.6 1.8 broadcast_divide_fusion
  137.5 1.2 fusion.25
  138.7 0.0 all-reduce.9.cloned.1.call-start
  138.8 125.4 %all-reduce.7.cloned.1.call-done = f32[128,128]{0,1:T(8,128)} async-done(((f32[128,128]{0,1:T(8,128)}), f32[128,128]{0,1:T(8,128)}) %all-reduce.7.cloned.1.call-update) | async-done | bytes 65552 | tf_op jit(solution)/shard_map/psum | solution.py:77
  264.2 0.8 broadcast_multiply_fusion.1
  265.0 0.1 copy.6
  265.1 0.9 fusion.36
  266.0 11.7 %cholesky.44 = f32[128,128]{1,0:T(8,128)S(1)} custom-call(f32[128,128]{1,0:T(8,128)S(1)} %fusion.36), custom_call_target="Cholesky" | custom-call | tf_op jit(solution)/shard_map/jit(cholesky)/cholesky | solution.py:78
  277.7 0.6 compare_reduce_fusion.1
  278.3 0.7 fusion.31
  279.0 9.8 custom-call.6
  288.8 1.4 fusion.1
  290.3 0.2 all-reduce.11.cloned.1.call-start
  290.5 125.9 %all-reduce.9.cloned.1.call-done = f32[1024,128]{0,1:T(8,128)} async-done(((f32[1024,128]{0,1:T(8,128)}), f32[1024,128]{0,1:T(8,128)}) %all-reduce.9.cloned.1.call-update) | async-done | bytes 524304 | tf_op jit(solution)/shard_map/psum | solution.py:33
  416.4 4.1 fusion.61
  420.5 0.0 all-reduce.13.cloned.1.call-start
  420.5 0.7 compare_reduce_fusion.2
  421.2 137.6 %all-reduce.11.cloned.1.call-done = f32[128,512]{1,0:T(8,128)} async-done(((f32[128,512]{1,0:T(8,128)}), f32[128,512]{1,0:T(8,128)}) %all-reduce.11.cloned.1.call-update) | async-done | bytes 262160 | tf_op jit(solution)/shard_map/psum | solution.py:83
  558.8 4.2 subtract_select_fusion.1
  563.0 2.6 constant_dynamic-update-slice_fusion
  565.6 1.2 fusion.62
  566.8 0.0 all-reduce.15.cloned.1.call-start
  566.9 126.6 %all-reduce.13.cloned.1.call-done = f32[128,128]{0,1:T(8,128)} async-done(((f32[128,128]{0,1:T(8,128)}), f32[128,128]{0,1:T(8,128)}) %all-reduce.13.cloned.1.call-update) | async-done | bytes 65552 | tf_op jit(solution)/shard_map/psum | solution.py:77
  693.5 0.8 broadcast_multiply_fusion
  694.3 0.1 copy.9
  694.4 0.9 fusion.34
  695.3 11.7 %cholesky.55 = f32[128,128]{1,0:T(8,128)S(1)} custom-call(f32[128,128]{1,0:T(8,128)S(1)} %fusion.34), custom_call_target="Cholesky" | custom-call | tf_op jit(solution)/shard_map/jit(cholesky)/cholesky | solution.py:78
  707.0 0.7 compare_reduce_fusion
  707.8 0.7 fusion.32
  708.5 9.8 custom-call.7
  718.3 1.4 fusion
  719.7 0.3 all-reduce.17.cloned.1.call-start
  720.0 125.8 %all-reduce.15.cloned.1.call-done = f32[1024,128]{0,1:T(8,128)} async-done(((f32[1024,128]{0,1:T(8,128)}), f32[1024,128]{0,1:T(8,128)}) %all-reduce.15.cloned.1.call-update) | async-done | bytes 524304 | tf_op jit(solution)/shard_map/psum | solution.py:33
  845.9 4.8 fusion.63
  850.6 138.3 %all-reduce.17.cloned.1.call-done = f32[128,512]{1,0:T(8,128)} async-done(((f32[128,512]{1,0:T(8,128)}), f32[128,512]{1,0:T(8,128)}) %all-reduce.17.cloned.1.call-update) | async-done | bytes 262160 | tf_op jit(solution)/shard_map/psum | solution.py:83
  988.9 3.6 subtract_select_fusion
  992.5 0.8 fusion.23
  993.3 1.8 copy.17
  (30 shorter events, 0.5 us)
Async XLA Ops:
  7.2 257.0 %all-reduce.7.cloned.1.call-start = ((), (), s32[]{:S(2)}) async-start(), calls=%async_computation | async-start | bytes 131072 | tf_op jit(solution)/shard_map/psum | solution.py:77
  9.0 14.3 %collective-permute-start = (f32[1,128,512]{2,1,0:T(8,128)}, f32[1,128,512]{2,1,0:T(8,128)}, u32[]{:S(2)}, u32[]{:S(2)}) collective-permute-start(f32[1,128,512]{2,1,0:T(8,128)} %get-tuple-element.34), channel_id=1, source_target_pairs={{16,0},{32,16},{48,32},{64,48},{80,64},{96,80},{112,96},{128,112},... | collective-permute-start | bytes 786440 | tf_op jit(solution)/shard_map/ppermute | solution.py:26
  17.8 5.5 collective-permute-start.1
  21.0 2.4 copy-start
  25.4 9.6 collective-permute-start.2
  32.9 5.2 collective-permute-start.3
  38.5 9.9 collective-permute-start.4
  46.2 5.2 collective-permute-start.5
  51.8 9.9 collective-permute-start.6
  59.6 5.2 collective-permute-start.7
  138.7 277.7 %all-reduce.9.cloned.1.call-start = ((), (), s32[]{:S(2)}) async-start(), calls=%async_computation.1 | async-start | bytes 1048576 | tf_op jit(solution)/shard_map/psum | solution.py:33
  290.3 268.6 %all-reduce.11.cloned.1.call-start = ((), (), s32[]{:S(2)}) async-start(), calls=%async_computation.2 | async-start | bytes 524288 | tf_op jit(solution)/shard_map/psum | solution.py:83
  416.4 142.4 %copy-start.1 = (f32[1024,128]{0,1:T(8,128)S(1)}, f32[1024,128]{0,1:T(8,128)}, u32[]{:S(2)}) copy-start(f32[1024,128]{0,1:T(8,128)} %all-reduce.9.cloned.1.call-done) | copy-start | bytes 1572868
  420.5 273.0 %all-reduce.13.cloned.1.call-start = ((), (), s32[]{:S(2)}) async-start(), calls=%async_computation.3 | async-start | bytes 131072 | tf_op jit(solution)/shard_map/psum | solution.py:77
  566.8 279.0 %all-reduce.15.cloned.1.call-start = ((), (), s32[]{:S(2)}) async-start(), calls=%async_computation.4 | async-start | bytes 1048576 | tf_op jit(solution)/shard_map/psum | solution.py:33
  719.7 269.2 %all-reduce.17.cloned.1.call-start = ((), (), s32[]{:S(2)}) async-start(), calls=%async_computation.5 | async-start | bytes 524288 | tf_op jit(solution)/shard_map/psum | solution.py:83
  845.8 143.1 %copy-start.2 = (f32[1024,128]{0,1:T(8,128)S(1)}, f32[1024,128]{0,1:T(8,128)}, u32[]{:S(2)}) copy-start(f32[1024,128]{0,1:T(8,128)} %all-reduce.15.cloned.1.call-done) | copy-start | bytes 1572868
Sparse Core Ops, SparseCore 0:
  138.8 125.2 all-reduce.6
  290.4 125.9 all-reduce.8
  420.6 138.1 all-reduce.10
  566.9 126.5 all-reduce.12
  719.9 125.9 all-reduce.14
  850.8 138.1 all-reduce.16
where the time goes:
time: 1000 us
  waiting for transfers between devices  789 us (79%)
  blocking collectives  67.8 us (7%)
  other arithmetic  59.8 us (6%)
  starting transfers between devices  40 us (4%)
  matrix products  21.9 us (2%)
  between operations  14.4 us (1%)
    psum x2, waiting for transfers between devices, on_device(): coeffs = lax.psum(contract(basis, matrix), 'row') / total_rows  276 us
    psum x2, waiting for transfers between devices, on_device(): gram = lax.psum(contract(raw, raw), 'row') / total_rows  252 us
    psum x2, waiting for transfers between devices, broadcast(): return lax.psum(jnp.where(mine, array, jnp.zeros_like(array)), axis)  252 us
    psum x1, blocking collectives, on_device(): squares = lax.psum(jnp.sum(matrix * matrix, 0), 'row')  67.8 us
    ppermute x4, starting transfers between devices, with_halo(): lax.ppermute(lax.slice_in_dim(block, 0, width, axis=dim), axis, backward)  31.6 us
    another operation x6, other arithmetic, on_device(): lower = jnp.linalg.cholesky(gram)  24.9 us
    another operation x4, other arithmetic, on_device(): lax.linalg.triangular_solve(lower, raw, left_side=False, lower=True, tran...  21 us
  transfers between devices with their start and end apart: 14, of which 9 were waited for; matrix products, arithmetic and copies ran while one was open for 0% of the time, Pallas kernels for 0%

commit v1 on v0

v1 whole, which is shorter than its diff:
```python
import functools

import jax
import jax.numpy as jnp
from jax import lax
from jax.experimental import pallas as pl
from jax.experimental.pallas import tpu as pltpu
from jax.sharding import PartitionSpec as P

PANEL = 128
LEVELS = 4096
BLOCK = 128

energy = 0.25
disorder = 16.5
tiny = 1e-06
highest = lax.Precision.HIGHEST
MIB = 2**20


def site_values(codes):
    return disorder * ((codes.astype(jnp.float32) + 0.5) / LEVELS - 0.5)


def dot(left, right, contract):
    return lax.dot_general(
        left, right, ((contract[:1], contract[1:]), ((), ())),
        precision=highest, preferred_element_type=jnp.float32,
    )


def stencil_kernel(depth, vec_ref, low_ref, high_ref, coef_ref, out_ref, a_ref, b_ref):
    rows = vec_ref.shape[1]
    for i in range(rows):
        a_ref[i] = low_ref[i]
        a_ref[rows + i] = vec_ref[0, i]
        a_ref[2 * rows + i] = high_ref[i]
        b_ref[rows + i] = vec_ref[1, i]
    for i in range(depth - 1):
        b_ref[rows - depth + 1 + i] = low_ref[rows + i]
        b_ref[2 * rows + i] = high_ref[rows + i]
    current, previous = a_ref, b_ref
    sites = vec_ref.shape[2]
    for step in range(depth):
        reach = depth - 1 - step

        def one_row(i, _, current=current, previous=previous, step=step):
            center = current[i]
            beside = current[i + 1] + current[i - 1]
            beside = beside + pltpu.roll(center, 1, 0) + pltpu.roll(center, sites - 1, 0)
            previous[i] = coef_ref[step, i - rows + depth - 1] * center - beside - previous[i]
            return 0

        lax.fori_loop(rows - reach, 2 * rows + reach, one_row, 0)
        current, previous = previous, current
    for i in range(rows):
        out_ref[0, i] = current[rows + i]
        out_ref[1, i] = previous[rows + i]


def stencil(vectors, low, high, coefs, first, count):
    _, rows, sites, _ = vectors.shape
    depth = coefs.shape[0]
    halo = low.shape[0]
    return pl.pallas_call(
        functools.partial(stencil_kernel, depth),
        grid=(count,),
        in_specs=[
            pl.BlockSpec((2, rows, sites, BLOCK), lambda i: (0, 0, 0, i + first)),
            pl.BlockSpec((halo, sites, BLOCK), lambda i: (0, 0, i)),
            pl.BlockSpec((halo, sites, BLOCK), lambda i: (0, 0, i)),
            pl.BlockSpec(coefs.shape, lambda i: (0, 0, 0, 0)),
        ],
        out_specs=pl.BlockSpec((2, rows, sites, BLOCK), lambda i: (0, 0, 0, i)),
        out_shape=jax.ShapeDtypeStruct((2, rows, sites, count * BLOCK), jnp.float32),
        scratch_shapes=[
            pltpu.VMEM((3 * rows, sites, BLOCK), jnp.float32),
            pltpu.VMEM((3 * rows, sites, BLOCK), jnp.float32),
        ],
        compiler_params=pltpu.CompilerParams(vmem_limit_bytes=40 * MIB),
        name="slices",
    )(vectors, low, high, coefs)


def eliminate(mat_ref, inv_ref, first, last):
    size = mat_ref.shape[0]
    lanes = lax.broadcasted_iota(jnp.int32, (size, size), 1)
    subs = lax.broadcasted_iota(jnp.int32, (size, size), 0)

    def one_column(j, _):
        mat = mat_ref[...]
        row = mat_ref[pl.ds(j, 1), :]
        inv_row = inv_ref[pl.ds(j, 1), :]
        pivot = jnp.sum(jnp.where(lanes[:1] == j, row, 0.0), axis=1, keepdims=True)
        column = jnp.sum(jnp.where(lanes == j, mat, 0.0), axis=1, keepdims=True)
        factor = jnp.where(subs[:, :1] > j, column * (1.0 / pivot), 0.0)
        mat_ref[...] = mat - factor * row
        inv_ref[...] = inv_ref[...] - factor * inv_row
        inv_ref[pl.ds(j, 1), :] = inv_row * lax.rsqrt(pivot)
        return 0

    lax.fori_loop(first, last, one_column, 0)


def identity(size):
    lanes = lax.broadcasted_iota(jnp.int32, (size, size), 1)
    subs = lax.broadcasted_iota(jnp.int32, (size, size), 0)
    return jnp.where(lanes == subs, 1.0, 0.0).astype(jnp.float32)


def block_scales(block, total):
    diag = identity(PANEL) * block
    along = lax.rsqrt(jnp.sum(diag, axis=0, keepdims=True) / total + tiny)
    down = lax.rsqrt(jnp.sum(diag, axis=1, keepdims=True) / total + tiny)
    return along, down


def start_kernel(total, pack_ref, mat_ref, inv_ref):
    block = pack_ref[0:PANEL]
    along, down = block_scales(block, total)
    mat_ref[...] = block * down * along / total
    inv_ref[...] = identity(PANEL)
    eliminate(mat_ref, inv_ref, 0, PANEL // 2)


def middle_kernel(total, pack_ref, mat_in, inv_in, rest_ref, inv_ref, cross_ref, mat_ref):
    mat_ref[...] = mat_in[...]
    inv_ref[...] = inv_in[...]
    eliminate(mat_ref, inv_ref, PANEL // 2, PANEL)
    _, down0 = block_scales(pack_ref[0:PANEL], total)
    block = pack_ref[2 * PANEL:3 * PANEL]
    along1, down1 = block_scales(block, total)
    cross = dot(inv_ref[...], pack_ref[PANEL:2 * PANEL] * down0 * along1 / total, (1, 0))
    cross_ref[...] = cross
    rest_ref[...] = block * down1 * along1 / total - dot(cross, cross, (0, 0))


def next_kernel(rest_ref, mat_ref, inv_ref):
    mat_ref[...] = rest_ref[...]
    inv_ref[...] = identity(PANEL)
    eliminate(mat_ref, inv_ref, 0, PANEL // 2)


def finish_kernel(total, pack_ref, inv0_ref, cross_ref, mat_in, inv_in, out_ref, mat_ref, inv_ref):
    mat_ref[...] = mat_in[...]
    inv_ref[...] = inv_in[...]
    eliminate(mat_ref, inv_ref, PANEL // 2, PANEL)
    along0, _ = block_scales(pack_ref[0:PANEL], total)
    along1, _ = block_scales(pack_ref[2 * PANEL:3 * PANEL], total)
    inv0 = inv0_ref[...]
    inv1 = inv_ref[...]
    mixed = -dot(dot(inv1, cross_ref[...], (1, 1)), inv0, (1, 0))
    out_ref[0:PANEL, 0:PANEL] = inv0 * along0
    out_ref[0:PANEL, PANEL:] = jnp.zeros((PANEL, PANEL), jnp.float32)
    out_ref[PANEL:, 0:PANEL] = mixed * along0
    out_ref[PANEL:, PANEL:] = inv1 * along1


def call(kernel, name, outs, scratch, *args):
    square = pltpu.VMEM((PANEL, PANEL), jnp.float32)
    shapes = [jax.ShapeDtypeStruct((k * PANEL, k * PANEL), jnp.float32) for k in outs]
    return pl.pallas_call(
        kernel,
        out_shape=shapes,
        scratch_shapes=[square] * scratch,
        compiler_params=pltpu.CompilerParams(vmem_limit_bytes=16 * MIB),
        cost_estimate=pl.CostEstimate(flops=2 * 10**9, bytes_accessed=10**6, transcendentals=0),
        name=name,
    )(*args)


def factor(pack, total):
    mat, inv = call(functools.partial(start_kernel, total), "factor_a", [1, 1], 0, pack)
    rest, inv0, cross = call(functools.partial(middle_kernel, total), "factor_b", [1, 1, 1], 1, pack, mat, inv)
    mat, inv = call(next_kernel, "factor_c", [1, 1], 0, rest)
    out, = call(functools.partial(finish_kernel, total), "factor_d", [2], 2, pack, inv0, cross, mat, inv)
    return out


def on_device(vectors, potential):
    depth = potential.shape[0]
    _, rows, sites, columns = vectors.shape
    row_count = lax.axis_size("row")
    row_index = lax.axis_index("row")
    col_index = lax.axis_index("col")
    total = 2 * rows * sites * row_count

    forward = [(i, (i + 1) % row_count) for i in range(row_count)]
    backward = [(target, source) for source, target in forward]

    def halos(first, last):
        current = vectors[0, :, :, first:last]
        previous = vectors[1, :, :, first:last]
        up = jnp.concatenate([current, previous[rows - depth + 1:]], 0)
        down = jnp.concatenate([current, previous[:depth - 1]], 0)
        return lax.ppermute(up, "row", forward), lax.ppermute(down, "row", backward)

    low_panel, high_panel = halos(0, PANEL)
    low_rest, high_rest = halos(PANEL, columns)
    site_rows = (row_index * rows - depth + 1 + jnp.arange(rows + 2 * depth - 2)) % potential.shape[1]
    coefs = energy - site_values(jnp.take(potential, site_rows, axis=1))
    coefs = jnp.broadcast_to(coefs[..., None], coefs.shape + (BLOCK,))

    own = stencil(vectors, low_panel, high_panel, coefs, 0, 1)
    rest = stencil(vectors, low_rest, high_rest, coefs, 1, columns // BLOCK - 1)
    own = own.reshape(-1, PANEL)
    matrix = jnp.concatenate([own, rest.reshape(own.shape[0], -1)], 1)

    held = jnp.where(col_index < 2, own, 0.0)
    stages = [
        [(0, 9), (1, 8)],
        [(0, 4), (8, 12), (1, 13), (9, 5)],
        [(1, 3), (13, 15), (5, 7), (9, 11), (4, 2), (0, 14), (8, 6), (12, 10)],
    ]
    for pairs in stages:
        held = held + lax.ppermute(held, "col", pairs)
    pairs = [(4, 3), (2, 1), (0, 15), (14, 13), (12, 11), (10, 9), (8, 7), (6, 5)]
    other = lax.ppermute(held, "col", pairs + [(b, a) for a, b in pairs])
    has_first = functools.reduce(jnp.logical_or, [col_index == c for c in (0, 2, 4, 5, 7, 9, 11, 14)])
    panel0 = jnp.where(has_first, held, other)
    panel1 = jnp.where(has_first, other, held)
    panels = jnp.concatenate([panel0, panel1], 1)

    products = dot(panels, panels, (0, 0))
    coeffs = dot(panels, matrix, (0, 0))
    squares = jnp.sum(matrix * matrix, 0).reshape(-1, BLOCK)
    small = jnp.concatenate([
        products[:PANEL, :PANEL],
        products[:PANEL, PANEL:],
        products[PANEL:, PANEL:],
        jnp.pad(squares, ((0, PANEL - squares.shape[0]), (0, 0))),
    ], 0)
    large = jnp.moveaxis(coeffs.reshape(2 * PANEL, -1, BLOCK), 1, 0).reshape(-1, BLOCK)

    def shares(array):
        return array.reshape(row_count, -1, BLOCK)

    def scattered(array):
        return jnp.sum(lax.all_to_all(array, "row", 0, 0), 0)

    def gathered(array):
        everywhere = jnp.broadcast_to(array, (row_count,) + array.shape)
        return lax.all_to_all(everywhere, "row", 0, 0).reshape(-1, BLOCK)

    share = scattered(jnp.concatenate([shares(small), shares(large)], 1))
    cut = small.shape[0] // row_count
    small = gathered(share[:cut])
    inverse = factor(small, total)
    large = gathered(share[cut:])

    coeffs = jnp.moveaxis(large.reshape(-1, 2 * PANEL, BLOCK), 0, 1).reshape(2 * PANEL, -1)
    squares = small[3 * PANEL:3 * PANEL + columns // BLOCK].reshape(-1)
    scale = jnp.sqrt(squares / total + tiny)
    growth = jnp.log(scale)
    weights = dot(inverse, dot(inverse, coeffs, (1, 0)), (0, 0)) / total
    basis = jnp.where(col_index == 0, inverse[:PANEL], inverse[PANEL:])
    holder = col_index < 2
    first = jnp.where(holder, -basis.T, weights[:, :PANEL])
    weights = jnp.concatenate([first, weights[:, PANEL:]], 1)
    is_panel = holder & (jnp.arange(columns) < PANEL)
    keep = jnp.where(is_panel, 0.0, 1.0)
    shrink = jnp.where(is_panel, 1.0, 1.0 / scale)
    result = (matrix * keep - dot(panels, weights, (1, 0))) * shrink
    return (result.reshape(vectors.shape), growth)


def solution(mesh):
    return jax.shard_map(
        on_device,
        mesh=mesh,
        in_specs=(P(None, "row", None, "col"), P()),
        out_specs=(P(None, "row", None, "col"), P("col")),
        check_vma=False,
    )
```

time: 1000 us -> 179 us (0.18)
  waiting for transfers between devices: 789 us -> 28.9 us
  other arithmetic: 59.8 us -> 6.46 us
  blocking collectives: 67.8 us -> 33 us
  Pallas kernels: 0 us -> 32.8 us
  between operations: 14.4 us -> 1.09 us
  matrix products: 21.9 us -> 9.92 us
  starting transfers between devices: 40 us -> 50.9 us
    psum x6 -> x0, waiting for transfers between devices: 780 us -> none  [the longest x2 276 us: on_device(): coeffs = lax.psum(contract(basis, matrix), 'row') / total_rows]
    psum x1 -> x0, blocking collectives: 67.8 us -> none  [on_device(): squares = lax.psum(jnp.sum(matrix * matrix, 0), 'row')]
    another operation x12 -> x0, other arithmetic: 46.8 us -> none  [the longest x6 24.9 us: on_device(): lower = jnp.linalg.cholesky(gram)]
    all_to_all x0 -> x1, blocking collectives: none -> 33 us  [scattered(): return jnp.sum(lax.all_to_all(array, 'row', 0, 0), 0)]
    pallas_call x0 -> x6, Pallas kernels: none -> 32.8 us  [the longest x4 27.8 us: call(): pl.pallas_call(kernel, out_shape=shapes, scratch_shapes=[square] * scratc...]
    ppermute x8, waiting for transfers between devices: 9.1 us -> 20 us  [the longest x3 15.3 us: on_device(): held = held + lax.ppermute(held, 'col', pairs)]
  transfers between devices with their start and end apart: 14 -> 10, of which waited for: 9 -> 5; matrix products, arithmetic and copies ran while one was open for 0% -> 2% of each run, Pallas kernels for 0% -> 18%
where the time goes in v1:
time: 179 us
  starting transfers between devices  50.9 us (28%)
  blocking collectives  33 us (18%)
  Pallas kernels  32.8 us (18%)
  waiting for transfers between devices  28.9 us (16%)
  local copies, waits for them, and re-layouts  15.5 us (9%)
  matrix products  9.92 us (6%)
  other arithmetic  6.46 us (4%)
    all_to_all x1, blocking collectives, scattered(): return jnp.sum(lax.all_to_all(array, 'row', 0, 0), 0)  33 us
    pallas_call x4, Pallas kernels, call(): pl.pallas_call(kernel, out_shape=shapes, scratch_shapes=[square] * scratc...  27.8 us
    ppermute x3, starting transfers between devices, on_device(): held = held + lax.ppermute(held, 'col', pairs)  17.4 us
    ppermute x3, waiting for transfers between devices, on_device(): held = held + lax.ppermute(held, 'col', pairs)  15.3 us
    ppermute x2, starting transfers between devices, halos(): lax.ppermute(down, 'row', backward)  14 us
    dot_general x5, matrix products, dot(): lax.dot_general(left, right, ((contract[:1], contract[1:]), ((), ())), pr...  9.92 us
    ppermute x2, starting transfers between devices, halos(): lax.ppermute(up, 'row', forward)  9.14 us
    all_to_all x2, waiting for transfers between devices, gathered(): return lax.all_to_all(everywhere, 'row', 0, 0).reshape(-1, BLOCK)  8.97 us
  transfers between devices with their start and end apart: 10, of which 5 were waited for; matrix products, arithmetic and copies ran while one was open for 2% of the time, Pallas kernels for 18%

profile of v1, /device:TPU:1, one launch (start us, length us, event | category | flops | bytes accessed | tf_op | source)
XLA Modules:
  0.0 178.6 jit_solution(11663516606179917101)
XLA Ops:
  0.6 0.0 copy-start
  0.6 1.0 slice_bitcast_fusion.3
  1.7 1.1 slice_bitcast_fusion.4
  2.7 0.0 copy-start.3
  2.7 1.0 pad_maximum_fusion.13
  3.7 4.6 %collective-permute-start = (f32[7,128,128]{2,1,0:T(8,128)}, f32[7,128,128]{2,1,0:T(8,128)S(1)}, u32[]{:S(2)}, u32[]{:S(2)}) collective-permute-start(f32[7,128,128]{2,1,0:T(8,128)} %get-tuple-element.25), channel_id=1, source_target_pairs={{0,16},{16,32},{32,48},{48,64},{64,80},{80,96},{96,112},{112,128},... | collective-permute-start | bytes 1376264 | tf_op jit(solution)/shard_map/ppermute | solution.py:196
  8.3 6.1 %collective-permute-start.1 = (f32[7,128,128]{2,1,0:T(8,128)}, f32[7,128,128]{2,1,0:T(8,128)S(1)}, u32[]{:S(2)}, u32[]{:S(2)}) collective-permute-start(f32[7,128,128]{2,1,0:T(8,128)} %get-tuple-element.24), channel_id=1, source_target_pairs={{16,0},{32,16},{48,32},{64,48},{80,64},{96,80},{112,96},{128,112},... | collective-permute-start | bytes 1376264 | tf_op jit(solution)/shard_map/ppermute | solution.py:196
  14.5 0.0 copy-done
  14.5 0.6 gather_fusion
  15.1 0.1 subtract_bitcast_fusion
  15.2 0.0 collective-permute-done.low_ref
  15.2 3.4 %collective-permute-done.1.high_ref = f32[7,128,128]{2,1,0:T(8,128)S(1)} collective-permute-done((f32[7,128,128]{2,1,0:T(8,128)}, f32[7,128,128]{2,1,0:T(8,128)S(1)}, u32[]{:S(2)}, u32[]{:S(2)}) %collective-permute-start.1) | collective-permute-done | bytes 458784 | tf_op jit(solution)/shard_map/ppermute | solution.py:196
  18.6 0.8 copy-done.7
  19.4 0.7 broadcast_in_dim.40.coef_ref
  20.2 0.0 copy-start.8
  20.2 1.0 copy-done.8
  21.2 0.9 slices.2
  22.1 0.6 copy-done.1
  22.7 14.7 %collective-permute-start.4 = (f32[1024,128]{1,0:T(8,128)S(1)}, f32[1024,128]{1,0:T(8,128)S(1)}, u32[]{:S(2)}, u32[]{:S(2)}) collective-permute-start(f32[1024,128]{1,0:T(8,128)S(1)} %broadcast_select_fusion), channel_id=1, source_target_pairs={{0,9},{1,8},{16,25},{17,24},{32,41},{33,40},{48,57},{49,56},{64,73... | collective-permute-start | bytes 1572872 | tf_op jit(solution)/shard_map/ppermute | solution.py:216
  37.5 0.1 slice_bitcast_fusion
  37.5 0.1 slice_bitcast_fusion.1
  37.6 8.9 %collective-permute-done.4 = f32[1024,128]{1,0:T(8,128)S(1)} collective-permute-done((f32[1024,128]{1,0:T(8,128)S(1)}, f32[1024,128]{1,0:T(8,128)S(1)}, u32[]{:S(2)}, u32[]{:S(2)}) %collective-permute-start.4) | collective-permute-done | bytes 524320 | tf_op jit(solution)/shard_map/ppermute | solution.py:216
  46.5 0.1 fusion.23
  46.6 1.3 collective-permute-start.5
  47.9 1.9 %pad_maximum_fusion.1 = (f32[7,128,384]{2,1,0:T(8,128)}, f32[7,128,384]{2,1,0:T(8,128)}) fusion(f32[4,128,384]{2,1,0:T(8,128)S(1)} %slice_bitcast_fusion, f32[3,128,384]{2,1,0:T(8,128)S(1)} %get-tuple-element.18, f32[3,128,384]{2,1,0:T(8,128)S(1)} %get-tuple-element.19), kind=kLoop, calls=%fused_computation.4 | loop fusion | flops 688128 | bytes 4718592 | tf_op jit(solution)/shard_map/concatenate | solution.py:195
  49.8 4.6 %collective-permute-start.2 = (f32[7,128,384]{2,1,0:T(8,128)}, f32[7,128,384]{2,1,0:T(8,128)S(1)}, u32[]{:S(2)}, u32[]{:S(2)}) collective-permute-start(f32[7,128,384]{2,1,0:T(8,128)} %get-tuple-element.23), channel_id=1, source_target_pairs={{0,16},{16,32},{32,48},{48,64},{64,80},{80,96},{96,112},{112,128},... | collective-permute-start | bytes 4128776 | tf_op jit(solution)/shard_map/ppermute | solution.py:196
  54.4 7.9 %collective-permute-start.3 = (f32[7,128,384]{2,1,0:T(8,128)}, f32[7,128,384]{2,1,0:T(8,128)}, u32[]{:S(2)}, u32[]{:S(2)}) collective-permute-start(f32[7,128,384]{2,1,0:T(8,128)} %get-tuple-element.22), channel_id=1, source_target_pairs={{16,0},{32,16},{48,32},{64,48},{80,64},{96,80},{112,96},{128,112},... | collective-permute-start | bytes 4128776 | tf_op jit(solution)/shard_map/ppermute | solution.py:196
  62.3 0.0 collective-permute-done.5
  62.3 0.1 add.102
  62.4 1.3 collective-permute-start.6
  63.7 6.4 %collective-permute-done.6 = f32[1024,128]{1,0:T(8,128)S(1)} collective-permute-done((f32[1024,128]{1,0:T(8,128)S(1)}, f32[1024,128]{1,0:T(8,128)S(1)}, u32[]{:S(2)}, u32[]{:S(2)}) %collective-permute-start.6) | collective-permute-done | bytes 524320 | tf_op jit(solution)/shard_map/ppermute | solution.py:216
  70.1 0.1 add.103
  70.2 1.9 %collective-permute-start.7 = (f32[1024,128]{1,0:T(8,128)S(1)}, f32[1024,128]{1,0:T(8,128)}, u32[]{:S(2)}, u32[]{:S(2)}) collective-permute-start(f32[1024,128]{1,0:T(8,128)S(1)} %add.103), channel_id=1, source_target_pairs={{4,3},{2,1},{0,15},{14,13},{12,11},{10,9},{8,7},{6,5},{3,4},{1,2},... | collective-permute-start | bytes 1572872 | tf_op jit(solution)/shard_map/ppermute | solution.py:218
  72.1 0.0 collective-permute-done.2.low_ref
  72.1 1.1 copy-done.5
  73.3 1.2 collective-permute-done.3.high_ref
  74.5 1.7 copy-done.2
  76.3 1.6 copy-done.4
  77.8 1.3 copy-done.6
  79.2 4.1 %slices.3 = f32[2,4,128,384]{3,2,1,0:T(8,128)S(1)} custom-call(f32[2,4,128,512]{3,2,1,0:T(8,128)S(1)} %copy-done.4, f32[7,128,384]{2,1,0:T(8,128)S(1)} %copy-done.6, f32[7,128,384]{2,1,0:T(8,128)} %collective-permute-done.3.high_ref, f32[4,10,128,128]{3,2,1,0:T(8,128)S(1)} %copy-done.2), custom_call_target="tpu_custom_call" | custom-call | tf_op jit(solution)/shard_map/slices/pallas_call | solution.py:65
  83.3 0.2 multiply_reduce_fusion
  83.5 0.0 collective-permute-done.7
  83.5 1.1 broadcast_select_fusion.2
  84.6 0.0 copy-start.9
  84.7 2.0 %fusion.1 = f32[32,4,8,128]{3,2,1,0:T(8,128)S(1)} fusion(f32[1024,384]{1,0:T(8,128)S(1)} %bitcast.50, f32[1024,128]{1,0:T(8,128)S(1)} %bitcast.53, f32[1024,128]{1,0:T(8,128)S(1)} %get-tuple-element.21, f32[1024,128]{1,0:T(8,128)S(1)} %get-tuple-element.20), kind=kOutput, calls=%fused_computation.7 | convolution fusion | flops 1611399168 | bytes 3670016 | tf_op jit(solution)/shard_map/dot_general | solution.py:26
  86.7 1.9 %fusion.3 = f32[256,256]{1,0:T(8,128)S(1)} fusion(f32[1024,128]{1,0:T(8,128)S(1)} %get-tuple-element.21, f32[1024,128]{1,0:T(8,128)S(1)} %get-tuple-element.20), kind=kOutput, calls=%fused_computation.13 | convolution fusion | flops 805568512 | bytes 1310720 | tf_op jit(solution)/shard_map/dot_general | solution.py:26
  88.7 0.1 pad_maximum_fusion.7
  88.7 33.0 %all_to_all.15 = f32[32,48,128]{2,1,0:T(8,128)} all-to-all(f32[32,48,128]{2,1,0:T(8,128)S(1)} %pad_maximum_fusion.7), channel_id=1, replica_groups=mesh['row'=32,'col'=16] {'row'}, dimensions={0} | all-to-all | bytes 1572864 | tf_op jit(solution)/shard_map/all_to_all | solution.py:239
  121.7 1.2 reduce_sum.19
  122.9 0.7 broadcast_in_dim.44
  123.7 3.8 %all-to-all-start.1 = ((f32[32,16,128]{2,1,0:T(8,128)}), f32[32,16,128]{2,1,0:T(8,128)S(1)}, u32[]{:S(2)}, u32[]{:S(2)}) async-start(f32[32,16,128]{2,1,0:T(8,128)} %broadcast_in_dim.44), calls=%async_computation.1 | async-start | bytes 524288 | tf_op jit(solution)/shard_map/all_to_all | solution.py:243
  127.5 9.0 %all-to-all-done.1 = f32[32,16,128]{2,1,0:T(8,128)S(1)} async-done(((f32[32,16,128]{2,1,0:T(8,128)}), f32[32,16,128]{2,1,0:T(8,128)S(1)}, u32[]{:S(2)}, u32[]{:S(2)}) %all-to-all-start.1) | async-done | bytes 262176 | tf_op jit(solution)/shard_map/all_to_all | solution.py:243
  136.5 0.9 broadcast_in_dim.45
  137.4 4.6 %all-to-all-start.2 = ((f32[32,32,128]{2,1,0:T(8,128)}), f32[32,32,128]{2,1,0:T(8,128)}, u32[]{:S(2)}, u32[]{:S(2)}) async-start(f32[32,32,128]{2,1,0:T(8,128)} %broadcast_in_dim.45), calls=%async_computation.2 | async-start | bytes 1048576 | tf_op jit(solution)/shard_map/all_to_all | solution.py:243
  141.9 6.8 %factor_a.1 = (f32[128,128]{1,0:T(8,128)S(1)}, f32[128,128]{1,0:T(8,128)S(1)}) custom-call(f32[512,128]{1,0:T(8,128)S(1)} %bitcast.55), custom_call_target="tpu_custom_call" | custom-call | flops 2000000000 | bytes 1000000 | tf_op jit(solution)/shard_map/factor_a/pallas_call | solution.py:162
  148.7 7.2 %factor_b.1 = (f32[128,128]{1,0:T(8,128)S(1)}, f32[128,128]{1,0:T(8,128)S(1)}, f32[128,128]{1,0:T(8,128)S(1)}) custom-call(f32[512,128]{1,0:T(8,128)S(1)} %bitcast.56, f32[128,128]{1,0:T(8,128)S(1)} %get-tuple-element.9.mat_in, f32[128,128]{1,0:T(8,128)S(1)} %get-tuple-element.10.inv_in), custom_call_target="tpu_custom_call" | custom-call | flops 2000000000 | bytes 1000000 | tf_op jit(solution)/shard_map/factor_b/pallas_call | solution.py:162
  156.0 6.6 %factor_c.1 = (f32[128,128]{1,0:T(8,128)S(1)}, f32[128,128]{1,0:T(8,128)S(1)}) custom-call(f32[128,128]{1,0:T(8,128)S(1)} %get-tuple-element.13.rest_ref), custom_call_target="tpu_custom_call" | custom-call | flops 2000000000 | bytes 1000000 | tf_op jit(solution)/shard_map/factor_c/pallas_call | solution.py:162
  162.6 7.2 %factor_d.1 = f32[256,256]{1,0:T(8,128)S(1)} custom-call(f32[512,128]{1,0:T(8,128)S(1)} %bitcast.57, f32[128,128]{1,0:T(8,128)S(1)} %get-tuple-element.11.inv0_ref, f32[128,128]{1,0:T(8,128)S(1)} %get-tuple-element.12.cross_ref, f32[128,128]{1,0:T(8,128)S(1)} %get-tuple-element.14.mat_in, f32[128,128]{1,0:T(8,128)S(1)} %get-tuple-element.15.inv_in), custom_call_target="tpu_custom_call" | custom-call | flops 2000000000 | bytes 1000000 | tf_op jit(solution)/shard_map/factor_d/pallas_call | solution.py:162
  169.8 0.6 multiply_bitcast_fusion
  170.4 0.0 all-to-all-done.2
  170.4 2.0 %copy.8 = f32[256,4,128]{0,2,1:T(8,128)} copy(f32[256,4,128]{2,0,1:T(8,128)} %bitcast.17) | data formatting | bytes 1048576 | tf_op jit(solution)/shard_map/transpose | solution.py:251
  172.4 1.7 fusion.18
  174.2 1.0 convolution_multiply_fusion
  175.3 3.3 %subtract_multiply_fusion = f32[1024,512]{1,0:T(8,128)} fusion(f32[1024,384]{1,0:T(8,128)S(1)} %bitcast.51, f32[1024,128]{1,0:T(8,128)S(1)} %bitcast.54, f32[512]{0:T(512)S(1)} %bitcast_select_fusion, f32[512]{0:T(512)S(1)} %fusion.11, f32[1024,128]{1,0:T(8,128)S(1)} %copy-done.10, f32[1024,128]{1,0:T(8,128)S(1)} %get-tuple-element.20, ...), kind=kOutput, calls=%fused_computation.2 | convolution fusion | flops 1613103104 | bytes 5771264 | tf_op jit(solution)/shard_map/dot_general | solution.py:26
  (24 shorter events, 0.2 us)
Async XLA Ops:
  0.6 13.9 %copy-start = (s32[4,128,128]{2,1,0:T(8,128)S(1)}, s32[4,128,128]{2,1,0:T(8,128)}, u32[]{:S(2)}) copy-start(s32[4,128,128]{2,1,0:T(8,128)} %param.3) | copy-start | bytes 786436
  2.7 17.4 %copy-start.3 = (f32[2,4,128,512]{3,2,1,0:T(8,128)S(1)}, f32[2,4,128,512]{3,2,1,0:T(8,128)}, u32[]{:S(2)}) copy-start(f32[2,4,128,512]{3,2,1,0:T(8,128)} %vec_ref.3) | copy-start | bytes 6291460
  3.7 11.5 %collective-permute-start = (f32[7,128,128]{2,1,0:T(8,128)}, f32[7,128,128]{2,1,0:T(8,128)S(1)}, u32[]{:S(2)}, u32[]{:S(2)}) collective-permute-start(f32[7,128,128]{2,1,0:T(8,128)} %get-tuple-element.25), channel_id=1, source_target_pairs={{0,16},{16,32},{32,48},{48,64},{64,80},{80,96},{96,112},{112,128},... | collective-permute-start | bytes 1376264 | tf_op jit(solution)/shard_map/ppermute | solution.py:196
  8.3 10.3 %collective-permute-start.1 = (f32[7,128,128]{2,1,0:T(8,128)}, f32[7,128,128]{2,1,0:T(8,128)S(1)}, u32[]{:S(2)}, u32[]{:S(2)}) collective-permute-start(f32[7,128,128]{2,1,0:T(8,128)} %get-tuple-element.24), channel_id=1, source_target_pairs={{16,0},{32,16},{48,32},{64,48},{80,64},{96,80},{112,96},{128,112},... | collective-permute-start | bytes 1376264 | tf_op jit(solution)/shard_map/ppermute | solution.py:196
  18.6 0.8 copy-start.7
  20.2 1.0 copy-start.8
  21.2 1.5 copy-start.1
  22.7 23.8 %collective-permute-start.4 = (f32[1024,128]{1,0:T(8,128)S(1)}, f32[1024,128]{1,0:T(8,128)S(1)}, u32[]{:S(2)}, u32[]{:S(2)}) collective-permute-start(f32[1024,128]{1,0:T(8,128)S(1)} %broadcast_select_fusion), channel_id=1, source_target_pairs={{0,9},{1,8},{16,25},{17,24},{32,41},{33,40},{48,57},{49,56},{64,73... | collective-permute-start | bytes 1572872 | tf_op jit(solution)/shard_map/ppermute | solution.py:216
  46.6 15.7 %collective-permute-start.5 = (f32[1024,128]{1,0:T(8,128)S(1)}, f32[1024,128]{1,0:T(8,128)S(1)}, u32[]{:S(2)}, u32[]{:S(2)}) collective-permute-start(f32[1024,128]{1,0:T(8,128)S(1)} %fusion.23), channel_id=1, source_target_pairs={{0,4},{8,12},{1,13},{9,5},{16,20},{24,28},{17,29},{25,21},{32,36},... | collective-permute-start | bytes 1572872 | tf_op jit(solution)/shard_map/ppermute | solution.py:216
  49.8 22.3 %collective-permute-start.2 = (f32[7,128,384]{2,1,0:T(8,128)}, f32[7,128,384]{2,1,0:T(8,128)S(1)}, u32[]{:S(2)}, u32[]{:S(2)}) collective-permute-start(f32[7,128,384]{2,1,0:T(8,128)} %get-tuple-element.23), channel_id=1, source_target_pairs={{0,16},{16,32},{32,48},{48,64},{64,80},{80,96},{96,112},{112,128},... | collective-permute-start | bytes 4128776 | tf_op jit(solution)/shard_map/ppermute | solution.py:196
  54.4 20.1 %collective-permute-start.3 = (f32[7,128,384]{2,1,0:T(8,128)}, f32[7,128,384]{2,1,0:T(8,128)}, u32[]{:S(2)}, u32[]{:S(2)}) collective-permute-start(f32[7,128,384]{2,1,0:T(8,128)} %get-tuple-element.22), channel_id=1, source_target_pairs={{16,0},{32,16},{48,32},{64,48},{80,64},{96,80},{112,96},{128,112},... | collective-permute-start | bytes 4128776 | tf_op jit(solution)/shard_map/ppermute | solution.py:196
  62.4 7.7 %collective-permute-start.6 = (f32[1024,128]{1,0:T(8,128)S(1)}, f32[1024,128]{1,0:T(8,128)S(1)}, u32[]{:S(2)}, u32[]{:S(2)}) collective-permute-start(f32[1024,128]{1,0:T(8,128)S(1)} %add.102), channel_id=1, source_target_pairs={{1,3},{13,15},{5,7},{9,11},{4,2},{0,14},{8,6},{12,10},{17,19},{29,... | collective-permute-start | bytes 1572872 | tf_op jit(solution)/shard_map/ppermute | solution.py:216
  70.2 13.4 %collective-permute-start.7 = (f32[1024,128]{1,0:T(8,128)S(1)}, f32[1024,128]{1,0:T(8,128)}, u32[]{:S(2)}, u32[]{:S(2)}) collective-permute-start(f32[1024,128]{1,0:T(8,128)S(1)} %add.103), channel_id=1, source_target_pairs={{4,3},{2,1},{0,15},{14,13},{12,11},{10,9},{8,7},{6,5},{3,4},{1,2},... | collective-permute-start | bytes 1572872 | tf_op jit(solution)/shard_map/ppermute | solution.py:218
  72.1 1.1 copy-start.5
  74.5 1.7 copy-start.2
  76.2 1.6 copy-start.4
  77.8 1.3 copy-start.6
  84.6 3.9 %copy-start.9 = (f32[1024,128]{1,0:T(8,128)}, f32[1024,128]{1,0:T(8,128)S(1)}, u32[]{:S(2)}) copy-start(f32[1024,128]{1,0:T(8,128)S(1)} %get-tuple-element.21) | copy-start | bytes 1572868
  123.7 12.8 %all-to-all-start.1 = ((f32[32,16,128]{2,1,0:T(8,128)}), f32[32,16,128]{2,1,0:T(8,128)S(1)}, u32[]{:S(2)}, u32[]{:S(2)}) async-start(f32[32,16,128]{2,1,0:T(8,128)} %broadcast_in_dim.44), calls=%async_computation.1 | async-start | bytes 524288 | tf_op jit(solution)/shard_map/all_to_all | solution.py:243
  137.4 33.0 %all-to-all-start.2 = ((f32[32,32,128]{2,1,0:T(8,128)}), f32[32,32,128]{2,1,0:T(8,128)}, u32[]{:S(2)}, u32[]{:S(2)}) async-start(f32[32,32,128]{2,1,0:T(8,128)} %broadcast_in_dim.45), calls=%async_computation.2 | async-start | bytes 1048576 | tf_op jit(solution)/shard_map/all_to_all | solution.py:243
  172.4 2.8 %copy-start.10 = (f32[1024,128]{1,0:T(8,128)S(1)}, f32[1024,128]{1,0:T(8,128)}, u32[]{:S(2)}) copy-start(f32[1024,128]{1,0:T(8,128)} %copy-done.9) | copy-start | bytes 1572868

commit v2 on v1

--- a/solution.py
+++ b/solution.py
@@ -82,24 +82,35 @@
     )(vectors, low, high, coefs)
 
 
-def eliminate(mat_ref, inv_ref, first, last):
+def eliminate(mat_ref, inv_ref):
     size = mat_ref.shape[0]
-    lanes = lax.broadcasted_iota(jnp.int32, (size, size), 1)
-    subs = lax.broadcasted_iota(jnp.int32, (size, size), 0)
-
-    def one_column(j, _):
-        mat = mat_ref[...]
-        row = mat_ref[pl.ds(j, 1), :]
-        inv_row = inv_ref[pl.ds(j, 1), :]
-        pivot = jnp.sum(jnp.where(lanes[:1] == j, row, 0.0), axis=1, keepdims=True)
-        column = jnp.sum(jnp.where(lanes == j, mat, 0.0), axis=1, keepdims=True)
-        factor = jnp.where(subs[:, :1] > j, column * (1.0 / pivot), 0.0)
-        mat_ref[...] = mat - factor * row
-        inv_ref[...] = inv_ref[...] - factor * inv_row
-        inv_ref[pl.ds(j, 1), :] = inv_row * lax.rsqrt(pivot)
-        return 0
-
-    lax.fori_loop(first, last, one_column, 0)
+    step = 8
+    wide = (step, 2 * size)
+    lanes = lax.broadcasted_iota(jnp.int32, (step, size), 1)
+    subs = lax.broadcasted_iota(jnp.int32, wide, 0)
+    inv_ref[...] = identity(size)
+    for first in range(0, size, step):
+        last = first + step
+        both = jnp.concatenate([mat_ref[first:last], inv_ref[first:last]], 1)
+        columns = [jnp.broadcast_to(both[:, first + k:first + k + 1], (step, size)) for k in range(step)]
+        entry = [[jnp.broadcast_to(columns[k][i:i + 1], (step, size)) for k in range(i + 1)] for i in range(step)]
+        rows = [jnp.broadcast_to(both[i:i + 1], wide) for i in range(step)]
+        result = jnp.zeros(wide, jnp.float32)
+        for k in range(step):
+            root = lax.rsqrt(entry[k][k])
+            done = rows[k] * jnp.concatenate([root, root], 1)
+            result = jnp.where(subs == k, done, result)
+            lower = {i: entry[i][k] * root for i in range(k + 1, step)}
+            for i in range(k + 1, step):
+                for j in range(k + 1, i + 1):
+                    entry[i][j] = entry[i][j] - lower[i] * lower[j]
+                rows[i] = rows[i] - jnp.concatenate([lower[i], lower[i]], 1) * done
+        inv_ref[first:last] = result[:, size:]
+        if last < size:
+            below = jnp.where(lanes >= last, result[:, :size], 0.0)
+            change = dot(below, result, (0, 0))
+            mat_ref[last:] = mat_ref[last:] - change[last:, :size]
+            inv_ref[last:] = inv_ref[last:] - change[last:, size:]
 
 
 def identity(size):
@@ -115,19 +126,11 @@
     return along, down
 
 
-def start_kernel(total, pack_ref, mat_ref, inv_ref):
+def first_kernel(total, pack_ref, rest_ref, inv_ref, cross_ref, mat_ref):
     block = pack_ref[0:PANEL]
-    along, down = block_scales(block, total)
-    mat_ref[...] = block * down * along / total
-    inv_ref[...] = identity(PANEL)
-    eliminate(mat_ref, inv_ref, 0, PANEL // 2)
-
-
-def middle_kernel(total, pack_ref, mat_in, inv_in, rest_ref, inv_ref, cross_ref, mat_ref):
-    mat_ref[...] = mat_in[...]
-    inv_ref[...] = inv_in[...]
-    eliminate(mat_ref, inv_ref, PANEL // 2, PANEL)
-    _, down0 = block_scales(pack_ref[0:PANEL], total)
+    along0, down0 = block_scales(block, total)
+    mat_ref[...] = block * down0 * along0 / total
+    eliminate(mat_ref, inv_ref)
     block = pack_ref[2 * PANEL:3 * PANEL]
     along1, down1 = block_scales(block, total)
     cross = dot(inv_ref[...], pack_ref[PANEL:2 * PANEL] * down0 * along1 / total, (1, 0))
@@ -135,16 +138,9 @@
     rest_ref[...] = block * down1 * along1 / total - dot(cross, cross, (0, 0))
 
 
-def next_kernel(rest_ref, mat_ref, inv_ref):
+def second_kernel(total, pack_ref, rest_ref, inv0_ref, cross_ref, out_ref, mat_ref, inv_ref):
     mat_ref[...] = rest_ref[...]
-    inv_ref[...] = identity(PANEL)
-    eliminate(mat_ref, inv_ref, 0, PANEL // 2)
-
-
-def finish_kernel(total, pack_ref, inv0_ref, cross_ref, mat_in, inv_in, out_ref, mat_ref, inv_ref):
-    mat_ref[...] = mat_in[...]
-    inv_ref[...] = inv_in[...]
-    eliminate(mat_ref, inv_ref, PANEL // 2, PANEL)
+    eliminate(mat_ref, inv_ref)
     along0, _ = block_scales(pack_ref[0:PANEL], total)
     along1, _ = block_scales(pack_ref[2 * PANEL:3 * PANEL], total)
     inv0 = inv0_ref[...]
@@ -170,11 +166,54 @@
 
 
 def factor(pack, total):
-    mat, inv = call(functools.partial(start_kernel, total), "factor_a", [1, 1], 0, pack)
-    rest, inv0, cross = call(functools.partial(middle_kernel, total), "factor_b", [1, 1, 1], 1, pack, mat, inv)
-    mat, inv = call(next_kernel, "factor_c", [1, 1], 0, rest)
-    out, = call(functools.partial(finish_kernel, total), "factor_d", [2], 2, pack, inv0, cross, mat, inv)
+    rest, inv0, cross = call(functools.partial(first_kernel, total), "factor_a", [1, 1, 1], 1, pack)
+    out, = call(functools.partial(second_kernel, total), "factor_b", [2], 2, pack, rest, inv0, cross)
     return out
+
+
+def finish_kernel(total, place_ref, inv_ref, coef_ref, squares_ref, panel0_ref, panel1_ref, own_ref, rest_ref, out_ref):
+    i = pl.program_id(0)
+    place = place_ref[0]
+    is_panel = jnp.logical_and(i == 0, place < 2)
+    inverse = inv_ref[...]
+    part = dot(inverse, coef_ref[...], (1, 0)) / total
+    subs = lax.broadcasted_iota(jnp.int32, part.shape, 0)
+    lanes = lax.broadcasted_iota(jnp.int32, part.shape, 1)
+    chosen = jnp.where(subs == lanes + place * PANEL, -1.0, 0.0)
+    part = jnp.where(is_panel, chosen, part)
+    weights = dot(inverse, part, (0, 0))
+    taken = dot(panel0_ref[...], weights[:PANEL], (1, 0)) + dot(panel1_ref[...], weights[PANEL:], (1, 0))
+    block = jnp.where(i == 0, own_ref[...], rest_ref[...]).reshape(taken.shape)
+    squares = squares_ref[pl.ds(i, 1), :]
+    shrink = 1.0 / jnp.sqrt(squares / total + tiny)
+    keep = jnp.where(is_panel, 0.0, 1.0)
+    shrink = jnp.where(is_panel, 1.0, shrink)
+    out_ref[...] = ((block * keep - taken) * shrink).reshape(out_ref.shape)
+
+
+def finish(col_index, inverse, large, squares, panel0, panel1, own, rest, total):
+    _, rows, sites, _ = own.shape
+    count = rest.shape[3] // BLOCK + 1
+    shape = (2, rows, sites, BLOCK)
+    fixed = lambda array: pl.BlockSpec(array.shape, lambda i: (0,) * array.ndim)
+    return pl.pallas_call(
+        functools.partial(finish_kernel, total),
+        grid=(count,),
+        in_specs=[
+            pl.BlockSpec(memory_space=pltpu.SMEM),
+            fixed(inverse),
+            pl.BlockSpec((2 * PANEL, BLOCK), lambda i: (i, 0)),
+            fixed(squares),
+            fixed(panel0),
+            fixed(panel1),
+            fixed(own),
+            pl.BlockSpec(shape, lambda i: (0, 0, 0, jnp.maximum(i - 1, 0))),
+        ],
+        out_specs=pl.BlockSpec(shape, lambda i: (0, 0, 0, i)),
+        out_shape=jax.ShapeDtypeStruct((2, rows, sites, count * BLOCK), jnp.float32),
+        compiler_params=pltpu.CompilerParams(vmem_limit_bytes=40 * MIB),
+        name="finish",
+    )(col_index.reshape(1), inverse, large, squares, panel0, panel1, own, rest)
 
 
 def on_device(vectors, potential):
@@ -203,65 +242,58 @@
 
     own = stencil(vectors, low_panel, high_panel, coefs, 0, 1)
     rest = stencil(vectors, low_rest, high_rest, coefs, 1, columns // BLOCK - 1)
-    own = own.reshape(-1, PANEL)
-    matrix = jnp.concatenate([own, rest.reshape(own.shape[0], -1)], 1)
-
-    held = jnp.where(col_index < 2, own, 0.0)
+    panel = own.reshape(-1, PANEL)
+    matrix = jnp.concatenate([panel, rest.reshape(panel.shape[0], -1)], 1)
+
     stages = [
         [(0, 9), (1, 8)],
         [(0, 4), (8, 12), (1, 13), (9, 5)],
         [(1, 3), (13, 15), (5, 7), (9, 11), (4, 2), (0, 14), (8, 6), (12, 10)],
     ]
-    for pairs in stages:
-        held = held + lax.ppermute(held, "col", pairs)
+
+    def spread(array):
+        array = jnp.where(col_index < 2, array, 0.0)
+        for pairs in stages:
+            array = array + lax.ppermute(array, "col", pairs)
+        return array
+
+    def scattered(array):
+        return jnp.sum(lax.all_to_all(array.reshape(row_count, -1, BLOCK), "row", 0, 0), 0)
+
+    def gathered(array):
+        everywhere = jnp.broadcast_to(array, (row_count,) + array.shape)
+        return lax.all_to_all(everywhere, "row", 0, 0)
+
+    swapped = lax.ppermute(panel, "col", [(0, 1), (1, 0)])
+    first = jnp.where(col_index == 0, panel, swapped)
+    second = jnp.where(col_index == 0, swapped, panel)
+    products = jnp.concatenate([
+        dot(first, first, (0, 0)),
+        dot(first, second, (0, 0)),
+        dot(second, second, (0, 0)),
+        jnp.zeros((PANEL, PANEL), jnp.float32),
+    ], 0)
+    inverse = factor(gathered(spread(scattered(products))).reshape(-1, BLOCK), total)
+
+    held = spread(panel)
     pairs = [(4, 3), (2, 1), (0, 15), (14, 13), (12, 11), (10, 9), (8, 7), (6, 5)]
     other = lax.ppermute(held, "col", pairs + [(b, a) for a, b in pairs])
     has_first = functools.reduce(jnp.logical_or, [col_index == c for c in (0, 2, 4, 5, 7, 9, 11, 14)])
     panel0 = jnp.where(has_first, held, other)
     panel1 = jnp.where(has_first, other, held)
-    panels = jnp.concatenate([panel0, panel1], 1)
-
-    products = dot(panels, panels, (0, 0))
-    coeffs = dot(panels, matrix, (0, 0))
+
+    coeffs = dot(jnp.concatenate([panel0, panel1], 1), matrix, (0, 0))
+    large = jnp.moveaxis(coeffs.reshape(2 * PANEL, -1, BLOCK), 1, 0).reshape(row_count, -1, BLOCK)
     squares = jnp.sum(matrix * matrix, 0).reshape(-1, BLOCK)
-    small = jnp.concatenate([
-        products[:PANEL, :PANEL],
-        products[:PANEL, PANEL:],
-        products[PANEL:, PANEL:],
-        jnp.pad(squares, ((0, PANEL - squares.shape[0]), (0, 0))),
-    ], 0)
-    large = jnp.moveaxis(coeffs.reshape(2 * PANEL, -1, BLOCK), 1, 0).reshape(-1, BLOCK)
-
-    def shares(array):
-        return array.reshape(row_count, -1, BLOCK)
-
-    def scattered(array):
-        return jnp.sum(lax.all_to_all(array, "row", 0, 0), 0)
-
-    def gathered(array):
-        everywhere = jnp.broadcast_to(array, (row_count,) + array.shape)
-        return lax.all_to_all(everywhere, "row", 0, 0).reshape(-1, BLOCK)
-
-    share = scattered(jnp.concatenate([shares(small), shares(large)], 1))
-    cut = small.shape[0] // row_count
-    small = gathered(share[:cut])
-    inverse = factor(small, total)
-    large = gathered(share[cut:])
-
-    coeffs = jnp.moveaxis(large.reshape(-1, 2 * PANEL, BLOCK), 0, 1).reshape(2 * PANEL, -1)
-    squares = small[3 * PANEL:3 * PANEL + columns // BLOCK].reshape(-1)
-    scale = jnp.sqrt(squares / total + tiny)
-    growth = jnp.log(scale)
-    weights = dot(inverse, dot(inverse, coeffs, (1, 0)), (0, 0)) / total
-    basis = jnp.where(col_index == 0, inverse[:PANEL], inverse[PANEL:])
-    holder = col_index < 2
-    first = jnp.where(holder, -basis.T, weights[:, :PANEL])
-    weights = jnp.concatenate([first, weights[:, PANEL:]], 1)
-    is_panel = holder & (jnp.arange(columns) < PANEL)
-    keep = jnp.where(is_panel, 0.0, 1.0)
-    shrink = jnp.where(is_panel, 1.0, 1.0 / scale)
-    result = (matrix * keep - dot(panels, weights, (1, 0))) * shrink
-    return (result.reshape(vectors.shape), growth)
+    squares = jnp.pad(squares, ((0, 8 * row_count - squares.shape[0]), (0, 0)))
+    cut = large.shape[1]
+    share = scattered(jnp.concatenate([large, squares.reshape(row_count, 8, BLOCK)], 1))
+    every = gathered(share)
+    large = every[:, :cut].reshape(-1, BLOCK)
+    squares = every[0, cut:]
+    result = finish(col_index, inverse, large, squares, panel0, panel1, own, rest, total)
+    scale = jnp.sqrt(squares[:columns // BLOCK].reshape(-1) / total + tiny)
+    return (result, jnp.log(scale))
 
 
 def solution(mesh):

time: 179 us -> 201 us (1.12)
  the two profiles are of different devices: /device:TPU:1 before, /device:TPU:71 now
where the time goes in v2:
time: 201 us; the launch traced here: 200 us
  starting transfers between devices  70.9 us (35%)
  waiting for transfers between devices  54.9 us (27%)
  Pallas kernels  33.7 us (17%)
  local copies, waits for them, and re-layouts  19.2 us (10%)
  other arithmetic  12.6 us (6%)
  matrix products  7.27 us (4%)
    ppermute x6, waiting for transfers between devices, spread(): array = array + lax.ppermute(array, 'col', pairs)  43.9 us
    all_to_all x2, starting transfers between devices, scattered(): lax.all_to_all(array.reshape(row_count, -1, BLOCK), 'row', 0, 0)  22.8 us
    pallas_call x2, Pallas kernels, call(): pl.pallas_call(kernel, out_shape=shapes, scratch_shapes=[square] * scratc...  20.4 us
    all_to_all x2, starting transfers between devices, gathered(): return lax.all_to_all(everywhere, 'row', 0, 0)  16.4 us
    unnamed x26, local copies, waits for them, and re-layouts  12.2 us
    ppermute x2, starting transfers between devices, halos(): lax.ppermute(down, 'row', backward)  10.5 us
    pallas_call x1, Pallas kernels, finish(): pl.pallas_call(functools.partial(finish_kernel, total), grid=(count,), in...  9.05 us
    ppermute x1, starting transfers between devices, on_device(): other = lax.ppermute(held, 'col', pairs + [(b, a) for a, b in pairs])  8.61 us
  transfers between devices with their start and end apart: 16, of which 5 were waited for; matrix products, arithmetic and copies ran while one was open for 9% of the time, Pallas kernels for 12%

profile of v2, /device:TPU:71, one launch (start us, length us, event | category | flops | bytes accessed | tf_op | source)
XLA Modules:
  0.0 199.6 jit_solution(16303616782825428040)
XLA Ops:
  0.6 1.0 slice_bitcast_fusion.3
  1.7 1.1 slice_bitcast_fusion.4
  2.7 1.0 pad_maximum_fusion.7
  3.7 2.6 %collective-permute-start.1 = (f32[7,128,128]{2,1,0:T(8,128)}, f32[7,128,128]{2,1,0:T(8,128)S(1)}, u32[]{:S(2)}, u32[]{:S(2)}) collective-permute-start(f32[7,128,128]{2,1,0:T(8,128)} %get-tuple-element.16), channel_id=1, source_target_pairs={{16,0},{32,16},{48,32},{64,48},{80,64},{96,80},{112,96},{128,112},... | collective-permute-start | bytes 1376264 | tf_op jit(solution)/shard_map/ppermute | solution.py:235
  6.3 3.1 %collective-permute-start = (f32[7,128,128]{2,1,0:T(8,128)}, f32[7,128,128]{2,1,0:T(8,128)S(1)}, u32[]{:S(2)}, u32[]{:S(2)}) collective-permute-start(f32[7,128,128]{2,1,0:T(8,128)} %get-tuple-element.17), channel_id=1, source_target_pairs={{0,16},{16,32},{32,48},{48,64},{64,80},{80,96},{96,112},{112,128},... | collective-permute-start | bytes 1376264 | tf_op jit(solution)/shard_map/ppermute | solution.py:235
  9.5 0.6 gather_fusion
  10.1 0.1 subtract_bitcast_fusion
  10.2 3.7 %collective-permute-done.1.high_ref = f32[7,128,128]{2,1,0:T(8,128)S(1)} collective-permute-done((f32[7,128,128]{2,1,0:T(8,128)}, f32[7,128,128]{2,1,0:T(8,128)S(1)}, u32[]{:S(2)}, u32[]{:S(2)}) %collective-permute-start.1) | collective-permute-done | bytes 458784 | tf_op jit(solution)/shard_map/ppermute | solution.py:235
  13.9 1.3 collective-permute-done.low_ref
  15.1 0.8 copy-done.9
  15.9 0.7 broadcast_in_dim.35.coef_ref
  16.7 1.0 copy-done.10
  17.7 0.9 slices.2.own_ref
  18.6 0.6 copy-done.1
  19.2 0.7 collective-permute-start.6
  19.9 0.1 slice_bitcast_fusion
  20.0 0.1 slice_bitcast_fusion.1
  20.1 1.5 collective-permute-start.2
  21.6 0.9 fusion.16
  22.5 1.5 collective-permute-start.7
  23.9 1.8 pad_maximum_fusion.2
  25.8 7.9 %collective-permute-start.11 = (f32[7,128,384]{2,1,0:T(8,128)}, f32[7,128,384]{2,1,0:T(8,128)S(1)}, u32[]{:S(2)}, u32[]{:S(2)}) collective-permute-start(f32[7,128,384]{2,1,0:T(8,128)} %get-tuple-element.14), channel_id=1, source_target_pairs={{16,0},{32,16},{48,32},{64,48},{80,64},{96,80},{112,96},{128,112},... | collective-permute-start | bytes 4128776 | tf_op jit(solution)/shard_map/ppermute | solution.py:235
  33.7 1.9 collective-permute-start.10
  35.7 1.3 add.110
  36.9 1.3 collective-permute-start.8
  38.3 1.0 fusion.7
  39.3 2.1 %fusion.5 = f32[128,128]{1,0:T(8,128)S(1)} fusion(f32[1024,128]{1,0:T(8,128)S(1)} %bitcast.42, f32[1024,128]{1,0:T(8,128)} %collective-permute-done.2, pred[]{:T(512)S(6)} %eq.28), kind=kOutput, calls=%fused_computation.24 | convolution fusion | flops 201588736 | bytes 1114113 | tf_op jit(solution)/shard_map/dot_general | solution.py:26
  41.4 24.3 %collective-permute-done.8 = f32[1024,128]{1,0:T(8,128)S(1)} collective-permute-done((f32[1024,128]{1,0:T(8,128)S(1)}, f32[1024,128]{1,0:T(8,128)S(1)}, u32[]{:S(2)}, u32[]{:S(2)}) %collective-permute-start.8) | collective-permute-done | bytes 524320 | tf_op jit(solution)/shard_map/ppermute | solution.py:257
  65.7 0.8 add.111
  66.6 8.6 %collective-permute-start.9 = (f32[1024,128]{1,0:T(8,128)}, f32[1024,128]{1,0:T(8,128)}, u32[]{:S(2)}, u32[]{:S(2)}) collective-permute-start(f32[1024,128]{1,0:T(8,128)} %add.111), channel_id=1, source_target_pairs={{4,3},{2,1},{0,15},{14,13},{12,11},{10,9},{8,7},{6,5},{3,4},{1,2},... | collective-permute-start | bytes 1572872 | tf_op jit(solution)/shard_map/ppermute | solution.py:280
  75.2 2.2 %fusion.6 = f32[128,128]{1,0:T(8,128)S(1)} fusion(f32[1024,128]{1,0:T(8,128)S(1)} %bitcast.43, f32[1024,128]{1,0:T(8,128)} %collective-permute-done.2, pred[]{:T(512)S(6)} %eq.28), kind=kOutput, calls=%fused_computation.25 | convolution fusion | flops 201457664 | bytes 1114113 | tf_op jit(solution)/shard_map/dot_general | solution.py:26
  77.4 0.9 maximum_maximum_fusion
  78.3 15.4 %all-to-all-start = ((f32[32,16,128]{2,1,0:T(8,128)}), f32[32,16,128]{2,1,0:T(8,128)}, u32[]{:S(2)}, u32[]{:S(2)}) async-start(f32[32,16,128]{2,1,0:T(8,128)} %bitcast.50), calls=%async_computation | async-start | bytes 524288 | tf_op jit(solution)/shard_map/all_to_all | solution.py:261
  93.7 1.1 copy-done.5
  94.8 1.1 copy-done.7
  95.9 1.7 copy-done.2
  97.6 1.6 copy-done.4
  99.2 1.3 copy-done.6
  100.5 1.3 copy-done.8
  101.9 3.3 %slices.3.rest_ref = f32[2,4,128,384]{3,2,1,0:T(8,128)S(1)} custom-call(f32[2,4,128,512]{3,2,1,0:T(8,128)S(1)} %copy-done.4, f32[7,128,384]{2,1,0:T(8,128)S(1)} %copy-done.8, f32[7,128,384]{2,1,0:T(8,128)S(1)} %copy-done.6, f32[4,10,128,128]{3,2,1,0:T(8,128)S(1)} %copy-done.2), custom_call_target="tpu_custom_call" | custom-call | tf_op jit(solution)/shard_map/slices/pallas_call | solution.py:65
  105.2 0.2 multiply_reduce_fusion
  105.4 1.3 broadcast_select_fusion.2
  106.7 1.9 fusion.1
  108.7 0.9 pad_maximum_fusion.6
  109.6 7.4 %all-to-all-start.2 = ((f32[32,40,128]{2,1,0:T(8,128)}), f32[32,40,128]{2,1,0:T(8,128)}, u32[]{:S(2)}, u32[]{:S(2)}) async-start(f32[32,40,128]{2,1,0:T(8,128)} %pad_maximum_fusion.6), calls=%async_computation.2 | async-start | bytes 1310720 | tf_op jit(solution)/shard_map/all_to_all | solution.py:261
  117.0 1.0 reduce_sum.27
  118.0 0.7 collective-permute-start.3
  118.7 0.7 collective-permute-start.4
  119.4 1.3 collective-permute-start.5
  120.7 19.5 %collective-permute-done.5 = f32[16,128]{1,0:T(8,128)S(1)} collective-permute-done((f32[16,128]{1,0:T(8,128)S(1)}, f32[16,128]{1,0:T(8,128)S(1)}, u32[]{:S(2)}, u32[]{:S(2)}) %collective-permute-start.5) | collective-permute-done | bytes 8224 | tf_op jit(solution)/shard_map/ppermute | solution.py:257
  140.2 0.7 broadcast_in_dim.38
  140.9 10.0 %all-to-all-start.1 = ((f32[32,16,128]{2,1,0:T(8,128)}), f32[32,16,128]{2,1,0:T(8,128)}, u32[]{:S(2)}, u32[]{:S(2)}) async-start(f32[32,16,128]{2,1,0:T(8,128)} %broadcast_in_dim.38), calls=%async_computation.1 | async-start | bytes 524288 | tf_op jit(solution)/shard_map/all_to_all | solution.py:265
  151.0 1.1 reduce_sum.29
  152.1 6.0 %all-to-all-done.1 = f32[32,16,128]{2,1,0:T(8,128)} async-done(((f32[32,16,128]{2,1,0:T(8,128)}), f32[32,16,128]{2,1,0:T(8,128)}, u32[]{:S(2)}, u32[]{:S(2)}) %all-to-all-start.1) | async-done | bytes 262176 | tf_op jit(solution)/shard_map/all_to_all | solution.py:265
  158.2 0.9 broadcast_in_dim.40
  159.0 6.4 %all-to-all-start.3 = ((f32[32,40,128]{2,1,0:T(8,128)}), f32[32,40,128]{2,1,0:T(8,128)}, u32[]{:S(2)}, u32[]{:S(2)}) async-start(f32[32,40,128]{2,1,0:T(8,128)} %broadcast_in_dim.40), calls=%async_computation.3 | async-start | bytes 1310720 | tf_op jit(solution)/shard_map/all_to_all | solution.py:265
  165.4 10.2 %factor_a.1 = (f32[128,128]{1,0:T(8,128)S(1)}, f32[128,128]{1,0:T(8,128)S(1)}, f32[128,128]{1,0:T(8,128)S(1)}) custom-call(f32[512,128]{1,0:T(8,128)} %bitcast.8.pack_ref), custom_call_target="tpu_custom_call" | custom-call | flops 2000000000 | bytes 1000000 | tf_op jit(solution)/shard_map/factor_a/pallas_call | solution.py:158
  175.7 10.2 %factor_b.1.inv_ref = f32[256,256]{1,0:T(8,128)S(1)} custom-call(f32[512,128]{1,0:T(8,128)} %bitcast.8.pack_ref, f32[128,128]{1,0:T(8,128)S(1)} %get-tuple-element.5.rest_ref, f32[128,128]{1,0:T(8,128)S(1)} %get-tuple-element.6.inv0_ref, f32[128,128]{1,0:T(8,128)S(1)} %get-tuple-element.7.cross_ref), custom_call_target="tpu_custom_call" | custom-call | flops 2000000000 | bytes 1000000 | tf_op jit(solution)/shard_map/factor_b/pallas_call | solution.py:158
  185.9 0.7 copy-done.11
  186.6 0.7 slice_bitcast_fusion.6.squares_ref
  187.3 1.1 slice.62
  188.4 0.9 copy-done.12
  189.3 9.1 %finish.1 = f32[2,4,128,512]{3,2,1,0:T(8,128)} custom-call(s32[1]{0:T(128)} %bitcast.place_ref, f32[256,256]{1,0:T(8,128)S(1)} %copy-done.12, f32[1024,128]{1,0:T(8,128)S(1)} %bitcast.48, f32[8,128]{1,0:T(8,128)S(1)} %slice_bitcast_fusion.6.squares_ref, f32[1024,128]{1,0:T(8,128)S(1)} %get-tuple-element.12.panel0_ref, ...), custom_call_target="tpu_custom_call" | custom-call | tf_op jit(solution)/shard_map/finish/pallas_call | solution.py:199
  198.4 1.3 fusion.11
  (38 shorter events, 0.2 us)
Async XLA Ops:
  0.6 8.8 %copy-start = (s32[4,128,128]{2,1,0:T(8,128)S(1)}, s32[4,128,128]{2,1,0:T(8,128)}, u32[]{:S(2)}) copy-start(s32[4,128,128]{2,1,0:T(8,128)} %param.3) | copy-start | bytes 786436
  2.7 13.9 %copy-start.3 = (f32[2,4,128,512]{3,2,1,0:T(8,128)S(1)}, f32[2,4,128,512]{3,2,1,0:T(8,128)}, u32[]{:S(2)}) copy-start(f32[2,4,128,512]{3,2,1,0:T(8,128)} %vec_ref.3) | copy-start | bytes 6291460
  3.7 10.1 %collective-permute-start.1 = (f32[7,128,128]{2,1,0:T(8,128)}, f32[7,128,128]{2,1,0:T(8,128)S(1)}, u32[]{:S(2)}, u32[]{:S(2)}) collective-permute-start(f32[7,128,128]{2,1,0:T(8,128)} %get-tuple-element.16), channel_id=1, source_target_pairs={{16,0},{32,16},{48,32},{64,48},{80,64},{96,80},{112,96},{128,112},... | collective-permute-start | bytes 1376264 | tf_op jit(solution)/shard_map/ppermute | solution.py:235
  6.3 8.8 %collective-permute-start = (f32[7,128,128]{2,1,0:T(8,128)}, f32[7,128,128]{2,1,0:T(8,128)S(1)}, u32[]{:S(2)}, u32[]{:S(2)}) collective-permute-start(f32[7,128,128]{2,1,0:T(8,128)} %get-tuple-element.17), channel_id=1, source_target_pairs={{0,16},{16,32},{32,48},{48,64},{64,80},{80,96},{96,112},{112,128},... | collective-permute-start | bytes 1376264 | tf_op jit(solution)/shard_map/ppermute | solution.py:235
  15.1 0.8 copy-start.9
  16.7 1.0 copy-start.10
  17.7 1.5 copy-start.1
  19.2 2.3 %collective-permute-start.6 = (f32[1024,128]{1,0:T(8,128)S(1)}, f32[1024,128]{1,0:T(8,128)S(1)}, u32[]{:S(2)}, u32[]{:S(2)}) collective-permute-start(f32[1024,128]{1,0:T(8,128)S(1)} %broadcast_select_fusion), channel_id=1, source_target_pairs={{0,9},{1,8},{16,25},{17,24},{32,41},{33,40},{48,57},{49,56},{64,73... | collective-permute-start | bytes 1572872 | tf_op jit(solution)/shard_map/ppermute | solution.py:257
  20.1 18.1 %collective-permute-start.2 = (f32[1024,128]{1,0:T(8,128)S(1)}, f32[1024,128]{1,0:T(8,128)}, u32[]{:S(2)}, u32[]{:S(2)}) collective-permute-start(f32[1024,128]{1,0:T(8,128)S(1)} %bitcast.40), channel_id=1, source_target_pairs={{0,1},{1,0},{16,17},{17,16},{32,33},{33,32},{48,49},{49,48},{64,65... | collective-permute-start | bytes 1572872 | tf_op jit(solution)/shard_map/ppermute | solution.py:267
  22.5 13.2 %collective-permute-start.7 = (f32[1024,128]{1,0:T(8,128)}, f32[1024,128]{1,0:T(8,128)}, u32[]{:S(2)}, u32[]{:S(2)}) collective-permute-start(f32[1024,128]{1,0:T(8,128)} %fusion.16), channel_id=1, source_target_pairs={{0,4},{8,12},{1,13},{9,5},{16,20},{24,28},{17,29},{25,21},{32,36},... | collective-permute-start | bytes 1572872 | tf_op jit(solution)/shard_map/ppermute | solution.py:257
  25.8 67.9 %collective-permute-start.11 = (f32[7,128,384]{2,1,0:T(8,128)}, f32[7,128,384]{2,1,0:T(8,128)S(1)}, u32[]{:S(2)}, u32[]{:S(2)}) collective-permute-start(f32[7,128,384]{2,1,0:T(8,128)} %get-tuple-element.14), channel_id=1, source_target_pairs={{16,0},{32,16},{48,32},{64,48},{80,64},{96,80},{112,96},{128,112},... | collective-permute-start | bytes 4128776 | tf_op jit(solution)/shard_map/ppermute | solution.py:235
  33.7 61.1 %collective-permute-start.10 = (f32[7,128,384]{2,1,0:T(8,128)}, f32[7,128,384]{2,1,0:T(8,128)S(1)}, u32[]{:S(2)}, u32[]{:S(2)}) collective-permute-start(f32[7,128,384]{2,1,0:T(8,128)} %get-tuple-element.15), channel_id=1, source_target_pairs={{0,16},{16,32},{32,48},{48,64},{64,80},{80,96},{96,112},{112,128},... | collective-permute-start | bytes 4128776 | tf_op jit(solution)/shard_map/ppermute | solution.py:235
  36.9 28.8 %collective-permute-start.8 = (f32[1024,128]{1,0:T(8,128)S(1)}, f32[1024,128]{1,0:T(8,128)S(1)}, u32[]{:S(2)}, u32[]{:S(2)}) collective-permute-start(f32[1024,128]{1,0:T(8,128)S(1)} %add.110), channel_id=1, source_target_pairs={{1,3},{13,15},{5,7},{9,11},{4,2},{0,14},{8,6},{12,10},{17,19},{29,... | collective-permute-start | bytes 1572872 | tf_op jit(solution)/shard_map/ppermute | solution.py:257
  66.6 38.8 %collective-permute-start.9 = (f32[1024,128]{1,0:T(8,128)}, f32[1024,128]{1,0:T(8,128)}, u32[]{:S(2)}, u32[]{:S(2)}) collective-permute-start(f32[1024,128]{1,0:T(8,128)} %add.111), channel_id=1, source_target_pairs={{4,3},{2,1},{0,15},{14,13},{12,11},{10,9},{8,7},{6,5},{3,4},{1,2},... | collective-permute-start | bytes 1572872 | tf_op jit(solution)/shard_map/ppermute | solution.py:280
  78.3 31.3 %all-to-all-start = ((f32[32,16,128]{2,1,0:T(8,128)}), f32[32,16,128]{2,1,0:T(8,128)}, u32[]{:S(2)}, u32[]{:S(2)}) async-start(f32[32,16,128]{2,1,0:T(8,128)} %bitcast.50), calls=%async_computation | async-start | bytes 524288 | tf_op jit(solution)/shard_map/all_to_all | solution.py:261
  93.7 1.1 copy-start.5
  94.8 1.1 copy-start.7
  95.9 1.7 copy-start.2
  97.6 1.6 copy-start.4
  99.2 1.3 copy-start.6
  100.5 1.3 copy-start.8
  109.6 30.7 %all-to-all-start.2 = ((f32[32,40,128]{2,1,0:T(8,128)}), f32[32,40,128]{2,1,0:T(8,128)}, u32[]{:S(2)}, u32[]{:S(2)}) async-start(f32[32,40,128]{2,1,0:T(8,128)} %pad_maximum_fusion.6), calls=%async_computation.2 | async-start | bytes 1310720 | tf_op jit(solution)/shard_map/all_to_all | solution.py:261
  118.0 0.7 collective-permute-start.3
  118.7 0.7 collective-permute-start.4
  119.4 20.8 %collective-permute-start.5 = (f32[16,128]{1,0:T(8,128)S(1)}, f32[16,128]{1,0:T(8,128)S(1)}, u32[]{:S(2)}, u32[]{:S(2)}) collective-permute-start(f32[16,128]{1,0:T(8,128)S(1)} %add.107), channel_id=1, source_target_pairs={{1,3},{13,15},{5,7},{9,11},{4,2},{0,14},{8,6},{12,10},{17,19},{29,... | collective-permute-start | bytes 24584 | tf_op jit(solution)/shard_map/ppermute | solution.py:257
  140.9 17.2 %all-to-all-start.1 = ((f32[32,16,128]{2,1,0:T(8,128)}), f32[32,16,128]{2,1,0:T(8,128)}, u32[]{:S(2)}, u32[]{:S(2)}) async-start(f32[32,16,128]{2,1,0:T(8,128)} %broadcast_in_dim.38), calls=%async_computation.1 | async-start | bytes 524288 | tf_op jit(solution)/shard_map/all_to_all | solution.py:265
  159.0 27.5 %all-to-all-start.3 = ((f32[32,40,128]{2,1,0:T(8,128)}), f32[32,40,128]{2,1,0:T(8,128)}, u32[]{:S(2)}, u32[]{:S(2)}) async-start(f32[32,40,128]{2,1,0:T(8,128)} %broadcast_in_dim.40), calls=%async_computation.3 | async-start | bytes 1310720 | tf_op jit(solution)/shard_map/all_to_all | solution.py:265
  185.9 0.7 copy-start.11
  188.4 1.0 copy-start.12

commit v3 on v2

v3 whole, which is shorter than its diff:
```python
import functools

import jax
import jax.numpy as jnp
from jax import lax
from jax.experimental import pallas as pl
from jax.experimental.pallas import tpu as pltpu
from jax.sharding import PartitionSpec as P

PANEL = 128
LEVELS = 4096
BLOCK = 128
SMALL = 16

energy = 0.25
disorder = 16.5
tiny = 1e-06
highest = lax.Precision.HIGHEST
MIB = 2**20


def site_values(codes):
    return disorder * ((codes.astype(jnp.float32) + 0.5) / LEVELS - 0.5)


def dot(left, right, contract):
    return lax.dot_general(
        left, right, ((contract[:1], contract[1:]), ((), ())),
        precision=highest, preferred_element_type=jnp.float32,
    )


def stencil_kernel(depth, vec_ref, low_ref, high_ref, coef_ref, out_ref, a_ref, b_ref):
    rows = vec_ref.shape[1]
    for i in range(rows):
        a_ref[i] = low_ref[0, i]
        a_ref[rows + i] = vec_ref[0, i]
        a_ref[2 * rows + i] = high_ref[0, i]
        b_ref[i] = low_ref[1, i]
        b_ref[rows + i] = vec_ref[1, i]
        b_ref[2 * rows + i] = high_ref[1, i]
    current, previous = a_ref, b_ref
    sites = vec_ref.shape[2]
    for step in range(depth):
        reach = depth - 1 - step

        def one_row(i, _, current=current, previous=previous, step=step):
            center = current[i]
            beside = current[i + 1] + current[i - 1]
            beside = beside + pltpu.roll(center, 1, 0) + pltpu.roll(center, sites - 1, 0)
            previous[i] = coef_ref[step, i - rows + depth - 1] * center - beside - previous[i]
            return 0

        lax.fori_loop(rows - reach, 2 * rows + reach, one_row, 0)
        current, previous = previous, current
    for i in range(rows):
        out_ref[0, i] = current[rows + i]
        out_ref[1, i] = previous[rows + i]


def stencil(vectors, low, high, coefs):
    _, rows, sites, columns = vectors.shape
    block = pl.BlockSpec((2, rows, sites, BLOCK), lambda i: (0, 0, 0, i))
    return pl.pallas_call(
        functools.partial(stencil_kernel, coefs.shape[0]),
        grid=(columns // BLOCK,),
        in_specs=[block, block, block, pl.BlockSpec(coefs.shape, lambda i: (0, 0, 0, 0))],
        out_specs=block,
        out_shape=jax.ShapeDtypeStruct(vectors.shape, jnp.float32),
        scratch_shapes=[pltpu.VMEM((3 * rows, sites, BLOCK), jnp.float32)] * 2,
        compiler_params=pltpu.CompilerParams(vmem_limit_bytes=40 * MIB),
        name="slices",
    )(vectors, low, high, coefs)


def eliminate(mat_ref, inv_ref):
    size = mat_ref.shape[0]
    step = 8
    wide = (step, 2 * size)
    lanes = lax.broadcasted_iota(jnp.int32, (step, size), 1)
    subs = lax.broadcasted_iota(jnp.int32, wide, 0)
    inv_ref[...] = identity(size)
    for first in range(0, size, step):
        last = first + step
        both = jnp.concatenate([mat_ref[first:last], inv_ref[first:last]], 1)
        columns = [jnp.broadcast_to(both[:, first + k:first + k + 1], (step, size)) for k in range(step)]
        entry = [[jnp.broadcast_to(columns[k][i:i + 1], (step, size)) for k in range(i + 1)] for i in range(step)]
        rows = [jnp.broadcast_to(both[i:i + 1], wide) for i in range(step)]
        result = jnp.zeros(wide, jnp.float32)
        for k in range(step):
            root = lax.rsqrt(entry[k][k])
            done = rows[k] * jnp.concatenate([root, root], 1)
            result = jnp.where(subs == k, done, result)
            lower = {i: entry[i][k] * root for i in range(k + 1, step)}
            for i in range(k + 1, step):
                for j in range(k + 1, i + 1):
                    entry[i][j] = entry[i][j] - lower[i] * lower[j]
                rows[i] = rows[i] - jnp.concatenate([lower[i], lower[i]], 1) * done
        inv_ref[first:last] = result[:, size:]
        if last < size:
            below = jnp.where(lanes >= last, result[:, :size], 0.0)
            change = dot(below, result, (0, 0))
            mat_ref[last:] = mat_ref[last:] - change[last:, :size]
            inv_ref[last:] = inv_ref[last:] - change[last:, size:]


def identity(size):
    lanes = lax.broadcasted_iota(jnp.int32, (size, size), 1)
    subs = lax.broadcasted_iota(jnp.int32, (size, size), 0)
    return jnp.where(lanes == subs, 1.0, 0.0).astype(jnp.float32)


def block_scales(block, total):
    diag = identity(PANEL) * block
    along = lax.rsqrt(jnp.sum(diag, axis=0, keepdims=True) / total + tiny)
    down = lax.rsqrt(jnp.sum(diag, axis=1, keepdims=True) / total + tiny)
    return along, down


def products_block(sums_ref, index):
    each = sums_ref.shape[0] // 4
    return sums_ref[index * each:(index + 1) * each, :SMALL].reshape(PANEL, PANEL)


def first_kernel(total, sums_ref, rest_ref, inv_ref, cross_ref, mat_ref):
    block = products_block(sums_ref, 0)
    along0, down0 = block_scales(block, total)
    mat_ref[...] = block * down0 * along0 / total
    eliminate(mat_ref, inv_ref)
    block = products_block(sums_ref, 2)
    along1, down1 = block_scales(block, total)
    cross = dot(inv_ref[...], products_block(sums_ref, 1) * down0 * along1 / total, (1, 0))
    cross_ref[...] = cross
    rest_ref[...] = block * down1 * along1 / total - dot(cross, cross, (0, 0))


def second_kernel(total, sums_ref, rest_ref, inv0_ref, cross_ref, out_ref, mat_ref, inv_ref):
    mat_ref[...] = rest_ref[...]
    eliminate(mat_ref, inv_ref)
    along0, _ = block_scales(products_block(sums_ref, 0), total)
    along1, _ = block_scales(products_block(sums_ref, 2), total)
    inv0 = inv0_ref[...]
    inv1 = inv_ref[...]
    mixed = -dot(dot(inv1, cross_ref[...], (1, 1)), inv0, (1, 0))
    out_ref[0:PANEL, 0:PANEL] = inv0 * along0
    out_ref[0:PANEL, PANEL:] = jnp.zeros((PANEL, PANEL), jnp.float32)
    out_ref[PANEL:, 0:PANEL] = mixed * along0
    out_ref[PANEL:, PANEL:] = inv1 * along1


def call(kernel, name, outs, scratch, *args):
    square = pltpu.VMEM((PANEL, PANEL), jnp.float32)
    shapes = [jax.ShapeDtypeStruct((k * PANEL, k * PANEL), jnp.float32) for k in outs]
    return pl.pallas_call(
        kernel,
        out_shape=shapes,
        scratch_shapes=[square] * scratch,
        compiler_params=pltpu.CompilerParams(vmem_limit_bytes=16 * MIB),
        cost_estimate=pl.CostEstimate(flops=2 * 10**9, bytes_accessed=10**6, transcendentals=0),
        name=name,
    )(*args)


def first_half(sums, total):
    return call(functools.partial(first_kernel, total), "factor_a", [1, 1, 1], 1, sums)


def second_half(sums, rest, inv0, cross, total):
    return call(functools.partial(second_kernel, total), "factor_b", [2], 2, sums, rest, inv0, cross)[0]


def finish_kernel(total, place_ref, inv_ref, sums_ref, panel0_ref, panel1_ref, matrix_ref,
                  out_ref, growth_ref, weights_ref, factors_ref):
    count = out_ref.shape[3] // BLOCK
    place = place_ref[0]
    holder = place < 2
    wide = (1, count * BLOCK)

    @pl.when(pl.program_id(0) == 0)
    def _():
        each = sums_ref.shape[0] // count
        inverse = inv_ref[...]
        sums = [sums_ref[each * i:each * (i + 1), SMALL:].reshape(2 * PANEL, BLOCK) for i in range(count)]
        part = dot(inverse, jnp.concatenate(sums, 1), (1, 0)) / total
        subs = lax.broadcasted_iota(jnp.int32, part.shape, 0)
        lanes = lax.broadcasted_iota(jnp.int32, part.shape, 1)
        chosen = jnp.where(subs == lanes + place * PANEL, -1.0, 0.0)
        part = jnp.where(jnp.logical_and(lanes < PANEL, holder), chosen, part)
        weights_ref[...] = dot(inverse, part, (0, 0))
        place4 = 3 * sums_ref.shape[0] // 4
        squares = jnp.concatenate([sums_ref[place4, i:i + 1] for i in range(count)], 1)
        scale = jnp.sqrt(squares / total + tiny)
        growth_ref[...] = jnp.log(scale)
        in_panel = jnp.logical_and(lax.broadcasted_iota(jnp.int32, wide, 1) < PANEL, holder)
        factors_ref[0:1] = jnp.where(in_panel, 0.0, 1.0)
        factors_ref[1:2] = jnp.where(in_panel, 1.0, 1.0 / scale)

    panels = jnp.concatenate([panel0_ref[...], panel1_ref[...]], 1)
    taken = dot(panels, weights_ref[...], (1, 0))
    rows = taken.shape[0]
    block = matrix_ref[...].reshape(rows, -1)
    out_ref[...] = ((block * factors_ref[0:1] - taken) * factors_ref[1:2]).reshape(out_ref.shape)


def finish(col_index, inverse, sums, panel0, panel1, matrix, total):
    _, rows, sites, columns = matrix.shape
    steps = 2 if rows % 2 == 0 else 1
    block = pl.BlockSpec((1, rows // steps, sites, columns), lambda i: (i // steps, i % steps, 0, 0))
    fixed = lambda array: pl.BlockSpec(array.shape, lambda i: (0,) * array.ndim)
    panel = pl.BlockSpec((rows // steps * sites, PANEL), lambda i: (i, 0))
    return pl.pallas_call(
        functools.partial(finish_kernel, total),
        grid=(2 * steps,),
        in_specs=[
            pl.BlockSpec(memory_space=pltpu.SMEM),
            fixed(inverse),
            fixed(sums),
            panel,
            panel,
            block,
        ],
        out_specs=[block, pl.BlockSpec((1, columns), lambda i: (0, 0))],
        out_shape=[
            jax.ShapeDtypeStruct((2, rows, sites, columns), jnp.float32),
            jax.ShapeDtypeStruct((1, columns), jnp.float32),
        ],
        scratch_shapes=[
            pltpu.VMEM((2 * PANEL, columns), jnp.float32),
            pltpu.VMEM((8, columns), jnp.float32),
        ],
        compiler_params=pltpu.CompilerParams(vmem_limit_bytes=40 * MIB),
        name="finish",
    )(col_index.reshape(1), inverse, sums, panel0, panel1, matrix)


def on_device(vectors, potential):
    depth = potential.shape[0]
    _, rows, sites, columns = vectors.shape
    row_count = lax.axis_size("row")
    row_index = lax.axis_index("row")
    col_index = lax.axis_index("col")
    total = 2 * rows * sites * row_count

    col_count = lax.axis_size("col")

    def neighbours(block, cols):
        ahead = [(i * col_count + c, (i + 1) % row_count * col_count + c) for i in range(row_count) for c in cols]
        back = [(target, source) for source, target in ahead]
        return lax.ppermute(block, ("row", "col"), ahead), lax.ppermute(block, ("row", "col"), back)

    site_rows = (row_index * rows - depth + 1 + jnp.arange(rows + 2 * depth - 2)) % potential.shape[1]
    coefs = energy - site_values(jnp.take(potential, site_rows, axis=1))
    coefs = jnp.broadcast_to(coefs[..., None], coefs.shape + (BLOCK,))

    panel = vectors[..., :PANEL]
    panel = stencil(panel, *neighbours(panel, [0, 1]), coefs).reshape(-1, PANEL)
    held = jnp.where(col_index < 2, panel, 0.0)
    stages = [
        [(0, 9), (1, 8)],
        [(0, 4), (8, 12), (1, 13), (9, 5)],
        [(1, 3), (13, 15), (5, 7), (9, 11), (4, 2), (0, 14), (8, 6), (12, 10)],
    ]
    for pairs in stages:
        held = held + lax.ppermute(held, "col", pairs)
    pairs = [(4, 3), (2, 1), (0, 15), (14, 13), (12, 11), (10, 9), (8, 7), (6, 5)]
    other = lax.ppermute(held, "col", pairs + [(b, a) for a, b in pairs])
    has_first = functools.reduce(jnp.logical_or, [col_index == c for c in (0, 2, 4, 5, 7, 9, 11, 14)])
    panel0 = jnp.where(has_first, held, other)
    panel1 = jnp.where(has_first, other, held)

    blocks = stencil(vectors, *neighbours(vectors, range(col_count)), coefs)
    matrix = blocks.reshape(-1, columns)
    panels = jnp.concatenate([panel0, panel1], 1)
    coeffs = dot(panels, matrix, (0, 0))
    products = dot(panels, panels, (0, 0))
    squares = jnp.sum(matrix * matrix, 0).reshape(-1, BLOCK)
    small = jnp.concatenate([
        products[:PANEL, :PANEL],
        products[:PANEL, PANEL:],
        products[PANEL:, PANEL:],
        jnp.pad(squares, ((0, PANEL - squares.shape[0]), (0, 0))),
    ], 0)
    large = jnp.moveaxis(coeffs.reshape(2 * PANEL, -1, BLOCK), 1, 0)

    sums = jnp.concatenate([small.reshape(row_count, -1, BLOCK), large.reshape(row_count, -1, BLOCK)], 1)
    share = jnp.sum(lax.all_to_all(sums, "row", 0, 0), 0)
    sums = lax.all_to_all(jnp.broadcast_to(share, (row_count,) + share.shape), "row", 0, 0)
    inverse = second_half(sums, *first_half(sums, total), total)
    result, growth = finish(col_index, inverse, sums, panel0, panel1, blocks, total)
    return (result, growth.reshape(-1))


def solution(mesh):
    return jax.shard_map(
        on_device,
        mesh=mesh,
        in_specs=(P(None, "row", None, "col"), P()),
        out_specs=(P(None, "row", None, "col"), P("col")),
        check_vma=False,
    )
```

time: 201 us -> 162 us (0.81)
  the two profiles are of different devices: /device:TPU:71 before, /device:TPU:289 now
where the time goes in v3:
time: 162 us; the launch traced here: 161 us
  blocking collectives  57.6 us (36%)
  waiting for transfers between devices  37 us (23%)
  Pallas kernels  29.8 us (18%)
  starting transfers between devices  16.3 us (10%)
  local copies, waits for them, and re-layouts  10.9 us (7%)
  matrix products  5.4 us (3%)
  other arithmetic  2.91 us (2%)
    all_to_all x1, blocking collectives, on_device(): share = jnp.sum(lax.all_to_all(sums, 'row', 0, 0), 0)  39.8 us
    ppermute x3, waiting for transfers between devices, on_device(): held = held + lax.ppermute(held, 'col', pairs)  37 us
    pallas_call x2, Pallas kernels, call(): pl.pallas_call(kernel, out_shape=shapes, scratch_shapes=[square] * scratc...  18.5 us
    all_to_all x1, blocking collectives, on_device(): lax.all_to_all(jnp.broadcast_to(share, (row_count,) + share.shape), 'row'...  17.9 us
    unnamed x20, local copies, waits for them, and re-layouts  6.57 us
    pallas_call x2, Pallas kernels, stencil(): pl.pallas_call(functools.partial(stencil_kernel, coefs.shape[0]), grid=(c...  6.5 us
    dot_general x2, matrix products, dot(): lax.dot_general(left, right, ((contract[:1], contract[1:]), ((), ())), pr...  5.4 us
    ppermute x1, starting transfers between devices, on_device(): other = lax.ppermute(held, 'col', pairs + [(b, a) for a, b in pairs])  5.13 us
  transfers between devices with their start and end apart: 8, of which 3 were waited for; matrix products, arithmetic and copies ran while one was open for 2% of the time, Pallas kernels for 3%

profile of v3, /device:TPU:289, one launch (start us, length us, event | category | flops | bytes accessed | tf_op | source)
XLA Modules:
  0.0 160.9 jit_solution(13834722638970384848)
XLA Ops:
  0.6 0.0 copy-start
  0.6 1.1 slice.11.vec_ref
  1.8 0.7 collective-permute-start
  2.5 0.7 collective-permute-start.1
  3.2 0.0 copy-done
  3.2 0.6 gather_fusion
  3.9 0.1 subtract_bitcast_fusion
  3.9 0.0 collective-permute-done.low_ref
  3.9 0.0 collective-permute-done.1.high_ref
  4.0 0.0 copy-start.5
  4.0 0.8 copy-done.5
  4.8 0.7 broadcast_in_dim.25.coef_ref
  5.5 0.0 copy-start.6
  5.5 1.0 copy-done.6
  6.5 0.0 copy-start.1
  6.5 0.0 copy-start.3
  6.5 0.9 slices.2
  7.5 0.6 copy-done.1
  8.1 1.4 collective-permute-start.2
  9.5 0.0 copy-done.3
  9.5 3.8 %collective-permute-start.6 = (f32[2,4,128,512]{3,2,1,0:T(8,128)S(1)}, f32[2,4,128,512]{3,2,1,0:T(8,128)}, u32[]{:S(2)}, u32[]{:S(2)}) collective-permute-start(f32[2,4,128,512]{3,2,1,0:T(8,128)S(1)} %copy-done.3), channel_id=1, source_target_pairs={{0,16},{1,17},{2,18},{3,19},{4,20},{5,21},{6,22},{7,23},{8,24},{9,... | collective-permute-start | bytes 6291464 | tf_op jit(solution)/shard_map/ppermute | solution.py:249
  13.3 1.9 %collective-permute-start.7 = (f32[2,4,128,512]{3,2,1,0:T(8,128)S(1)}, f32[2,4,128,512]{3,2,1,0:T(8,128)}, u32[]{:S(2)}, u32[]{:S(2)}) collective-permute-start(f32[2,4,128,512]{3,2,1,0:T(8,128)S(1)} %copy-done.3), channel_id=1, source_target_pairs={{16,0},{17,1},{18,2},{19,3},{20,4},{21,5},{22,6},{23,7},{24,8},{25... | collective-permute-start | bytes 6291464 | tf_op jit(solution)/shard_map/ppermute | solution.py:249
  15.2 10.7 %collective-permute-done.2 = f32[1024,128]{1,0:T(8,128)S(1)} collective-permute-done((f32[1024,128]{1,0:T(8,128)S(1)}, f32[1024,128]{1,0:T(8,128)S(1)}, u32[]{:S(2)}, u32[]{:S(2)}) %collective-permute-start.2) | collective-permute-done | bytes 524320 | tf_op jit(solution)/shard_map/ppermute | solution.py:264
  26.0 0.1 bitcast_add_fusion
  26.0 1.3 collective-permute-start.3
  27.3 6.1 %collective-permute-done.3 = f32[1024,128]{1,0:T(8,128)S(1)} collective-permute-done((f32[1024,128]{1,0:T(8,128)S(1)}, f32[1024,128]{1,0:T(8,128)S(1)}, u32[]{:S(2)}, u32[]{:S(2)}) %collective-permute-start.3) | collective-permute-done | bytes 524320 | tf_op jit(solution)/shard_map/ppermute | solution.py:264
  33.4 0.1 add.91
  33.5 1.3 collective-permute-start.4
  34.8 20.2 %collective-permute-done.4 = f32[1024,128]{1,0:T(8,128)S(1)} collective-permute-done((f32[1024,128]{1,0:T(8,128)S(1)}, f32[1024,128]{1,0:T(8,128)S(1)}, u32[]{:S(2)}, u32[]{:S(2)}) %collective-permute-start.4) | collective-permute-done | bytes 524320 | tf_op jit(solution)/shard_map/ppermute | solution.py:264
  55.0 0.1 add.92
  55.1 0.0 copy-start.8
  55.1 5.1 %collective-permute-start.5 = (f32[1024,128]{1,0:T(8,128)S(1)}, f32[1024,128]{1,0:T(8,128)}, u32[]{:S(2)}, u32[]{:S(2)}) collective-permute-start(f32[1024,128]{1,0:T(8,128)S(1)} %add.92), channel_id=1, source_target_pairs={{4,3},{2,1},{0,15},{14,13},{12,11},{10,9},{8,7},{6,5},{3,4},{1,2},... | collective-permute-start | bytes 1572872 | tf_op jit(solution)/shard_map/ppermute | solution.py:266
  60.2 0.0 collective-permute-done.6.low_ref
  60.3 0.0 collective-permute-done.7.high_ref
  60.3 0.0 copy-start.2
  60.3 1.7 %copy-done.2 = f32[4,10,128,128]{3,2,1,0:T(8,128)S(1)} copy-done((f32[4,10,128,128]{3,2,1,0:T(8,128)S(1)}, f32[4,10,128,128]{3,2,1,0:T(8,128)}, u32[]{:S(2)}) %copy-start.2) | copy-done | bytes 2621464
  62.0 0.0 copy-start.4
  62.0 1.6 copy-done.4
  63.6 5.6 %slices.3.matrix_ref = f32[2,4,128,512]{3,2,1,0:T(8,128)S(1)} custom-call(f32[2,4,128,512]{3,2,1,0:T(8,128)S(1)} %copy-done.4, f32[2,4,128,512]{3,2,1,0:T(8,128)} %collective-permute-done.6.low_ref, f32[2,4,128,512]{3,2,1,0:T(8,128)} %collective-permute-done.7.high_ref, f32[4,10,128,128]{3,2,1,0:T(8,128)S(1)} %copy-done.2), custom_call_target="tpu_custom_call" | custom-call | tf_op jit(solution)/shard_map/slices/pallas_call | solution.py:64
  69.2 0.0 copy-done.8
  69.2 1.8 %copy.6 = f32[512,1024]{1,0:T(8,128)} copy(f32[512,1024]{0,1:T(8,128)S(1)} %bitcast.21) | data formatting | bytes 4194304 | tf_op jit(solution)/shard_map/dot_general | solution.py:27
  71.0 0.0 copy-start.9
  71.0 0.2 multiply_reduce_fusion
  71.3 0.0 copy-start.7
  71.3 0.0 collective-permute-done.5
  71.3 0.8 copy-done.9
  72.1 1.1 broadcast_select_fusion.2
  73.2 1.8 %fusion.2 = f32[256,256]{1,0:T(8,128)S(1)} fusion(f32[1024,128]{1,0:T(8,128)S(1)} %get-tuple-element.13.panel1_ref, f32[1024,128]{1,0:T(8,128)S(1)} %get-tuple-element.12.panel0_ref), kind=kOutput, calls=%fused_computation.5 | convolution fusion | flops 805568512 | bytes 1310720 | tf_op jit(solution)/shard_map/dot_general | solution.py:27
  75.1 0.0 copy-done.7
  75.1 3.6 %fusion = f32[256,4,128]{2,0,1:T(8,128)S(1)} fusion(f32[4,128,1024]{2,1,0:T(8,128)S(1)} %bitcast.22, f32[1024,128]{1,0:T(8,128)S(1)} %get-tuple-element.13.panel1_ref, f32[1024,128]{1,0:T(8,128)S(1)} %get-tuple-element.12.panel0_ref), kind=kOutput, calls=%fused_computation.3 | convolution fusion | flops 1610874880 | bytes 3670016 | tf_op jit(solution)/shard_map/dot_general | solution.py:27
  78.7 0.1 pad_maximum_fusion.3
  78.7 39.8 %all_to_all.10 = f32[32,48,128]{2,1,0:T(8,128)} all-to-all(f32[32,48,128]{2,1,0:T(8,128)S(1)} %pad_maximum_fusion.3), channel_id=1, replica_groups=mesh['row'=32,'col'=16] {'row'}, dimensions={0} | all-to-all | bytes 1572864 | tf_op jit(solution)/shard_map/all_to_all | solution.py:286
  118.5 1.2 reduce_sum.19
  119.7 0.1 broadcast_in_dim.27
  119.8 17.9 %all_to_all.11.sums_ref = f32[32,48,128]{2,1,0:T(8,128)S(1)} all-to-all(f32[32,48,128]{2,1,0:T(8,128)S(1)} %broadcast_in_dim.27), channel_id=1, replica_groups=mesh['row'=32,'col'=16] {'row'}, dimensions={0} | all-to-all | bytes 1572864 | tf_op jit(solution)/shard_map/all_to_all | solution.py:287
  137.6 9.3 %factor_a.1 = (f32[128,128]{1,0:T(8,128)S(1)}, f32[128,128]{1,0:T(8,128)S(1)}, f32[128,128]{1,0:T(8,128)S(1)}) custom-call(f32[32,48,128]{2,1,0:T(8,128)S(1)} %all_to_all.11.sums_ref), custom_call_target="tpu_custom_call" | custom-call | flops 2000000000 | bytes 1000000 | tf_op jit(solution)/shard_map/factor_a/pallas_call | solution.py:154
  146.9 9.3 %factor_b.1.inv_ref = f32[256,256]{1,0:T(8,128)S(1)} custom-call(f32[32,48,128]{2,1,0:T(8,128)S(1)} %all_to_all.11.sums_ref, f32[128,128]{1,0:T(8,128)S(1)} %get-tuple-element.7.rest_ref, f32[128,128]{1,0:T(8,128)S(1)} %get-tuple-element.8.inv0_ref, f32[128,128]{1,0:T(8,128)S(1)} %get-tuple-element.9.cross_ref), custom_call_target="tpu_custom_call" | custom-call | flops 2000000000 | bytes 1000000 | tf_op jit(solution)/shard_map/factor_b/pallas_call | solution.py:154
  156.2 4.8 %finish.1 = (f32[2,4,128,512]{3,2,1,0:T(8,128)}, f32[1,512]{1,0:T(1,128)}) custom-call(s32[1]{0:T(128)} %bitcast.place_ref, f32[256,256]{1,0:T(8,128)S(1)} %factor_b.1.inv_ref, f32[32,48,128]{2,1,0:T(8,128)S(1)} %all_to_all.11.sums_ref, f32[1024,128]{1,0:T(8,128)S(1)} %get-tuple-element.12.panel0_ref, f32[1024,128]{1,0:T(8,128)S(1)} %get-tuple-element.13.panel1_ref, ...), custom_call_target="tpu_custom_call" | custom-call | tf_op jit(solution)/shard_map/finish/pallas_call | solution.py:211
  (7 shorter events, 0.1 us)
Async XLA Ops:
  0.6 2.6 %copy-start = (s32[4,128,128]{2,1,0:T(8,128)S(1)}, s32[4,128,128]{2,1,0:T(8,128)}, u32[]{:S(2)}) copy-start(s32[4,128,128]{2,1,0:T(8,128)} %param.3) | copy-start | bytes 786436
  1.8 2.2 %collective-permute-start = (f32[2,4,128,128]{3,2,1,0:T(8,128)S(1)}, f32[2,4,128,128]{3,2,1,0:T(8,128)S(1)}, u32[]{:S(2)}, u32[]{:S(2)}) collective-permute-start(f32[2,4,128,128]{3,2,1,0:T(8,128)S(1)} %slice.11.vec_ref), channel_id=1, source_target_pairs={{0,16},{1,17},{16,32},{17,33},{32,48},{33,49},{48,64},{49,65},{64,... | collective-permute-start | bytes 1572872 | tf_op jit(solution)/shard_map/ppermute | solution.py:249
  2.5 1.5 collective-permute-start.1
  4.0 0.8 copy-start.5
  5.5 1.0 copy-start.6
  6.5 1.5 copy-start.1
  6.5 3.0 %copy-start.3 = (f32[2,4,128,512]{3,2,1,0:T(8,128)S(1)}, f32[2,4,128,512]{3,2,1,0:T(8,128)}, u32[]{:S(2)}) copy-start(f32[2,4,128,512]{3,2,1,0:T(8,128)} %vec_ref.1) | copy-start | bytes 6291460
  8.1 17.9 %collective-permute-start.2 = (f32[1024,128]{1,0:T(8,128)S(1)}, f32[1024,128]{1,0:T(8,128)S(1)}, u32[]{:S(2)}, u32[]{:S(2)}) collective-permute-start(f32[1024,128]{1,0:T(8,128)S(1)} %bitcast.24), channel_id=1, source_target_pairs={{0,9},{1,8},{16,25},{17,24},{32,41},{33,40},{48,57},{49,56},{64,73... | collective-permute-start | bytes 1572872 | tf_op jit(solution)/shard_map/ppermute | solution.py:264
  9.5 50.7 %collective-permute-start.6 = (f32[2,4,128,512]{3,2,1,0:T(8,128)S(1)}, f32[2,4,128,512]{3,2,1,0:T(8,128)}, u32[]{:S(2)}, u32[]{:S(2)}) collective-permute-start(f32[2,4,128,512]{3,2,1,0:T(8,128)S(1)} %copy-done.3), channel_id=1, source_target_pairs={{0,16},{1,17},{2,18},{3,19},{4,20},{5,21},{6,22},{7,23},{8,24},{9,... | collective-permute-start | bytes 6291464 | tf_op jit(solution)/shard_map/ppermute | solution.py:249
  13.3 47.0 %collective-permute-start.7 = (f32[2,4,128,512]{3,2,1,0:T(8,128)S(1)}, f32[2,4,128,512]{3,2,1,0:T(8,128)}, u32[]{:S(2)}, u32[]{:S(2)}) collective-permute-start(f32[2,4,128,512]{3,2,1,0:T(8,128)S(1)} %copy-done.3), channel_id=1, source_target_pairs={{16,0},{17,1},{18,2},{19,3},{20,4},{21,5},{22,6},{23,7},{24,8},{25... | collective-permute-start | bytes 6291464 | tf_op jit(solution)/shard_map/ppermute | solution.py:249
  26.0 7.4 %collective-permute-start.3 = (f32[1024,128]{1,0:T(8,128)S(1)}, f32[1024,128]{1,0:T(8,128)S(1)}, u32[]{:S(2)}, u32[]{:S(2)}) collective-permute-start(f32[1024,128]{1,0:T(8,128)S(1)} %bitcast_add_fusion), channel_id=1, source_target_pairs={{0,4},{8,12},{1,13},{9,5},{16,20},{24,28},{17,29},{25,21},{32,36},... | collective-permute-start | bytes 1572872 | tf_op jit(solution)/shard_map/ppermute | solution.py:264
  33.5 21.5 %collective-permute-start.4 = (f32[1024,128]{1,0:T(8,128)S(1)}, f32[1024,128]{1,0:T(8,128)S(1)}, u32[]{:S(2)}, u32[]{:S(2)}) collective-permute-start(f32[1024,128]{1,0:T(8,128)S(1)} %add.91), channel_id=1, source_target_pairs={{1,3},{13,15},{5,7},{9,11},{4,2},{0,14},{8,6},{12,10},{17,19},{29,... | collective-permute-start | bytes 1572872 | tf_op jit(solution)/shard_map/ppermute | solution.py:264
  55.1 14.1 %copy-start.8 = (f32[1024,128]{1,0:T(8,128)}, f32[1024,128]{1,0:T(8,128)S(1)}, u32[]{:S(2)}) copy-start(f32[1024,128]{1,0:T(8,128)S(1)} %add.92) | copy-start | bytes 1572868
  55.1 16.2 %collective-permute-start.5 = (f32[1024,128]{1,0:T(8,128)S(1)}, f32[1024,128]{1,0:T(8,128)}, u32[]{:S(2)}, u32[]{:S(2)}) collective-permute-start(f32[1024,128]{1,0:T(8,128)S(1)} %add.92), channel_id=1, source_target_pairs={{4,3},{2,1},{0,15},{14,13},{12,11},{10,9},{8,7},{6,5},{3,4},{1,2},... | collective-permute-start | bytes 1572872 | tf_op jit(solution)/shard_map/ppermute | solution.py:266
  60.3 1.7 %copy-start.2 = (f32[4,10,128,128]{3,2,1,0:T(8,128)S(1)}, f32[4,10,128,128]{3,2,1,0:T(8,128)}, u32[]{:S(2)}) copy-start(f32[4,10,128,128]{3,2,1,0:T(8,128)} %copy-done.1) | copy-start | bytes 7864324
  62.0 1.6 copy-start.4
  71.0 1.0 copy-start.9
  71.3 3.8 %copy-start.7 = (f32[512,1024]{1,0:T(8,128)S(1)}, f32[512,1024]{1,0:T(8,128)}, u32[]{:S(2)}) copy-start(f32[512,1024]{1,0:T(8,128)} %copy.6) | copy-start | bytes 6291460

commit v4 on v3

--- a/solution.py
+++ b/solution.py
@@ -73,35 +73,48 @@
     )(vectors, low, high, coefs)
 
 
-def eliminate(mat_ref, inv_ref):
-    size = mat_ref.shape[0]
+def eliminate(block):
+    size = block.shape[0]
     step = 8
     wide = (step, 2 * size)
-    lanes = lax.broadcasted_iota(jnp.int32, (step, size), 1)
     subs = lax.broadcasted_iota(jnp.int32, wide, 0)
-    inv_ref[...] = identity(size)
-    for first in range(0, size, step):
-        last = first + step
-        both = jnp.concatenate([mat_ref[first:last], inv_ref[first:last]], 1)
-        columns = [jnp.broadcast_to(both[:, first + k:first + k + 1], (step, size)) for k in range(step)]
-        entry = [[jnp.broadcast_to(columns[k][i:i + 1], (step, size)) for k in range(i + 1)] for i in range(step)]
-        rows = [jnp.broadcast_to(both[i:i + 1], wide) for i in range(step)]
+    both = jnp.concatenate([block, identity(size)], 1)
+    parts = [both[first:first + step] for first in range(0, size, step)]
+    spread = lambda value: jnp.broadcast_to(value, (step, size))
+    twice = lambda value: jnp.concatenate([value, value], 1)
+    inverse = []
+    for index, part in enumerate(parts):
+        first = index * step
+        more = index + 1 < len(parts)
+        columns = [spread(part[:, first + k:first + k + 1]) for k in range(step)]
+        entry = [[spread(columns[k][i:i + 1]) for k in range(i + 1)] for i in range(step)]
+        rows = [jnp.broadcast_to(part[i:i + 1], wide) for i in range(step)]
+        if more:
+            after = parts[index + 1]
+            beside = [spread(after[:, first + k:first + k + 1]) for k in range(step)]
         result = jnp.zeros(wide, jnp.float32)
         for k in range(step):
             root = lax.rsqrt(entry[k][k])
-            done = rows[k] * jnp.concatenate([root, root], 1)
+            done = rows[k] * twice(root)
             result = jnp.where(subs == k, done, result)
             lower = {i: entry[i][k] * root for i in range(k + 1, step)}
             for i in range(k + 1, step):
                 for j in range(k + 1, i + 1):
                     entry[i][j] = entry[i][j] - lower[i] * lower[j]
-                rows[i] = rows[i] - jnp.concatenate([lower[i], lower[i]], 1) * done
-        inv_ref[first:last] = result[:, size:]
-        if last < size:
-            below = jnp.where(lanes >= last, result[:, :size], 0.0)
-            change = dot(below, result, (0, 0))
-            mat_ref[last:] = mat_ref[last:] - change[last:, :size]
-            inv_ref[last:] = inv_ref[last:] - change[last:, size:]
+                rows[i] = rows[i] - twice(lower[i]) * done
+            if more:
+                factor = beside[k] * root
+                for j in range(k + 1, step):
+                    beside[j] = beside[j] - factor * lower[j]
+                after = after - twice(factor) * done
+        inverse.append(result[:, size:])
+        if more:
+            parts[index + 1] = after
+        if index + 2 < len(parts):
+            change = dot(result[:, :size], result, (0, 0))
+            for later in range(index + 2, len(parts)):
+                parts[later] = parts[later] - change[later * step:(later + 1) * step]
+    return jnp.concatenate(inverse, 0)
 
 
 def identity(size):
@@ -122,25 +135,23 @@
     return sums_ref[index * each:(index + 1) * each, :SMALL].reshape(PANEL, PANEL)
 
 
-def first_kernel(total, sums_ref, rest_ref, inv_ref, cross_ref, mat_ref):
+def first_kernel(total, sums_ref, rest_ref, inv_ref, cross_ref):
     block = products_block(sums_ref, 0)
     along0, down0 = block_scales(block, total)
-    mat_ref[...] = block * down0 * along0 / total
-    eliminate(mat_ref, inv_ref)
+    inverse = eliminate(block * down0 * along0 / total)
+    inv_ref[...] = inverse
     block = products_block(sums_ref, 2)
     along1, down1 = block_scales(block, total)
-    cross = dot(inv_ref[...], products_block(sums_ref, 1) * down0 * along1 / total, (1, 0))
+    cross = dot(inverse, products_block(sums_ref, 1) * down0 * along1 / total, (1, 0))
     cross_ref[...] = cross
     rest_ref[...] = block * down1 * along1 / total - dot(cross, cross, (0, 0))
 
 
-def second_kernel(total, sums_ref, rest_ref, inv0_ref, cross_ref, out_ref, mat_ref, inv_ref):
-    mat_ref[...] = rest_ref[...]
-    eliminate(mat_ref, inv_ref)
+def second_kernel(total, sums_ref, rest_ref, inv0_ref, cross_ref, out_ref):
+    inv1 = eliminate(rest_ref[...])
     along0, _ = block_scales(products_block(sums_ref, 0), total)
     along1, _ = block_scales(products_block(sums_ref, 2), total)
     inv0 = inv0_ref[...]
-    inv1 = inv_ref[...]
     mixed = -dot(dot(inv1, cross_ref[...], (1, 1)), inv0, (1, 0))
     out_ref[0:PANEL, 0:PANEL] = inv0 * along0
     out_ref[0:PANEL, PANEL:] = jnp.zeros((PANEL, PANEL), jnp.float32)
@@ -148,28 +159,60 @@
     out_ref[PANEL:, PANEL:] = inv1 * along1
 
 
-def call(kernel, name, outs, scratch, *args):
-    square = pltpu.VMEM((PANEL, PANEL), jnp.float32)
+def call(kernel, name, outs, *args):
     shapes = [jax.ShapeDtypeStruct((k * PANEL, k * PANEL), jnp.float32) for k in outs]
     return pl.pallas_call(
         kernel,
         out_shape=shapes,
-        scratch_shapes=[square] * scratch,
         compiler_params=pltpu.CompilerParams(vmem_limit_bytes=16 * MIB),
-        cost_estimate=pl.CostEstimate(flops=2 * 10**9, bytes_accessed=10**6, transcendentals=0),
         name=name,
     )(*args)
 
 
 def first_half(sums, total):
-    return call(functools.partial(first_kernel, total), "factor_a", [1, 1, 1], 1, sums)
+    return call(functools.partial(first_kernel, total), "factor_a", [1, 1, 1], sums)
 
 
 def second_half(sums, rest, inv0, cross, total):
-    return call(functools.partial(second_kernel, total), "factor_b", [2], 2, sums, rest, inv0, cross)[0]
-
-
-def finish_kernel(total, place_ref, inv_ref, sums_ref, panel0_ref, panel1_ref, matrix_ref,
+    return call(functools.partial(second_kernel, total), "factor_b", [2], sums, rest, inv0, cross)[0]
+
+
+def sums_kernel(place_ref, held_ref, other_ref, matrix_ref, out_ref):
+    shares = out_ref.shape[0]
+    each = shares // 4
+    ordered = place_ref[1] == 1
+    held = held_ref[...]
+    other = other_ref[...]
+    panels = jnp.concatenate([jnp.where(ordered, held, other), jnp.where(ordered, other, held)], 1)
+    matrix = matrix_ref[...].reshape(panels.shape[0], -1)
+    products = dot(panels, jnp.concatenate([panels, matrix], 1), (0, 0))
+    blocks = [products[:PANEL, :PANEL], products[:PANEL, PANEL:2 * PANEL], products[PANEL:, PANEL:2 * PANEL]]
+    for i, block in enumerate(blocks):
+        out_ref[i * each:(i + 1) * each, :SMALL] = block.reshape(each, SMALL, BLOCK)
+    squares = jnp.sum(matrix * matrix, 0, keepdims=True)
+    count = matrix.shape[1] // BLOCK
+    out_ref[3 * each:, :SMALL] = jnp.zeros((shares - 3 * each, SMALL, BLOCK), jnp.float32)
+    for i in range(count):
+        out_ref[3 * each, i:i + 1] = squares[:, i * BLOCK:(i + 1) * BLOCK]
+        block = products[:, 2 * PANEL + i * BLOCK:2 * PANEL + (i + 1) * BLOCK]
+        out_ref[i * shares // count:(i + 1) * shares // count, SMALL:] = block.reshape(shares // count, -1, BLOCK)
+
+
+def shared_sums(place, held, other, matrix, shares):
+    columns = matrix.shape[3]
+    depth = SMALL + 2 * PANEL * (columns // BLOCK) // shares
+    vmem = pl.BlockSpec(memory_space=pltpu.VMEM)
+    return pl.pallas_call(
+        sums_kernel,
+        in_specs=[pl.BlockSpec(memory_space=pltpu.SMEM), vmem, vmem, vmem],
+        out_specs=vmem,
+        out_shape=jax.ShapeDtypeStruct((shares, depth, BLOCK), jnp.float32),
+        compiler_params=pltpu.CompilerParams(vmem_limit_bytes=48 * MIB),
+        name="shared_sums",
+    )(place, held, other, matrix)
+
+
+def finish_kernel(total, place_ref, inv_ref, sums_ref, held_ref, other_ref, matrix_ref,
                   out_ref, growth_ref, weights_ref, factors_ref):
     count = out_ref.shape[3] // BLOCK
     place = place_ref[0]
@@ -186,7 +229,10 @@
         lanes = lax.broadcasted_iota(jnp.int32, part.shape, 1)
         chosen = jnp.where(subs == lanes + place * PANEL, -1.0, 0.0)
         part = jnp.where(jnp.logical_and(lanes < PANEL, holder), chosen, part)
-        weights_ref[...] = dot(inverse, part, (0, 0))
+        weights = dot(inverse, part, (0, 0))
+        ordered = place_ref[1] == 1
+        weights_ref[:PANEL] = jnp.where(ordered, weights[:PANEL], weights[PANEL:])
+        weights_ref[PANEL:] = jnp.where(ordered, weights[PANEL:], weights[:PANEL])
         place4 = 3 * sums_ref.shape[0] // 4
         squares = jnp.concatenate([sums_ref[place4, i:i + 1] for i in range(count)], 1)
         scale = jnp.sqrt(squares / total + tiny)
@@ -195,14 +241,14 @@
         factors_ref[0:1] = jnp.where(in_panel, 0.0, 1.0)
         factors_ref[1:2] = jnp.where(in_panel, 1.0, 1.0 / scale)
 
-    panels = jnp.concatenate([panel0_ref[...], panel1_ref[...]], 1)
+    panels = jnp.concatenate([held_ref[...], other_ref[...]], 1)
     taken = dot(panels, weights_ref[...], (1, 0))
     rows = taken.shape[0]
     block = matrix_ref[...].reshape(rows, -1)
     out_ref[...] = ((block * factors_ref[0:1] - taken) * factors_ref[1:2]).reshape(out_ref.shape)
 
 
-def finish(col_index, inverse, sums, panel0, panel1, matrix, total):
+def finish(place, inverse, sums, held, other, matrix, total):
     _, rows, sites, columns = matrix.shape
     steps = 2 if rows % 2 == 0 else 1
     block = pl.BlockSpec((1, rows // steps, sites, columns), lambda i: (i // steps, i % steps, 0, 0))
@@ -230,7 +276,7 @@
         ],
         compiler_params=pltpu.CompilerParams(vmem_limit_bytes=40 * MIB),
         name="finish",
-    )(col_index.reshape(1), inverse, sums, panel0, panel1, matrix)
+    )(place, inverse, sums, held, other, matrix)
 
 
 def on_device(vectors, potential):
@@ -265,28 +311,14 @@
     pairs = [(4, 3), (2, 1), (0, 15), (14, 13), (12, 11), (10, 9), (8, 7), (6, 5)]
     other = lax.ppermute(held, "col", pairs + [(b, a) for a, b in pairs])
     has_first = functools.reduce(jnp.logical_or, [col_index == c for c in (0, 2, 4, 5, 7, 9, 11, 14)])
-    panel0 = jnp.where(has_first, held, other)
-    panel1 = jnp.where(has_first, other, held)
+    place = jnp.stack([col_index, has_first.astype(jnp.int32)])
 
     blocks = stencil(vectors, *neighbours(vectors, range(col_count)), coefs)
-    matrix = blocks.reshape(-1, columns)
-    panels = jnp.concatenate([panel0, panel1], 1)
-    coeffs = dot(panels, matrix, (0, 0))
-    products = dot(panels, panels, (0, 0))
-    squares = jnp.sum(matrix * matrix, 0).reshape(-1, BLOCK)
-    small = jnp.concatenate([
-        products[:PANEL, :PANEL],
-        products[:PANEL, PANEL:],
-        products[PANEL:, PANEL:],
-        jnp.pad(squares, ((0, PANEL - squares.shape[0]), (0, 0))),
-    ], 0)
-    large = jnp.moveaxis(coeffs.reshape(2 * PANEL, -1, BLOCK), 1, 0)
-
-    sums = jnp.concatenate([small.reshape(row_count, -1, BLOCK), large.reshape(row_count, -1, BLOCK)], 1)
-    share = jnp.sum(lax.all_to_all(sums, "row", 0, 0), 0)
+    sums = lax.all_to_all(shared_sums(place, held, other, blocks, row_count), "row", 0, 0)
+    share = jnp.sum(sums, 0)
     sums = lax.all_to_all(jnp.broadcast_to(share, (row_count,) + share.shape), "row", 0, 0)
     inverse = second_half(sums, *first_half(sums, total), total)
-    result, growth = finish(col_index, inverse, sums, panel0, panel1, blocks, total)
+    result, growth = finish(place, inverse, sums, held, other, blocks, total)
     return (result, growth.reshape(-1))
 
 

time: 162 us -> 143 us (0.88)
  the two profiles are of different devices: /device:TPU:289 before, /device:TPU:1 now
where the time goes in v4:
time: 143 us; the launch traced here: 142 us
  blocking collectives  53 us (37%)
  starting transfers between devices  35.1 us (25%)
  Pallas kernels  28.4 us (20%)
  waiting for transfers between devices  17.3 us (12%)
  local copies, waits for them, and re-layouts  6.75 us (5%)
    all_to_all x1, blocking collectives, on_device(): lax.all_to_all(shared_sums(place, held, other, blocks, row_count), 'row',...  35 us
    all_to_all x1, blocking collectives, on_device(): lax.all_to_all(jnp.broadcast_to(share, (row_count,) + share.shape), 'row'...  18 us
    ppermute x3, waiting for transfers between devices, on_device(): held = held + lax.ppermute(held, 'col', pairs)  12.5 us
    pallas_call x2, Pallas kernels, call(): pl.pallas_call(kernel, out_shape=shapes, compiler_params=pltpu.CompilerPa...  11.7 us
    ppermute x2, starting transfers between devices, neighbours(): lax.ppermute(block, ('row', 'col'), back)  10.8 us
    ppermute x1, starting transfers between devices, on_device(): other = lax.ppermute(held, 'col', pairs + [(b, a) for a, b in pairs])  9.5 us
    ppermute x2, starting transfers between devices, neighbours(): lax.ppermute(block, ('row', 'col'), ahead)  8.64 us
    pallas_call x2, Pallas kernels, stencil(): pl.pallas_call(functools.partial(stencil_kernel, coefs.shape[0]), grid=(c...  6.7 us
  transfers between devices with their start and end apart: 8, of which 4 were waited for; matrix products, arithmetic and copies ran while one was open for 1% of the time, Pallas kernels for 4%

profile of v4, /device:TPU:1, one launch (start us, length us, event | category | flops | bytes accessed | tf_op | source)
XLA Modules:
  0.0 141.9 jit_solution(9916331294558967118)
XLA Ops:
  0.6 0.0 copy-start
  0.6 1.1 slice.3.vec_ref
  1.8 4.6 %collective-permute-start = (f32[2,4,128,128]{3,2,1,0:T(8,128)S(1)}, f32[2,4,128,128]{3,2,1,0:T(8,128)S(1)}, u32[]{:S(2)}, u32[]{:S(2)}) collective-permute-start(f32[2,4,128,128]{3,2,1,0:T(8,128)S(1)} %slice.3.vec_ref), channel_id=1, source_target_pairs={{0,16},{1,17},{16,32},{17,33},{32,48},{33,49},{48,64},{49,65},{64,... | collective-permute-start | bytes 1572872 | tf_op jit(solution)/shard_map/ppermute | solution.py:295
  6.4 6.1 %collective-permute-start.1 = (f32[2,4,128,128]{3,2,1,0:T(8,128)S(1)}, f32[2,4,128,128]{3,2,1,0:T(8,128)S(1)}, u32[]{:S(2)}, u32[]{:S(2)}) collective-permute-start(f32[2,4,128,128]{3,2,1,0:T(8,128)S(1)} %slice.3.vec_ref), channel_id=1, source_target_pairs={{16,0},{17,1},{32,16},{33,17},{48,32},{49,33},{64,48},{65,49},{80,... | collective-permute-start | bytes 1572872 | tf_op jit(solution)/shard_map/ppermute | solution.py:295
  12.5 0.0 copy-done
  12.5 0.6 gather_fusion
  13.2 0.1 subtract_bitcast_fusion
  13.3 0.0 collective-permute-done.low_ref
  13.3 0.0 copy-start.3
  13.3 0.8 copy-done.3
  14.1 3.1 %collective-permute-done.1.high_ref = f32[2,4,128,128]{3,2,1,0:T(8,128)S(1)} collective-permute-done((f32[2,4,128,128]{3,2,1,0:T(8,128)S(1)}, f32[2,4,128,128]{3,2,1,0:T(8,128)S(1)}, u32[]{:S(2)}, u32[]{:S(2)}) %collective-permute-start.1) | collective-permute-done | bytes 524320 | tf_op jit(solution)/shard_map/ppermute | solution.py:295
  17.2 0.0 copy-start.5
  17.2 0.8 copy-done.5
  18.0 0.0 copy-start.4
  18.0 0.7 broadcast_in_dim.25.coef_ref
  18.7 0.3 copy-done.4
  19.0 0.0 copy-start.6
  19.0 1.0 copy-done.6
  20.0 0.9 slices.2
  21.0 3.4 %collective-permute-start.2 = (f32[1024,128]{1,0:T(8,128)S(1)}, f32[1024,128]{1,0:T(8,128)S(1)}, u32[]{:S(2)}, u32[]{:S(2)}) collective-permute-start(f32[1024,128]{1,0:T(8,128)S(1)} %bitcast.9), channel_id=1, source_target_pairs={{0,9},{1,8},{16,25},{17,24},{32,41},{33,40},{48,57},{49,56},{64,73... | collective-permute-start | bytes 1572872 | tf_op jit(solution)/shard_map/ppermute | solution.py:310
  24.4 4.0 %collective-permute-start.6 = (f32[2,4,128,512]{3,2,1,0:T(8,128)}, f32[2,4,128,512]{3,2,1,0:T(8,128)}, u32[]{:S(2)}, u32[]{:S(2)}) collective-permute-start(f32[2,4,128,512]{3,2,1,0:T(8,128)} %vec_ref.1), channel_id=1, source_target_pairs={{0,16},{1,17},{2,18},{3,19},{4,20},{5,21},{6,22},{7,23},{8,24},{9,... | collective-permute-start | bytes 6291464 | tf_op jit(solution)/shard_map/ppermute | solution.py:295
  28.5 4.7 %collective-permute-start.7 = (f32[2,4,128,512]{3,2,1,0:T(8,128)}, f32[2,4,128,512]{3,2,1,0:T(8,128)}, u32[]{:S(2)}, u32[]{:S(2)}) collective-permute-start(f32[2,4,128,512]{3,2,1,0:T(8,128)} %vec_ref.1), channel_id=1, source_target_pairs={{16,0},{17,1},{18,2},{19,3},{20,4},{21,5},{22,6},{23,7},{24,8},{25... | collective-permute-start | bytes 6291464 | tf_op jit(solution)/shard_map/ppermute | solution.py:295
  33.2 0.0 collective-permute-done.2
  33.2 0.1 bitcast_add_fusion
  33.3 1.3 collective-permute-start.3
  34.6 6.1 %collective-permute-done.3 = f32[1024,128]{1,0:T(8,128)S(1)} collective-permute-done((f32[1024,128]{1,0:T(8,128)S(1)}, f32[1024,128]{1,0:T(8,128)S(1)}, u32[]{:S(2)}, u32[]{:S(2)}) %collective-permute-start.3) | collective-permute-done | bytes 524320 | tf_op jit(solution)/shard_map/ppermute | solution.py:310
  40.8 0.1 add.89
  40.8 1.3 collective-permute-start.4
  42.1 6.4 %collective-permute-done.4 = f32[1024,128]{1,0:T(8,128)S(1)} collective-permute-done((f32[1024,128]{1,0:T(8,128)S(1)}, f32[1024,128]{1,0:T(8,128)S(1)}, u32[]{:S(2)}, u32[]{:S(2)}) %collective-permute-start.4) | collective-permute-done | bytes 524320 | tf_op jit(solution)/shard_map/ppermute | solution.py:310
  48.5 0.1 add.90.held_ref
  48.6 9.5 %collective-permute-start.5 = (f32[1024,128]{1,0:T(8,128)S(1)}, f32[1024,128]{1,0:T(8,128)}, u32[]{:S(2)}, u32[]{:S(2)}) collective-permute-start(f32[1024,128]{1,0:T(8,128)S(1)} %add.90.held_ref), channel_id=1, source_target_pairs={{4,3},{2,1},{0,15},{14,13},{12,11},{10,9},{8,7},{6,5},{3,4},{1,2},... | collective-permute-start | bytes 1572872 | tf_op jit(solution)/shard_map/ppermute | solution.py:312
  58.1 0.1 pad_add_fusion.place_ref
  58.2 0.0 collective-permute-done.6.low_ref
  58.2 0.0 collective-permute-done.7.high_ref
  58.2 5.8 %slices.3.matrix_ref = f32[2,4,128,512]{3,2,1,0:T(8,128)S(1)} custom-call(f32[2,4,128,512]{3,2,1,0:T(8,128)} %vec_ref.1, f32[2,4,128,512]{3,2,1,0:T(8,128)} %collective-permute-done.6.low_ref, f32[2,4,128,512]{3,2,1,0:T(8,128)} %collective-permute-done.7.high_ref, f32[4,10,128,128]{3,2,1,0:T(8,128)S(1)} %broadcast_in_dim.25.coef_ref), custom_call_target="tpu_custom_call" | custom-call | tf_op jit(solution)/shard_map/slices/pallas_call | solution.py:64
  64.0 1.7 %collective-permute-done.5.other_ref = f32[1024,128]{1,0:T(8,128)} collective-permute-done((f32[1024,128]{1,0:T(8,128)S(1)}, f32[1024,128]{1,0:T(8,128)}, u32[]{:S(2)}, u32[]{:S(2)}) %collective-permute-start.5) | collective-permute-done | bytes 524320 | tf_op jit(solution)/shard_map/ppermute | solution.py:312
  65.7 4.0 %shared_sums.1 = f32[32,48,128]{2,1,0:T(8,128)S(1)} custom-call(s32[2]{0:T(128)S(1)} %pad_add_fusion.place_ref, f32[1024,128]{1,0:T(8,128)S(1)} %add.90.held_ref, f32[1024,128]{1,0:T(8,128)} %collective-permute-done.5.other_ref, f32[2,4,128,512]{3,2,1,0:T(8,128)S(1)} %slices.3.matrix_ref), custom_call_target="tpu_custom_call" | custom-call | tf_op jit(solution)/shard_map/shared_sums/pallas_call | solution.py:205
  69.7 0.0 copy-start.1
  69.7 1.3 copy-done.1
  71.0 35.0 %all_to_all.10 = f32[32,48,128]{2,1,0:T(8,128)S(1)} all-to-all(f32[32,48,128]{2,1,0:T(8,128)S(1)} %shared_sums.1), channel_id=1, replica_groups=mesh['row'=32,'col'=16] {'row'}, dimensions={0} | all-to-all | bytes 1572864 | tf_op jit(solution)/shard_map/all_to_all | solution.py:317
  106.0 0.1 reduce_sum.9
  106.1 0.0 copy-start.2
  106.1 0.1 broadcast_in_dim.27
  106.2 18.0 %all_to_all.11.sums_ref = f32[32,48,128]{2,1,0:T(8,128)S(1)} all-to-all(f32[32,48,128]{2,1,0:T(8,128)S(1)} %broadcast_in_dim.27), channel_id=1, replica_groups=mesh['row'=32,'col'=16] {'row'}, dimensions={0} | all-to-all | bytes 1572864 | tf_op jit(solution)/shard_map/all_to_all | solution.py:319
  124.2 5.9 %factor_a.1 = (f32[128,128]{1,0:T(8,128)S(1)}, f32[128,128]{1,0:T(8,128)S(1)}, f32[128,128]{1,0:T(8,128)S(1)}) custom-call(f32[32,48,128]{2,1,0:T(8,128)S(1)} %all_to_all.11.sums_ref), custom_call_target="tpu_custom_call" | custom-call | tf_op jit(solution)/shard_map/factor_a/pallas_call | solution.py:164
  130.1 5.8 %factor_b.1.inv_ref = f32[256,256]{1,0:T(8,128)S(1)} custom-call(f32[32,48,128]{2,1,0:T(8,128)S(1)} %all_to_all.11.sums_ref, f32[128,128]{1,0:T(8,128)S(1)} %get-tuple-element.7.rest_ref, f32[128,128]{1,0:T(8,128)S(1)} %get-tuple-element.8.inv0_ref, f32[128,128]{1,0:T(8,128)S(1)} %get-tuple-element.9.cross_ref), custom_call_target="tpu_custom_call" | custom-call | tf_op jit(solution)/shard_map/factor_b/pallas_call | solution.py:164
  135.8 0.0 copy-done.2
  135.9 6.0 %finish.1 = (f32[2,4,128,512]{3,2,1,0:T(8,128)}, f32[1,512]{1,0:T(1,128)}) custom-call(s32[2]{0:T(128)S(1)} %pad_add_fusion.place_ref, f32[256,256]{1,0:T(8,128)S(1)} %factor_b.1.inv_ref, f32[32,48,128]{2,1,0:T(8,128)S(1)} %all_to_all.11.sums_ref, f32[1024,128]{1,0:T(8,128)S(1)} %add.90.held_ref, f32[1024,128]{1,0:T(8,128)} %collective-permute-done.5.other_ref, ...), custom_call_target="tpu_custom_call" | custom-call | tf_op jit(solution)/shard_map/finish/pallas_call | solution.py:257
  (4 shorter events, 0.1 us)
Async XLA Ops:
  0.6 11.9 %copy-start = (s32[4,128,128]{2,1,0:T(8,128)S(1)}, s32[4,128,128]{2,1,0:T(8,128)}, u32[]{:S(2)}) copy-start(s32[4,128,128]{2,1,0:T(8,128)} %param.3) | copy-start | bytes 786436
  1.8 11.5 %collective-permute-start = (f32[2,4,128,128]{3,2,1,0:T(8,128)S(1)}, f32[2,4,128,128]{3,2,1,0:T(8,128)S(1)}, u32[]{:S(2)}, u32[]{:S(2)}) collective-permute-start(f32[2,4,128,128]{3,2,1,0:T(8,128)S(1)} %slice.3.vec_ref), channel_id=1, source_target_pairs={{0,16},{1,17},{16,32},{17,33},{32,48},{33,49},{48,64},{49,65},{64,... | collective-permute-start | bytes 1572872 | tf_op jit(solution)/shard_map/ppermute | solution.py:295
  6.4 10.8 %collective-permute-start.1 = (f32[2,4,128,128]{3,2,1,0:T(8,128)S(1)}, f32[2,4,128,128]{3,2,1,0:T(8,128)S(1)}, u32[]{:S(2)}, u32[]{:S(2)}) collective-permute-start(f32[2,4,128,128]{3,2,1,0:T(8,128)S(1)} %slice.3.vec_ref), channel_id=1, source_target_pairs={{16,0},{17,1},{32,16},{33,17},{48,32},{49,33},{64,48},{65,49},{80,... | collective-permute-start | bytes 1572872 | tf_op jit(solution)/shard_map/ppermute | solution.py:295
  13.3 0.8 copy-start.3
  17.2 0.8 copy-start.5
  18.0 1.0 copy-start.4
  19.0 1.0 copy-start.6
  21.0 12.2 %collective-permute-start.2 = (f32[1024,128]{1,0:T(8,128)S(1)}, f32[1024,128]{1,0:T(8,128)S(1)}, u32[]{:S(2)}, u32[]{:S(2)}) collective-permute-start(f32[1024,128]{1,0:T(8,128)S(1)} %bitcast.9), channel_id=1, source_target_pairs={{0,9},{1,8},{16,25},{17,24},{32,41},{33,40},{48,57},{49,56},{64,73... | collective-permute-start | bytes 1572872 | tf_op jit(solution)/shard_map/ppermute | solution.py:310
  24.4 33.7 %collective-permute-start.6 = (f32[2,4,128,512]{3,2,1,0:T(8,128)}, f32[2,4,128,512]{3,2,1,0:T(8,128)}, u32[]{:S(2)}, u32[]{:S(2)}) collective-permute-start(f32[2,4,128,512]{3,2,1,0:T(8,128)} %vec_ref.1), channel_id=1, source_target_pairs={{0,16},{1,17},{2,18},{3,19},{4,20},{5,21},{6,22},{7,23},{8,24},{9,... | collective-permute-start | bytes 6291464 | tf_op jit(solution)/shard_map/ppermute | solution.py:295
  28.5 29.7 %collective-permute-start.7 = (f32[2,4,128,512]{3,2,1,0:T(8,128)}, f32[2,4,128,512]{3,2,1,0:T(8,128)}, u32[]{:S(2)}, u32[]{:S(2)}) collective-permute-start(f32[2,4,128,512]{3,2,1,0:T(8,128)} %vec_ref.1), channel_id=1, source_target_pairs={{16,0},{17,1},{18,2},{19,3},{20,4},{21,5},{22,6},{23,7},{24,8},{25... | collective-permute-start | bytes 6291464 | tf_op jit(solution)/shard_map/ppermute | solution.py:295
  33.3 7.5 %collective-permute-start.3 = (f32[1024,128]{1,0:T(8,128)S(1)}, f32[1024,128]{1,0:T(8,128)S(1)}, u32[]{:S(2)}, u32[]{:S(2)}) collective-permute-start(f32[1024,128]{1,0:T(8,128)S(1)} %bitcast_add_fusion), channel_id=1, source_target_pairs={{0,4},{8,12},{1,13},{9,5},{16,20},{24,28},{17,29},{25,21},{32,36},... | collective-permute-start | bytes 1572872 | tf_op jit(solution)/shard_map/ppermute | solution.py:310
  40.8 7.7 %collective-permute-start.4 = (f32[1024,128]{1,0:T(8,128)S(1)}, f32[1024,128]{1,0:T(8,128)S(1)}, u32[]{:S(2)}, u32[]{:S(2)}) collective-permute-start(f32[1024,128]{1,0:T(8,128)S(1)} %add.89), channel_id=1, source_target_pairs={{1,3},{13,15},{5,7},{9,11},{4,2},{0,14},{8,6},{12,10},{17,19},{29,... | collective-permute-start | bytes 1572872 | tf_op jit(solution)/shard_map/ppermute | solution.py:310
  48.6 17.1 %collective-permute-start.5 = (f32[1024,128]{1,0:T(8,128)S(1)}, f32[1024,128]{1,0:T(8,128)}, u32[]{:S(2)}, u32[]{:S(2)}) collective-permute-start(f32[1024,128]{1,0:T(8,128)S(1)} %add.90.held_ref), channel_id=1, source_target_pairs={{4,3},{2,1},{0,15},{14,13},{12,11},{10,9},{8,7},{6,5},{3,4},{1,2},... | collective-permute-start | bytes 1572872 | tf_op jit(solution)/shard_map/ppermute | solution.py:312
  69.7 1.3 copy-start.1
  106.1 29.7 %copy-start.2 = (f32[2,4,128,512]{3,2,1,0:T(8,128)S(1)}, f32[2,4,128,512]{3,2,1,0:T(8,128)}, u32[]{:S(2)}) copy-start(f32[2,4,128,512]{3,2,1,0:T(8,128)} %copy-done.1) | copy-start | bytes 6291460

commit v5 on v4

--- a/solution.py
+++ b/solution.py
@@ -68,7 +68,7 @@
         out_specs=block,
         out_shape=jax.ShapeDtypeStruct(vectors.shape, jnp.float32),
         scratch_shapes=[pltpu.VMEM((3 * rows, sites, BLOCK), jnp.float32)] * 2,
-        compiler_params=pltpu.CompilerParams(vmem_limit_bytes=40 * MIB),
+        compiler_params=pltpu.CompilerParams(vmem_limit_bytes=16 * MIB),
         name="slices",
     )(vectors, low, high, coefs)
 
@@ -135,46 +135,18 @@
     return sums_ref[index * each:(index + 1) * each, :SMALL].reshape(PANEL, PANEL)
 
 
-def first_kernel(total, sums_ref, rest_ref, inv_ref, cross_ref):
+def inverse_factor(total, sums_ref):
     block = products_block(sums_ref, 0)
     along0, down0 = block_scales(block, total)
-    inverse = eliminate(block * down0 * along0 / total)
-    inv_ref[...] = inverse
+    inv0 = eliminate(block * down0 * along0 / total)
     block = products_block(sums_ref, 2)
     along1, down1 = block_scales(block, total)
-    cross = dot(inverse, products_block(sums_ref, 1) * down0 * along1 / total, (1, 0))
-    cross_ref[...] = cross
-    rest_ref[...] = block * down1 * along1 / total - dot(cross, cross, (0, 0))
-
-
-def second_kernel(total, sums_ref, rest_ref, inv0_ref, cross_ref, out_ref):
-    inv1 = eliminate(rest_ref[...])
-    along0, _ = block_scales(products_block(sums_ref, 0), total)
-    along1, _ = block_scales(products_block(sums_ref, 2), total)
-    inv0 = inv0_ref[...]
-    mixed = -dot(dot(inv1, cross_ref[...], (1, 1)), inv0, (1, 0))
-    out_ref[0:PANEL, 0:PANEL] = inv0 * along0
-    out_ref[0:PANEL, PANEL:] = jnp.zeros((PANEL, PANEL), jnp.float32)
-    out_ref[PANEL:, 0:PANEL] = mixed * along0
-    out_ref[PANEL:, PANEL:] = inv1 * along1
-
-
-def call(kernel, name, outs, *args):
-    shapes = [jax.ShapeDtypeStruct((k * PANEL, k * PANEL), jnp.float32) for k in outs]
-    return pl.pallas_call(
-        kernel,
-        out_shape=shapes,
-        compiler_params=pltpu.CompilerParams(vmem_limit_bytes=16 * MIB),
-        name=name,
-    )(*args)
-
-
-def first_half(sums, total):
-    return call(functools.partial(first_kernel, total), "factor_a", [1, 1, 1], sums)
-
-
-def second_half(sums, rest, inv0, cross, total):
-    return call(functools.partial(second_kernel, total), "factor_b", [2], sums, rest, inv0, cross)[0]
+    cross = dot(inv0, products_block(sums_ref, 1) * down0 * along1 / total, (1, 0))
+    inv1 = eliminate(block * down1 * along1 / total - dot(cross, cross, (0, 0)))
+    mixed = -dot(dot(inv1, cross, (1, 1)), inv0, (1, 0))
+    above = jnp.concatenate([inv0 * along0, jnp.zeros((PANEL, PANEL), jnp.float32)], 1)
+    below = jnp.concatenate([mixed * along0, inv1 * along1], 1)
+    return jnp.concatenate([above, below], 0)
 
 
 def sums_kernel(place_ref, held_ref, other_ref, matrix_ref, out_ref):
@@ -207,12 +179,12 @@
         in_specs=[pl.BlockSpec(memory_space=pltpu.SMEM), vmem, vmem, vmem],
         out_specs=vmem,
         out_shape=jax.ShapeDtypeStruct((shares, depth, BLOCK), jnp.float32),
-        compiler_params=pltpu.CompilerParams(vmem_limit_bytes=48 * MIB),
+        compiler_params=pltpu.CompilerParams(vmem_limit_bytes=24 * MIB),
         name="shared_sums",
     )(place, held, other, matrix)
 
 
-def finish_kernel(total, place_ref, inv_ref, sums_ref, held_ref, other_ref, matrix_ref,
+def finish_kernel(total, place_ref, sums_ref, held_ref, other_ref, matrix_ref,
                   out_ref, growth_ref, weights_ref, factors_ref):
     count = out_ref.shape[3] // BLOCK
     place = place_ref[0]
@@ -222,7 +194,7 @@
     @pl.when(pl.program_id(0) == 0)
     def _():
         each = sums_ref.shape[0] // count
-        inverse = inv_ref[...]
+        inverse = inverse_factor(total, sums_ref)
         sums = [sums_ref[each * i:each * (i + 1), SMALL:].reshape(2 * PANEL, BLOCK) for i in range(count)]
         part = dot(inverse, jnp.concatenate(sums, 1), (1, 0)) / total
         subs = lax.broadcasted_iota(jnp.int32, part.shape, 0)
@@ -248,7 +220,7 @@
     out_ref[...] = ((block * factors_ref[0:1] - taken) * factors_ref[1:2]).reshape(out_ref.shape)
 
 
-def finish(place, inverse, sums, held, other, matrix, total):
+def finish(place, sums, held, other, matrix, total):
     _, rows, sites, columns = matrix.shape
     steps = 2 if rows % 2 == 0 else 1
     block = pl.BlockSpec((1, rows // steps, sites, columns), lambda i: (i // steps, i % steps, 0, 0))
@@ -259,7 +231,6 @@
         grid=(2 * steps,),
         in_specs=[
             pl.BlockSpec(memory_space=pltpu.SMEM),
-            fixed(inverse),
             fixed(sums),
             panel,
             panel,
@@ -274,9 +245,9 @@
             pltpu.VMEM((2 * PANEL, columns), jnp.float32),
             pltpu.VMEM((8, columns), jnp.float32),
         ],
-        compiler_params=pltpu.CompilerParams(vmem_limit_bytes=40 * MIB),
+        compiler_params=pltpu.CompilerParams(vmem_limit_bytes=20 * MIB),
         name="finish",
-    )(place, inverse, sums, held, other, matrix)
+    )(place, sums, held, other, matrix)
 
 
 def on_device(vectors, potential):
@@ -317,8 +288,7 @@
     sums = lax.all_to_all(shared_sums(place, held, other, blocks, row_count), "row", 0, 0)
     share = jnp.sum(sums, 0)
     sums = lax.all_to_all(jnp.broadcast_to(share, (row_count,) + share.shape), "row", 0, 0)
-    inverse = second_half(sums, *first_half(sums, total), total)
-    result, growth = finish(place, inverse, sums, held, other, blocks, total)
+    result, growth = finish(place, sums, held, other, blocks, total)
     return (result, growth.reshape(-1))
 
 

time: 143 us -> 144 us (level)
    pallas_call x1, Pallas kernels: 6 us -> 17.9 us  [finish(): pl.pallas_call(functools.partial(finish_kernel, total), grid=(2 * steps,)...]
    pallas_call x2 -> x0, Pallas kernels: 11.7 us -> none  [call(): pl.pallas_call(kernel, out_shape=shapes, compiler_params=pltpu.CompilerPa...]
where the time goes in v5:
time: 144 us; the launch traced here: 143 us
  blocking collectives  53 us (37%)
  starting transfers between devices  35.1 us (24%)
  Pallas kernels  28.6 us (20%)
  waiting for transfers between devices  17.3 us (12%)
  local copies, waits for them, and re-layouts  6.76 us (5%)
  other arithmetic  1.74 us (1%)
    all_to_all x1, blocking collectives, on_device(): lax.all_to_all(shared_sums(place, held, other, blocks, row_count), 'row',...  35.1 us
    pallas_call x1, Pallas kernels, finish(): pl.pallas_call(functools.partial(finish_kernel, total), grid=(2 * steps,)...  17.9 us
    all_to_all x1, blocking collectives, on_device(): lax.all_to_all(jnp.broadcast_to(share, (row_count,) + share.shape), 'row'...  17.9 us
    ppermute x3, waiting for transfers between devices, on_device(): held = held + lax.ppermute(held, 'col', pairs)  12.5 us
    ppermute x2, starting transfers between devices, neighbours(): lax.ppermute(block, ('row', 'col'), back)  10.8 us
    ppermute x1, starting transfers between devices, on_device(): other = lax.ppermute(held, 'col', pairs + [(b, a) for a, b in pairs])  9.5 us
    ppermute x2, starting transfers between devices, neighbours(): lax.ppermute(block, ('row', 'col'), ahead)  8.64 us
    pallas_call x2, Pallas kernels, stencil(): pl.pallas_call(functools.partial(stencil_kernel, coefs.shape[0]), grid=(c...  6.7 us
  transfers between devices with their start and end apart: 8, of which 4 were waited for; matrix products, arithmetic and copies ran while one was open for 1% of the time, Pallas kernels for 4%

profile of v5, /device:TPU:1, one launch (start us, length us, event | category | flops | bytes accessed | tf_op | source)
XLA Modules:
  0.0 143.3 jit_solution(17572205652458799879)
XLA Ops:
  0.6 0.0 copy-start
  0.6 1.1 slice.3.vec_ref
  1.8 4.6 %collective-permute-start = (f32[2,4,128,128]{3,2,1,0:T(8,128)S(1)}, f32[2,4,128,128]{3,2,1,0:T(8,128)S(1)}, u32[]{:S(2)}, u32[]{:S(2)}) collective-permute-start(f32[2,4,128,128]{3,2,1,0:T(8,128)S(1)} %slice.3.vec_ref), channel_id=1, source_target_pairs={{0,16},{1,17},{16,32},{17,33},{32,48},{33,49},{48,64},{49,65},{64,... | collective-permute-start | bytes 1572872 | tf_op jit(solution)/shard_map/ppermute | solution.py:266
  6.4 6.1 %collective-permute-start.1 = (f32[2,4,128,128]{3,2,1,0:T(8,128)S(1)}, f32[2,4,128,128]{3,2,1,0:T(8,128)S(1)}, u32[]{:S(2)}, u32[]{:S(2)}) collective-permute-start(f32[2,4,128,128]{3,2,1,0:T(8,128)S(1)} %slice.3.vec_ref), channel_id=1, source_target_pairs={{16,0},{17,1},{32,16},{33,17},{48,32},{49,33},{64,48},{65,49},{80,... | collective-permute-start | bytes 1572872 | tf_op jit(solution)/shard_map/ppermute | solution.py:266
  12.5 0.0 copy-done
  12.5 0.6 gather_fusion
  13.2 0.1 subtract_bitcast_fusion
  13.3 0.0 collective-permute-done.low_ref
  13.3 0.0 copy-start.3
  13.3 0.8 copy-done.3
  14.1 3.1 %collective-permute-done.1.high_ref = f32[2,4,128,128]{3,2,1,0:T(8,128)S(1)} collective-permute-done((f32[2,4,128,128]{3,2,1,0:T(8,128)S(1)}, f32[2,4,128,128]{3,2,1,0:T(8,128)S(1)}, u32[]{:S(2)}, u32[]{:S(2)}) %collective-permute-start.1) | collective-permute-done | bytes 524320 | tf_op jit(solution)/shard_map/ppermute | solution.py:266
  17.2 0.0 copy-start.5
  17.2 0.8 copy-done.5
  18.0 0.0 copy-start.4
  18.0 0.7 broadcast_in_dim.25.coef_ref
  18.7 0.3 copy-done.4
  19.0 0.0 copy-start.6
  19.0 1.0 copy-done.6
  20.0 0.9 slices.2
  21.0 3.4 %collective-permute-start.2 = (f32[1024,128]{1,0:T(8,128)S(1)}, f32[1024,128]{1,0:T(8,128)S(1)}, u32[]{:S(2)}, u32[]{:S(2)}) collective-permute-start(f32[1024,128]{1,0:T(8,128)S(1)} %bitcast.9), channel_id=1, source_target_pairs={{0,9},{1,8},{16,25},{17,24},{32,41},{33,40},{48,57},{49,56},{64,73... | collective-permute-start | bytes 1572872 | tf_op jit(solution)/shard_map/ppermute | solution.py:281
  24.4 4.0 %collective-permute-start.6 = (f32[2,4,128,512]{3,2,1,0:T(8,128)}, f32[2,4,128,512]{3,2,1,0:T(8,128)}, u32[]{:S(2)}, u32[]{:S(2)}) collective-permute-start(f32[2,4,128,512]{3,2,1,0:T(8,128)} %vec_ref.1), channel_id=1, source_target_pairs={{0,16},{1,17},{2,18},{3,19},{4,20},{5,21},{6,22},{7,23},{8,24},{9,... | collective-permute-start | bytes 6291464 | tf_op jit(solution)/shard_map/ppermute | solution.py:266
  28.5 4.7 %collective-permute-start.7 = (f32[2,4,128,512]{3,2,1,0:T(8,128)}, f32[2,4,128,512]{3,2,1,0:T(8,128)}, u32[]{:S(2)}, u32[]{:S(2)}) collective-permute-start(f32[2,4,128,512]{3,2,1,0:T(8,128)} %vec_ref.1), channel_id=1, source_target_pairs={{16,0},{17,1},{18,2},{19,3},{20,4},{21,5},{22,6},{23,7},{24,8},{25... | collective-permute-start | bytes 6291464 | tf_op jit(solution)/shard_map/ppermute | solution.py:266
  33.2 0.0 collective-permute-done.2
  33.3 0.1 bitcast_add_fusion
  33.3 1.3 collective-permute-start.3
  34.6 6.1 %collective-permute-done.3 = f32[1024,128]{1,0:T(8,128)S(1)} collective-permute-done((f32[1024,128]{1,0:T(8,128)S(1)}, f32[1024,128]{1,0:T(8,128)S(1)}, u32[]{:S(2)}, u32[]{:S(2)}) %collective-permute-start.3) | collective-permute-done | bytes 524320 | tf_op jit(solution)/shard_map/ppermute | solution.py:281
  40.8 0.1 add.89
  40.8 1.3 collective-permute-start.4
  42.2 6.4 %collective-permute-done.4 = f32[1024,128]{1,0:T(8,128)S(1)} collective-permute-done((f32[1024,128]{1,0:T(8,128)S(1)}, f32[1024,128]{1,0:T(8,128)S(1)}, u32[]{:S(2)}, u32[]{:S(2)}) %collective-permute-start.4) | collective-permute-done | bytes 524320 | tf_op jit(solution)/shard_map/ppermute | solution.py:281
  48.5 0.1 add.90.held_ref
  48.6 9.5 %collective-permute-start.5 = (f32[1024,128]{1,0:T(8,128)S(1)}, f32[1024,128]{1,0:T(8,128)}, u32[]{:S(2)}, u32[]{:S(2)}) collective-permute-start(f32[1024,128]{1,0:T(8,128)S(1)} %add.90.held_ref), channel_id=1, source_target_pairs={{4,3},{2,1},{0,15},{14,13},{12,11},{10,9},{8,7},{6,5},{3,4},{1,2},... | collective-permute-start | bytes 1572872 | tf_op jit(solution)/shard_map/ppermute | solution.py:283
  58.1 0.1 pad_add_fusion.place_ref
  58.2 0.0 collective-permute-done.6.low_ref
  58.2 0.0 collective-permute-done.7.high_ref
  58.2 5.8 %slices.3.matrix_ref = f32[2,4,128,512]{3,2,1,0:T(8,128)S(1)} custom-call(f32[2,4,128,512]{3,2,1,0:T(8,128)} %vec_ref.1, f32[2,4,128,512]{3,2,1,0:T(8,128)} %collective-permute-done.6.low_ref, f32[2,4,128,512]{3,2,1,0:T(8,128)} %collective-permute-done.7.high_ref, f32[4,10,128,128]{3,2,1,0:T(8,128)S(1)} %broadcast_in_dim.25.coef_ref), custom_call_target="tpu_custom_call" | custom-call | tf_op jit(solution)/shard_map/slices/pallas_call | solution.py:64
  64.0 1.7 %collective-permute-done.5.other_ref = f32[1024,128]{1,0:T(8,128)} collective-permute-done((f32[1024,128]{1,0:T(8,128)S(1)}, f32[1024,128]{1,0:T(8,128)}, u32[]{:S(2)}, u32[]{:S(2)}) %collective-permute-start.5) | collective-permute-done | bytes 524320 | tf_op jit(solution)/shard_map/ppermute | solution.py:283
  65.7 4.0 %shared_sums.1 = f32[32,48,128]{2,1,0:T(8,128)S(1)} custom-call(s32[2]{0:T(128)S(1)} %pad_add_fusion.place_ref, f32[1024,128]{1,0:T(8,128)S(1)} %add.90.held_ref, f32[1024,128]{1,0:T(8,128)} %collective-permute-done.5.other_ref, f32[2,4,128,512]{3,2,1,0:T(8,128)S(1)} %slices.3.matrix_ref), custom_call_target="tpu_custom_call" | custom-call | tf_op jit(solution)/shard_map/shared_sums/pallas_call | solution.py:177
  69.6 0.0 copy-start.1
  69.6 1.3 copy-done.1
  71.0 35.1 %all_to_all.10 = f32[32,48,128]{2,1,0:T(8,128)} all-to-all(f32[32,48,128]{2,1,0:T(8,128)S(1)} %shared_sums.1), channel_id=1, replica_groups=mesh['row'=32,'col'=16] {'row'}, dimensions={0} | all-to-all | bytes 1572864 | tf_op jit(solution)/shard_map/all_to_all | solution.py:288
  106.1 0.0 copy-start.2
  106.1 1.3 reduce_sum.9
  107.4 0.1 broadcast_in_dim.27
  107.5 17.9 %all_to_all.11.sums_ref = f32[32,48,128]{2,1,0:T(8,128)S(1)} all-to-all(f32[32,48,128]{2,1,0:T(8,128)S(1)} %broadcast_in_dim.27), channel_id=1, replica_groups=mesh['row'=32,'col'=16] {'row'}, dimensions={0} | all-to-all | bytes 1572864 | tf_op jit(solution)/shard_map/all_to_all | solution.py:290
  125.4 0.0 copy-done.2
  125.4 17.9 %finish.1 = (f32[2,4,128,512]{3,2,1,0:T(8,128)}, f32[1,512]{1,0:T(1,128)}) custom-call(s32[2]{0:T(128)S(1)} %pad_add_fusion.place_ref, f32[32,48,128]{2,1,0:T(8,128)S(1)} %all_to_all.11.sums_ref, f32[1024,128]{1,0:T(8,128)S(1)} %add.90.held_ref, f32[1024,128]{1,0:T(8,128)} %collective-permute-done.5.other_ref, f32[2,4,128,512]{3,2,1,0:T(8,128)S(1)} %copy-done.2), custom_call_target="tpu_custom_call" | custom-call | tf_op jit(solution)/shard_map/finish/pallas_call | solution.py:229
  (4 shorter events, 0.1 us)
Async XLA Ops:
  0.6 11.9 %copy-start = (s32[4,128,128]{2,1,0:T(8,128)S(1)}, s32[4,128,128]{2,1,0:T(8,128)}, u32[]{:S(2)}) copy-start(s32[4,128,128]{2,1,0:T(8,128)} %param.3) | copy-start | bytes 786436
  1.8 11.5 %collective-permute-start = (f32[2,4,128,128]{3,2,1,0:T(8,128)S(1)}, f32[2,4,128,128]{3,2,1,0:T(8,128)S(1)}, u32[]{:S(2)}, u32[]{:S(2)}) collective-permute-start(f32[2,4,128,128]{3,2,1,0:T(8,128)S(1)} %slice.3.vec_ref), channel_id=1, source_target_pairs={{0,16},{1,17},{16,32},{17,33},{32,48},{33,49},{48,64},{49,65},{64,... | collective-permute-start | bytes 1572872 | tf_op jit(solution)/shard_map/ppermute | solution.py:266
  6.4 10.8 %collective-permute-start.1 = (f32[2,4,128,128]{3,2,1,0:T(8,128)S(1)}, f32[2,4,128,128]{3,2,1,0:T(8,128)S(1)}, u32[]{:S(2)}, u32[]{:S(2)}) collective-permute-start(f32[2,4,128,128]{3,2,1,0:T(8,128)S(1)} %slice.3.vec_ref), channel_id=1, source_target_pairs={{16,0},{17,1},{32,16},{33,17},{48,32},{49,33},{64,48},{65,49},{80,... | collective-permute-start | bytes 1572872 | tf_op jit(solution)/shard_map/ppermute | solution.py:266
  13.3 0.8 copy-start.3
  17.2 0.8 copy-start.5
  18.0 1.0 copy-start.4
  19.0 1.0 copy-start.6
  21.0 12.2 %collective-permute-start.2 = (f32[1024,128]{1,0:T(8,128)S(1)}, f32[1024,128]{1,0:T(8,128)S(1)}, u32[]{:S(2)}, u32[]{:S(2)}) collective-permute-start(f32[1024,128]{1,0:T(8,128)S(1)} %bitcast.9), channel_id=1, source_target_pairs={{0,9},{1,8},{16,25},{17,24},{32,41},{33,40},{48,57},{49,56},{64,73... | collective-permute-start | bytes 1572872 | tf_op jit(solution)/shard_map/ppermute | solution.py:281
  24.4 33.7 %collective-permute-start.6 = (f32[2,4,128,512]{3,2,1,0:T(8,128)}, f32[2,4,128,512]{3,2,1,0:T(8,128)}, u32[]{:S(2)}, u32[]{:S(2)}) collective-permute-start(f32[2,4,128,512]{3,2,1,0:T(8,128)} %vec_ref.1), channel_id=1, source_target_pairs={{0,16},{1,17},{2,18},{3,19},{4,20},{5,21},{6,22},{7,23},{8,24},{9,... | collective-permute-start | bytes 6291464 | tf_op jit(solution)/shard_map/ppermute | solution.py:266
  28.5 29.7 %collective-permute-start.7 = (f32[2,4,128,512]{3,2,1,0:T(8,128)}, f32[2,4,128,512]{3,2,1,0:T(8,128)}, u32[]{:S(2)}, u32[]{:S(2)}) collective-permute-start(f32[2,4,128,512]{3,2,1,0:T(8,128)} %vec_ref.1), channel_id=1, source_target_pairs={{16,0},{17,1},{18,2},{19,3},{20,4},{21,5},{22,6},{23,7},{24,8},{25... | collective-permute-start | bytes 6291464 | tf_op jit(solution)/shard_map/ppermute | solution.py:266
  33.3 7.5 %collective-permute-start.3 = (f32[1024,128]{1,0:T(8,128)S(1)}, f32[1024,128]{1,0:T(8,128)S(1)}, u32[]{:S(2)}, u32[]{:S(2)}) collective-permute-start(f32[1024,128]{1,0:T(8,128)S(1)} %bitcast_add_fusion), channel_id=1, source_target_pairs={{0,4},{8,12},{1,13},{9,5},{16,20},{24,28},{17,29},{25,21},{32,36},... | collective-permute-start | bytes 1572872 | tf_op jit(solution)/shard_map/ppermute | solution.py:281
  40.8 7.7 %collective-permute-start.4 = (f32[1024,128]{1,0:T(8,128)S(1)}, f32[1024,128]{1,0:T(8,128)S(1)}, u32[]{:S(2)}, u32[]{:S(2)}) collective-permute-start(f32[1024,128]{1,0:T(8,128)S(1)} %add.89), channel_id=1, source_target_pairs={{1,3},{13,15},{5,7},{9,11},{4,2},{0,14},{8,6},{12,10},{17,19},{29,... | collective-permute-start | bytes 1572872 | tf_op jit(solution)/shard_map/ppermute | solution.py:281
  48.6 17.1 %collective-permute-start.5 = (f32[1024,128]{1,0:T(8,128)S(1)}, f32[1024,128]{1,0:T(8,128)}, u32[]{:S(2)}, u32[]{:S(2)}) collective-permute-start(f32[1024,128]{1,0:T(8,128)S(1)} %add.90.held_ref), channel_id=1, source_target_pairs={{4,3},{2,1},{0,15},{14,13},{12,11},{10,9},{8,7},{6,5},{3,4},{1,2},... | collective-permute-start | bytes 1572872 | tf_op jit(solution)/shard_map/ppermute | solution.py:283
  69.6 1.3 copy-start.1
  106.1 19.3 %copy-start.2 = (f32[2,4,128,512]{3,2,1,0:T(8,128)S(1)}, f32[2,4,128,512]{3,2,1,0:T(8,128)}, u32[]{:S(2)}) copy-start(f32[2,4,128,512]{3,2,1,0:T(8,128)} %copy-done.1) | copy-start | bytes 6291460

commit v6 on v4

--- a/solution.py
+++ b/solution.py
@@ -48,7 +48,9 @@
             center = current[i]
             beside = current[i + 1] + current[i - 1]
             beside = beside + pltpu.roll(center, 1, 0) + pltpu.roll(center, sites - 1, 0)
-            previous[i] = coef_ref[step, i - rows + depth - 1] * center - beside - previous[i]
+            along = coef_ref[step, pl.ds(i - rows + depth - 1, 1), :]
+            coef = jnp.broadcast_to(along, (center.shape[1], sites)).T
+            previous[i] = coef * center - beside - previous[i]
             return 0
 
         lax.fori_loop(rows - reach, 2 * rows + reach, one_row, 0)
@@ -64,7 +66,7 @@
     return pl.pallas_call(
         functools.partial(stencil_kernel, coefs.shape[0]),
         grid=(columns // BLOCK,),
-        in_specs=[block, block, block, pl.BlockSpec(coefs.shape, lambda i: (0, 0, 0, 0))],
+        in_specs=[block, block, block, pl.BlockSpec(coefs.shape, lambda i: (0, 0, 0))],
         out_specs=block,
         out_shape=jax.ShapeDtypeStruct(vectors.shape, jnp.float32),
         scratch_shapes=[pltpu.VMEM((3 * rows, sites, BLOCK), jnp.float32)] * 2,
@@ -296,7 +298,6 @@
 
     site_rows = (row_index * rows - depth + 1 + jnp.arange(rows + 2 * depth - 2)) % potential.shape[1]
     coefs = energy - site_values(jnp.take(potential, site_rows, axis=1))
-    coefs = jnp.broadcast_to(coefs[..., None], coefs.shape + (BLOCK,))
 
     panel = vectors[..., :PANEL]
     panel = stencil(panel, *neighbours(panel, [0, 1]), coefs).reshape(-1, PANEL)

time: 143 us -> 146 us (1.021)
  Pallas kernels: 28.4 us -> 38.3 us
  starting transfers between devices: 35.1 us -> 26.3 us
  waiting for transfers between devices: 17.3 us -> 25.8 us
  blocking collectives: 53 us -> 49 us
  local copies, waits for them, and re-layouts: 6.75 us -> 3.49 us
    pallas_call x2, Pallas kernels: 6.7 us -> 17.9 us  [stencil(): pl.pallas_call(functools.partial(stencil_kernel, coefs.shape[0]), grid=(c...]
    ppermute x3, waiting for transfers between devices: 12.5 us -> 20.4 us  [on_device(): held = held + lax.ppermute(held, 'col', pairs)]
    ppermute x1, starting transfers between devices: 9.5 us -> 1.92 us  [on_device(): other = lax.ppermute(held, 'col', pairs + [(b, a) for a, b in pairs])]
    ppermute x2, waiting for transfers between devices: 0.01 us -> 5.34 us  [neighbours(): lax.ppermute(block, ('row', 'col'), ahead)]
    all_to_all x1, blocking collectives: 35 us -> 31.1 us  [on_device(): lax.all_to_all(shared_sums(place, held, other, blocks, row_count), 'row',...]
    ppermute x2, waiting for transfers between devices: 3.11 us -> 0.01 us  [neighbours(): lax.ppermute(block, ('row', 'col'), back)]
    ppermute x2, starting transfers between devices: 10.8 us -> 13.8 us  [neighbours(): lax.ppermute(block, ('row', 'col'), back)]
    ppermute x2, starting transfers between devices: 8.64 us -> 5.97 us  [neighbours(): lax.ppermute(block, ('row', 'col'), ahead)]
  transfers between devices with their start and end apart: 8 -> 8, of which waited for: 4 -> 3; matrix products, arithmetic and copies ran while one was open for 1% -> 1% of each run, Pallas kernels for 4% -> 9%
where the time goes in v6:
time: 146 us; the launch traced here: 145 us
  blocking collectives  49 us (34%)
  Pallas kernels  38.3 us (26%)
  starting transfers between devices  26.3 us (18%)
  waiting for transfers between devices  25.8 us (18%)
  local copies, waits for them, and re-layouts  3.49 us (2%)
  other arithmetic  1.59 us (1%)
    all_to_all x1, blocking collectives, on_device(): lax.all_to_all(shared_sums(place, held, other, blocks, row_count), 'row',...  31.1 us
    ppermute x3, waiting for transfers between devices, on_device(): held = held + lax.ppermute(held, 'col', pairs)  20.4 us
    pallas_call x2, Pallas kernels, stencil(): pl.pallas_call(functools.partial(stencil_kernel, coefs.shape[0]), grid=(c...  17.9 us
    all_to_all x1, blocking collectives, on_device(): lax.all_to_all(jnp.broadcast_to(share, (row_count,) + share.shape), 'row'...  17.9 us
    ppermute x2, starting transfers between devices, neighbours(): lax.ppermute(block, ('row', 'col'), back)  13.8 us
    pallas_call x2, Pallas kernels, call(): pl.pallas_call(kernel, out_shape=shapes, compiler_params=pltpu.CompilerPa...  11.7 us
    ppermute x2, starting transfers between devices, neighbours(): lax.ppermute(block, ('row', 'col'), ahead)  5.97 us
    ppermute x2, waiting for transfers between devices, neighbours(): lax.ppermute(block, ('row', 'col'), ahead)  5.34 us
  transfers between devices with their start and end apart: 8, of which 3 were waited for; matrix products, arithmetic and copies ran while one was open for 1% of the time, Pallas kernels for 9%

profile of v6, /device:TPU:1, one launch (start us, length us, event | category | flops | bytes accessed | tf_op | source)
XLA Modules:
  0.0 145.4 jit_solution(1722183768431159056)
XLA Ops:
  0.6 0.0 copy-start
  0.6 0.0 copy-start.1
  0.7 1.2 slice.3.vec_ref
  1.9 8.8 %collective-permute-start.1 = (f32[2,4,128,128]{3,2,1,0:T(8,128)S(1)}, f32[2,4,128,128]{3,2,1,0:T(8,128)S(1)}, u32[]{:S(2)}, u32[]{:S(2)}) collective-permute-start(f32[2,4,128,128]{3,2,1,0:T(8,128)S(1)} %slice.3.vec_ref), channel_id=1, source_target_pairs={{16,0},{17,1},{32,16},{33,17},{48,32},{49,33},{64,48},{65,49},{80,... | collective-permute-start | bytes 1572872 | tf_op jit(solution)/shard_map/ppermute | solution.py:297
  10.7 1.9 %collective-permute-start = (f32[2,4,128,128]{3,2,1,0:T(8,128)S(1)}, f32[2,4,128,128]{3,2,1,0:T(8,128)}, u32[]{:S(2)}, u32[]{:S(2)}) collective-permute-start(f32[2,4,128,128]{3,2,1,0:T(8,128)S(1)} %slice.3.vec_ref), channel_id=1, source_target_pairs={{0,16},{1,17},{16,32},{17,33},{32,48},{33,49},{48,64},{49,65},{64,... | collective-permute-start | bytes 1572872 | tf_op jit(solution)/shard_map/ppermute | solution.py:297
  12.7 0.0 copy-done
  12.7 0.6 gather_fusion
  13.3 0.1 subtract_bitcast_fusion.coef_ref
  13.4 0.0 collective-permute-done.1.high_ref
  13.4 5.3 %collective-permute-done.low_ref = f32[2,4,128,128]{3,2,1,0:T(8,128)} collective-permute-done((f32[2,4,128,128]{3,2,1,0:T(8,128)S(1)}, f32[2,4,128,128]{3,2,1,0:T(8,128)}, u32[]{:S(2)}, u32[]{:S(2)}) %collective-permute-start) | collective-permute-done | bytes 524320 | tf_op jit(solution)/shard_map/ppermute | solution.py:297
  18.7 4.1 %slices.2 = f32[2,4,128,128]{3,2,1,0:T(8,128)S(1)} custom-call(f32[2,4,128,128]{3,2,1,0:T(8,128)S(1)} %slice.3.vec_ref, f32[2,4,128,128]{3,2,1,0:T(8,128)} %collective-permute-done.low_ref, f32[2,4,128,128]{3,2,1,0:T(8,128)S(1)} %collective-permute-done.1.high_ref, f32[4,10,128]{2,1,0:T(8,128)S(1)} %subtract_bitcast_fusion.coef_ref), custom_call_target="tpu_custom_call" | custom-call | tf_op jit(solution)/shard_map/slices/pallas_call | solution.py:66
  22.8 2.0 %collective-permute-start.2 = (f32[1024,128]{1,0:T(8,128)S(1)}, f32[1024,128]{1,0:T(8,128)S(1)}, u32[]{:S(2)}, u32[]{:S(2)}) collective-permute-start(f32[1024,128]{1,0:T(8,128)S(1)} %bitcast.9), channel_id=1, source_target_pairs={{0,9},{1,8},{16,25},{17,24},{32,41},{33,40},{48,57},{49,56},{64,73... | collective-permute-start | bytes 1572872 | tf_op jit(solution)/shard_map/ppermute | solution.py:311
  24.8 0.0 copy-done.1
  24.8 4.0 %collective-permute-start.6 = (f32[2,4,128,512]{3,2,1,0:T(8,128)S(1)}, f32[2,4,128,512]{3,2,1,0:T(8,128)}, u32[]{:S(2)}, u32[]{:S(2)}) collective-permute-start(f32[2,4,128,512]{3,2,1,0:T(8,128)S(1)} %copy-done.1), channel_id=1, source_target_pairs={{0,16},{1,17},{2,18},{3,19},{4,20},{5,21},{6,22},{7,23},{8,24},{9,... | collective-permute-start | bytes 6291464 | tf_op jit(solution)/shard_map/ppermute | solution.py:297
  28.9 5.0 %collective-permute-start.7 = (f32[2,4,128,512]{3,2,1,0:T(8,128)S(1)}, f32[2,4,128,512]{3,2,1,0:T(8,128)}, u32[]{:S(2)}, u32[]{:S(2)}) collective-permute-start(f32[2,4,128,512]{3,2,1,0:T(8,128)S(1)} %copy-done.1), channel_id=1, source_target_pairs={{16,0},{17,1},{18,2},{19,3},{20,4},{21,5},{22,6},{23,7},{24,8},{25... | collective-permute-start | bytes 6291464 | tf_op jit(solution)/shard_map/ppermute | solution.py:297
  33.9 0.0 collective-permute-done.2
  33.9 0.1 bitcast_add_fusion
  34.0 1.3 collective-permute-start.3
  35.3 6.5 %collective-permute-done.3 = f32[1024,128]{1,0:T(8,128)S(1)} collective-permute-done((f32[1024,128]{1,0:T(8,128)S(1)}, f32[1024,128]{1,0:T(8,128)S(1)}, u32[]{:S(2)}, u32[]{:S(2)}) %collective-permute-start.3) | collective-permute-done | bytes 524320 | tf_op jit(solution)/shard_map/ppermute | solution.py:311
  41.8 0.1 add.81
  41.9 1.3 collective-permute-start.4
  43.2 13.9 %collective-permute-done.4 = f32[1024,128]{1,0:T(8,128)S(1)} collective-permute-done((f32[1024,128]{1,0:T(8,128)S(1)}, f32[1024,128]{1,0:T(8,128)S(1)}, u32[]{:S(2)}, u32[]{:S(2)}) %collective-permute-start.4) | collective-permute-done | bytes 524320 | tf_op jit(solution)/shard_map/ppermute | solution.py:311
  57.1 0.1 add.82.held_ref
  57.2 1.9 %collective-permute-start.5 = (f32[1024,128]{1,0:T(8,128)S(1)}, f32[1024,128]{1,0:T(8,128)S(1)}, u32[]{:S(2)}, u32[]{:S(2)}) collective-permute-start(f32[1024,128]{1,0:T(8,128)S(1)} %add.82.held_ref), channel_id=1, source_target_pairs={{4,3},{2,1},{0,15},{14,13},{12,11},{10,9},{8,7},{6,5},{3,4},{1,2},... | collective-permute-start | bytes 1572872 | tf_op jit(solution)/shard_map/ppermute | solution.py:313
  59.1 0.1 pad_add_fusion.place_ref
  59.2 0.0 collective-permute-done.6.low_ref
  59.2 0.0 collective-permute-done.7.high_ref
  59.2 0.0 copy-start.2
  59.2 1.6 %copy-done.2 = f32[2,4,128,512]{3,2,1,0:T(8,128)S(1)} copy-done((f32[2,4,128,512]{3,2,1,0:T(8,128)S(1)}, f32[2,4,128,512]{3,2,1,0:T(8,128)}, u32[]{:S(2)}) %copy-start.2) | copy-done | bytes 2097176
  60.8 13.8 %slices.3.matrix_ref = f32[2,4,128,512]{3,2,1,0:T(8,128)S(1)} custom-call(f32[2,4,128,512]{3,2,1,0:T(8,128)S(1)} %copy-done.2, f32[2,4,128,512]{3,2,1,0:T(8,128)} %collective-permute-done.6.low_ref, f32[2,4,128,512]{3,2,1,0:T(8,128)} %collective-permute-done.7.high_ref, f32[4,10,128]{2,1,0:T(8,128)S(1)} %subtract_bitcast_fusion.coef_ref), custom_call_target="tpu_custom_call" | custom-call | tf_op jit(solution)/shard_map/slices/pallas_call | solution.py:66
  74.6 0.0 collective-permute-done.5.other_ref
  74.7 3.5 %shared_sums.1 = f32[32,48,128]{2,1,0:T(8,128)S(1)} custom-call(s32[2]{0:T(128)S(1)} %pad_add_fusion.place_ref, f32[1024,128]{1,0:T(8,128)S(1)} %add.82.held_ref, f32[1024,128]{1,0:T(8,128)S(1)} %collective-permute-done.5.other_ref, f32[2,4,128,512]{3,2,1,0:T(8,128)S(1)} %slices.3.matrix_ref), custom_call_target="tpu_custom_call" | custom-call | tf_op jit(solution)/shard_map/shared_sums/pallas_call | solution.py:207
  78.1 31.1 %all_to_all.10 = f32[32,48,128]{2,1,0:T(8,128)} all-to-all(f32[32,48,128]{2,1,0:T(8,128)S(1)} %shared_sums.1), channel_id=1, replica_groups=mesh['row'=32,'col'=16] {'row'}, dimensions={0} | all-to-all | bytes 1572864 | tf_op jit(solution)/shard_map/all_to_all | solution.py:318
  109.2 1.2 reduce_sum.9
  110.4 0.1 broadcast_in_dim.20
  110.5 17.9 %all_to_all.11.sums_ref = f32[32,48,128]{2,1,0:T(8,128)S(1)} all-to-all(f32[32,48,128]{2,1,0:T(8,128)S(1)} %broadcast_in_dim.20), channel_id=1, replica_groups=mesh['row'=32,'col'=16] {'row'}, dimensions={0} | all-to-all | bytes 1572864 | tf_op jit(solution)/shard_map/all_to_all | solution.py:320
  128.4 5.9 %factor_a.1 = (f32[128,128]{1,0:T(8,128)S(1)}, f32[128,128]{1,0:T(8,128)S(1)}, f32[128,128]{1,0:T(8,128)S(1)}) custom-call(f32[32,48,128]{2,1,0:T(8,128)S(1)} %all_to_all.11.sums_ref), custom_call_target="tpu_custom_call" | custom-call | tf_op jit(solution)/shard_map/factor_a/pallas_call | solution.py:166
  134.3 5.8 %factor_b.1.inv_ref = f32[256,256]{1,0:T(8,128)S(1)} custom-call(f32[32,48,128]{2,1,0:T(8,128)S(1)} %all_to_all.11.sums_ref, f32[128,128]{1,0:T(8,128)S(1)} %get-tuple-element.7.rest_ref, f32[128,128]{1,0:T(8,128)S(1)} %get-tuple-element.8.inv0_ref, f32[128,128]{1,0:T(8,128)S(1)} %get-tuple-element.9.cross_ref), custom_call_target="tpu_custom_call" | custom-call | tf_op jit(solution)/shard_map/factor_b/pallas_call | solution.py:166
  140.0 5.3 %finish.1 = (f32[2,4,128,512]{3,2,1,0:T(8,128)}, f32[1,512]{1,0:T(1,128)}) custom-call(s32[2]{0:T(128)S(1)} %pad_add_fusion.place_ref, f32[256,256]{1,0:T(8,128)S(1)} %factor_b.1.inv_ref, f32[32,48,128]{2,1,0:T(8,128)S(1)} %all_to_all.11.sums_ref, f32[1024,128]{1,0:T(8,128)S(1)} %add.82.held_ref, f32[1024,128]{1,0:T(8,128)S(1)} %collective-permute-done.5.other_ref, ...), custom_call_target="tpu_custom_call" | custom-call | tf_op jit(solution)/shard_map/finish/pallas_call | solution.py:259
  (4 shorter events, 0.1 us)
Async XLA Ops:
  0.6 12.0 %copy-start = (s32[4,128,128]{2,1,0:T(8,128)S(1)}, s32[4,128,128]{2,1,0:T(8,128)}, u32[]{:S(2)}) copy-start(s32[4,128,128]{2,1,0:T(8,128)} %param.3) | copy-start | bytes 786436
  0.6 24.2 %copy-start.1 = (f32[2,4,128,512]{3,2,1,0:T(8,128)S(1)}, f32[2,4,128,512]{3,2,1,0:T(8,128)}, u32[]{:S(2)}) copy-start(f32[2,4,128,512]{3,2,1,0:T(8,128)} %vec_ref.1) | copy-start | bytes 6291460
  1.9 11.5 %collective-permute-start.1 = (f32[2,4,128,128]{3,2,1,0:T(8,128)S(1)}, f32[2,4,128,128]{3,2,1,0:T(8,128)S(1)}, u32[]{:S(2)}, u32[]{:S(2)}) collective-permute-start(f32[2,4,128,128]{3,2,1,0:T(8,128)S(1)} %slice.3.vec_ref), channel_id=1, source_target_pairs={{16,0},{17,1},{32,16},{33,17},{48,32},{49,33},{64,48},{65,49},{80,... | collective-permute-start | bytes 1572872 | tf_op jit(solution)/shard_map/ppermute | solution.py:297
  10.7 8.0 %collective-permute-start = (f32[2,4,128,128]{3,2,1,0:T(8,128)S(1)}, f32[2,4,128,128]{3,2,1,0:T(8,128)}, u32[]{:S(2)}, u32[]{:S(2)}) collective-permute-start(f32[2,4,128,128]{3,2,1,0:T(8,128)S(1)} %slice.3.vec_ref), channel_id=1, source_target_pairs={{0,16},{1,17},{16,32},{17,33},{32,48},{33,49},{48,64},{49,65},{64,... | collective-permute-start | bytes 1572872 | tf_op jit(solution)/shard_map/ppermute | solution.py:297
  22.8 11.1 %collective-permute-start.2 = (f32[1024,128]{1,0:T(8,128)S(1)}, f32[1024,128]{1,0:T(8,128)S(1)}, u32[]{:S(2)}, u32[]{:S(2)}) collective-permute-start(f32[1024,128]{1,0:T(8,128)S(1)} %bitcast.9), channel_id=1, source_target_pairs={{0,9},{1,8},{16,25},{17,24},{32,41},{33,40},{48,57},{49,56},{64,73... | collective-permute-start | bytes 1572872 | tf_op jit(solution)/shard_map/ppermute | solution.py:311
  24.8 34.4 %collective-permute-start.6 = (f32[2,4,128,512]{3,2,1,0:T(8,128)S(1)}, f32[2,4,128,512]{3,2,1,0:T(8,128)}, u32[]{:S(2)}, u32[]{:S(2)}) collective-permute-start(f32[2,4,128,512]{3,2,1,0:T(8,128)S(1)} %copy-done.1), channel_id=1, source_target_pairs={{0,16},{1,17},{2,18},{3,19},{4,20},{5,21},{6,22},{7,23},{8,24},{9,... | collective-permute-start | bytes 6291464 | tf_op jit(solution)/shard_map/ppermute | solution.py:297
  28.9 30.4 %collective-permute-start.7 = (f32[2,4,128,512]{3,2,1,0:T(8,128)S(1)}, f32[2,4,128,512]{3,2,1,0:T(8,128)}, u32[]{:S(2)}, u32[]{:S(2)}) collective-permute-start(f32[2,4,128,512]{3,2,1,0:T(8,128)S(1)} %copy-done.1), channel_id=1, source_target_pairs={{16,0},{17,1},{18,2},{19,3},{20,4},{21,5},{22,6},{23,7},{24,8},{25... | collective-permute-start | bytes 6291464 | tf_op jit(solution)/shard_map/ppermute | solution.py:297
  34.0 7.8 %collective-permute-start.3 = (f32[1024,128]{1,0:T(8,128)S(1)}, f32[1024,128]{1,0:T(8,128)S(1)}, u32[]{:S(2)}, u32[]{:S(2)}) collective-permute-start(f32[1024,128]{1,0:T(8,128)S(1)} %bitcast_add_fusion), channel_id=1, source_target_pairs={{0,4},{8,12},{1,13},{9,5},{16,20},{24,28},{17,29},{25,21},{32,36},... | collective-permute-start | bytes 1572872 | tf_op jit(solution)/shard_map/ppermute | solution.py:311
  41.9 15.3 %collective-permute-start.4 = (f32[1024,128]{1,0:T(8,128)S(1)}, f32[1024,128]{1,0:T(8,128)S(1)}, u32[]{:S(2)}, u32[]{:S(2)}) collective-permute-start(f32[1024,128]{1,0:T(8,128)S(1)} %add.81), channel_id=1, source_target_pairs={{1,3},{13,15},{5,7},{9,11},{4,2},{0,14},{8,6},{12,10},{17,19},{29,... | collective-permute-start | bytes 1572872 | tf_op jit(solution)/shard_map/ppermute | solution.py:311
  57.2 17.5 %collective-permute-start.5 = (f32[1024,128]{1,0:T(8,128)S(1)}, f32[1024,128]{1,0:T(8,128)S(1)}, u32[]{:S(2)}, u32[]{:S(2)}) collective-permute-start(f32[1024,128]{1,0:T(8,128)S(1)} %add.82.held_ref), channel_id=1, source_target_pairs={{4,3},{2,1},{0,15},{14,13},{12,11},{10,9},{8,7},{6,5},{3,4},{1,2},... | collective-permute-start | bytes 1572872 | tf_op jit(solution)/shard_map/ppermute | solution.py:313
  59.2 1.6 %copy-start.2 = (f32[2,4,128,512]{3,2,1,0:T(8,128)S(1)}, f32[2,4,128,512]{3,2,1,0:T(8,128)}, u32[]{:S(2)}) copy-start(f32[2,4,128,512]{3,2,1,0:T(8,128)} %vec_ref.1) | copy-start | bytes 6291460

commit v7 on v6

--- a/solution.py
+++ b/solution.py
@@ -44,29 +44,26 @@
     for step in range(depth):
         reach = depth - 1 - step
 
-        def one_row(i, _, current=current, previous=previous, step=step):
+        for i in range(rows - reach, 2 * rows + reach):
             center = current[i]
             beside = current[i + 1] + current[i - 1]
             beside = beside + pltpu.roll(center, 1, 0) + pltpu.roll(center, sites - 1, 0)
-            along = coef_ref[step, pl.ds(i - rows + depth - 1, 1), :]
-            coef = jnp.broadcast_to(along, (center.shape[1], sites)).T
+            k = step * (rows + 2 * depth - 2) + i - rows + depth - 1
+            coef = jnp.broadcast_to(coef_ref[:, k:k + 1], center.shape)
             previous[i] = coef * center - beside - previous[i]
-            return 0
-
-        lax.fori_loop(rows - reach, 2 * rows + reach, one_row, 0)
         current, previous = previous, current
     for i in range(rows):
         out_ref[0, i] = current[rows + i]
         out_ref[1, i] = previous[rows + i]
 
 
-def stencil(vectors, low, high, coefs):
+def stencil(vectors, low, high, coefs, depth):
     _, rows, sites, columns = vectors.shape
     block = pl.BlockSpec((2, rows, sites, BLOCK), lambda i: (0, 0, 0, i))
     return pl.pallas_call(
-        functools.partial(stencil_kernel, coefs.shape[0]),
+        functools.partial(stencil_kernel, depth),
         grid=(columns // BLOCK,),
-        in_specs=[block, block, block, pl.BlockSpec(coefs.shape, lambda i: (0, 0, 0))],
+        in_specs=[block, block, block, pl.BlockSpec(coefs.shape, lambda i: (0, 0))],
         out_specs=block,
         out_shape=jax.ShapeDtypeStruct(vectors.shape, jnp.float32),
         scratch_shapes=[pltpu.VMEM((3 * rows, sites, BLOCK), jnp.float32)] * 2,
@@ -298,9 +295,11 @@
 
     site_rows = (row_index * rows - depth + 1 + jnp.arange(rows + 2 * depth - 2)) % potential.shape[1]
     coefs = energy - site_values(jnp.take(potential, site_rows, axis=1))
+    coefs = coefs.reshape(-1, sites).T
+    coefs = jnp.pad(coefs, ((0, 0), (0, BLOCK - coefs.shape[1])))
 
     panel = vectors[..., :PANEL]
-    panel = stencil(panel, *neighbours(panel, [0, 1]), coefs).reshape(-1, PANEL)
+    panel = stencil(panel, *neighbours(panel, [0, 1]), coefs, depth).reshape(-1, PANEL)
     held = jnp.where(col_index < 2, panel, 0.0)
     stages = [
         [(0, 9), (1, 8)],
@@ -314,7 +313,7 @@
     has_first = functools.reduce(jnp.logical_or, [col_index == c for c in (0, 2, 4, 5, 7, 9, 11, 14)])
     place = jnp.stack([col_index, has_first.astype(jnp.int32)])
 
-    blocks = stencil(vectors, *neighbours(vectors, range(col_count)), coefs)
+    blocks = stencil(vectors, *neighbours(vectors, range(col_count)), coefs, depth)
     sums = lax.all_to_all(shared_sums(place, held, other, blocks, row_count), "row", 0, 0)
     share = jnp.sum(sums, 0)
     sums = lax.all_to_all(jnp.broadcast_to(share, (row_count,) + share.shape), "row", 0, 0)

time: 146 us -> 138 us (0.945)
  Pallas kernels: 38.3 us -> 27.3 us
  starting transfers between devices: 26.3 us -> 32.4 us
  waiting for transfers between devices: 25.8 us -> 20 us
  blocking collectives: 49 us -> 51.6 us
    pallas_call x2, Pallas kernels: 17.9 us -> 6.88 us  [stencil(): pl.pallas_call(functools.partial(stencil_kernel, depth), grid=(columns //...]
    ppermute x3, waiting for transfers between devices: 20.4 us -> 12.6 us  [on_device(): held = held + lax.ppermute(held, 'col', pairs)]
    ppermute x1, starting transfers between devices: 1.92 us -> 7.9 us  [on_device(): other = lax.ppermute(held, 'col', pairs + [(b, a) for a, b in pairs])]
    all_to_all x1, blocking collectives: 31.1 us -> 33.8 us  [on_device(): lax.all_to_all(shared_sums(place, held, other, blocks, row_count), 'row',...]
    ppermute x1, waiting for transfers between devices: 0.01 us -> 2.27 us  [on_device(): other = lax.ppermute(held, 'col', pairs + [(b, a) for a, b in pairs])]
  transfers between devices with their start and end apart: 8 -> 8, of which waited for: 3 -> 4; matrix products, arithmetic and copies ran while one was open for 1% -> 1% of each run, Pallas kernels for 9% -> 4%
where the time goes in v7:
time: 138 us; the launch traced here: 137 us
  blocking collectives  51.6 us (37%)
  starting transfers between devices  32.4 us (23%)
  Pallas kernels  27.3 us (20%)
  waiting for transfers between devices  20 us (14%)
  local copies, waits for them, and re-layouts  3.58 us (3%)
  other arithmetic  1.53 us (1%)
    all_to_all x1, blocking collectives, on_device(): lax.all_to_all(shared_sums(place, held, other, blocks, row_count), 'row',...  33.8 us
    all_to_all x1, blocking collectives, on_device(): lax.all_to_all(jnp.broadcast_to(share, (row_count,) + share.shape), 'row'...  17.9 us
    ppermute x2, starting transfers between devices, neighbours(): lax.ppermute(block, ('row', 'col'), back)  13.8 us
    ppermute x3, waiting for transfers between devices, on_device(): held = held + lax.ppermute(held, 'col', pairs)  12.6 us
    pallas_call x2, Pallas kernels, call(): pl.pallas_call(kernel, out_shape=shapes, compiler_params=pltpu.CompilerPa...  11.7 us
    ppermute x1, starting transfers between devices, on_device(): other = lax.ppermute(held, 'col', pairs + [(b, a) for a, b in pairs])  7.9 us
    pallas_call x2, Pallas kernels, stencil(): pl.pallas_call(functools.partial(stencil_kernel, depth), grid=(columns //...  6.88 us
    ppermute x2, starting transfers between devices, neighbours(): lax.ppermute(block, ('row', 'col'), ahead)  5.97 us
  transfers between devices with their start and end apart: 8, of which 4 were waited for; matrix products, arithmetic and copies ran while one was open for 1% of the time, Pallas kernels for 4%

profile of v7, /device:TPU:1, one launch (start us, length us, event | category | flops | bytes accessed | tf_op | source)
XLA Modules:
  0.0 137.5 jit_solution(743396098441250554)
XLA Ops:
  0.6 0.0 copy-start
  0.6 1.1 slice.3.vec_ref
  1.8 0.0 copy-start.1
  1.8 8.9 %collective-permute-start.1 = (f32[2,4,128,128]{3,2,1,0:T(8,128)S(1)}, f32[2,4,128,128]{3,2,1,0:T(8,128)S(1)}, u32[]{:S(2)}, u32[]{:S(2)}) collective-permute-start(f32[2,4,128,128]{3,2,1,0:T(8,128)S(1)} %slice.3.vec_ref), channel_id=1, source_target_pairs={{16,0},{17,1},{32,16},{33,17},{48,32},{49,33},{64,48},{65,49},{80,... | collective-permute-start | bytes 1572872 | tf_op jit(solution)/shard_map/ppermute | solution.py:294
  10.7 1.9 %collective-permute-start = (f32[2,4,128,128]{3,2,1,0:T(8,128)S(1)}, f32[2,4,128,128]{3,2,1,0:T(8,128)}, u32[]{:S(2)}, u32[]{:S(2)}) collective-permute-start(f32[2,4,128,128]{3,2,1,0:T(8,128)S(1)} %slice.3.vec_ref), channel_id=1, source_target_pairs={{0,16},{1,17},{16,32},{17,33},{32,48},{33,49},{48,64},{49,65},{64,... | collective-permute-start | bytes 1572872 | tf_op jit(solution)/shard_map/ppermute | solution.py:294
  12.7 0.1 broadcast_in_dim.22
  12.8 0.0 copy-done
  12.8 0.6 gather_fusion
  13.4 0.1 copy.6
  13.6 0.0 collective-permute-done.1.high_ref
  13.6 5.2 %collective-permute-done.low_ref = f32[2,4,128,128]{3,2,1,0:T(8,128)} collective-permute-done((f32[2,4,128,128]{3,2,1,0:T(8,128)S(1)}, f32[2,4,128,128]{3,2,1,0:T(8,128)}, u32[]{:S(2)}, u32[]{:S(2)}) %collective-permute-start) | collective-permute-done | bytes 524320 | tf_op jit(solution)/shard_map/ppermute | solution.py:294
  18.7 1.8 %slices.2 = f32[2,4,128,128]{3,2,1,0:T(8,128)S(1)} custom-call(f32[2,4,128,128]{3,2,1,0:T(8,128)S(1)} %slice.3.vec_ref, f32[2,4,128,128]{3,2,1,0:T(8,128)} %collective-permute-done.low_ref, f32[2,4,128,128]{3,2,1,0:T(8,128)S(1)} %collective-permute-done.1.high_ref, f32[128,128]{1,0:T(8,128)S(1)} %pad.4.coef_ref), custom_call_target="tpu_custom_call" | custom-call | tf_op jit(solution)/shard_map/slices/pallas_call | solution.py:63
  20.6 2.1 %collective-permute-start.2 = (f32[1024,128]{1,0:T(8,128)S(1)}, f32[1024,128]{1,0:T(8,128)S(1)}, u32[]{:S(2)}, u32[]{:S(2)}) collective-permute-start(f32[1024,128]{1,0:T(8,128)S(1)} %bitcast.10), channel_id=1, source_target_pairs={{0,9},{1,8},{16,25},{17,24},{32,41},{33,40},{48,57},{49,56},{64,73... | collective-permute-start | bytes 1572872 | tf_op jit(solution)/shard_map/ppermute | solution.py:310
  22.7 0.0 copy-done.1
  22.7 4.0 %collective-permute-start.6 = (f32[2,4,128,512]{3,2,1,0:T(8,128)S(1)}, f32[2,4,128,512]{3,2,1,0:T(8,128)}, u32[]{:S(2)}, u32[]{:S(2)}) collective-permute-start(f32[2,4,128,512]{3,2,1,0:T(8,128)S(1)} %copy-done.1), channel_id=1, source_target_pairs={{0,16},{1,17},{2,18},{3,19},{4,20},{5,21},{6,22},{7,23},{8,24},{9,... | collective-permute-start | bytes 6291464 | tf_op jit(solution)/shard_map/ppermute | solution.py:294
  26.8 4.9 %collective-permute-start.7 = (f32[2,4,128,512]{3,2,1,0:T(8,128)S(1)}, f32[2,4,128,512]{3,2,1,0:T(8,128)}, u32[]{:S(2)}, u32[]{:S(2)}) collective-permute-start(f32[2,4,128,512]{3,2,1,0:T(8,128)S(1)} %copy-done.1), channel_id=1, source_target_pairs={{16,0},{17,1},{18,2},{19,3},{20,4},{21,5},{22,6},{23,7},{24,8},{25... | collective-permute-start | bytes 6291464 | tf_op jit(solution)/shard_map/ppermute | solution.py:294
  31.7 0.0 collective-permute-done.2
  31.7 0.1 bitcast_add_fusion
  31.7 1.3 collective-permute-start.3
  33.1 6.5 %collective-permute-done.3 = f32[1024,128]{1,0:T(8,128)S(1)} collective-permute-done((f32[1024,128]{1,0:T(8,128)S(1)}, f32[1024,128]{1,0:T(8,128)S(1)}, u32[]{:S(2)}, u32[]{:S(2)}) %collective-permute-start.3) | collective-permute-done | bytes 524320 | tf_op jit(solution)/shard_map/ppermute | solution.py:310
  39.5 0.1 add.85
  39.6 1.3 collective-permute-start.4
  40.9 6.1 %collective-permute-done.4 = f32[1024,128]{1,0:T(8,128)S(1)} collective-permute-done((f32[1024,128]{1,0:T(8,128)S(1)}, f32[1024,128]{1,0:T(8,128)S(1)}, u32[]{:S(2)}, u32[]{:S(2)}) %collective-permute-start.4) | collective-permute-done | bytes 524320 | tf_op jit(solution)/shard_map/ppermute | solution.py:310
  47.0 0.1 add.86.held_ref
  47.1 7.9 %collective-permute-start.5 = (f32[1024,128]{1,0:T(8,128)S(1)}, f32[1024,128]{1,0:T(8,128)S(1)}, u32[]{:S(2)}, u32[]{:S(2)}) collective-permute-start(f32[1024,128]{1,0:T(8,128)S(1)} %add.86.held_ref), channel_id=1, source_target_pairs={{4,3},{2,1},{0,15},{14,13},{12,11},{10,9},{8,7},{6,5},{3,4},{1,2},... | collective-permute-start | bytes 1572872 | tf_op jit(solution)/shard_map/ppermute | solution.py:312
  55.0 0.1 pad_add_fusion.place_ref
  55.1 0.0 collective-permute-done.6.low_ref
  55.1 0.0 collective-permute-done.7.high_ref
  55.1 0.0 copy-start.2
  55.1 1.6 %copy-done.2 = f32[2,4,128,512]{3,2,1,0:T(8,128)S(1)} copy-done((f32[2,4,128,512]{3,2,1,0:T(8,128)S(1)}, f32[2,4,128,512]{3,2,1,0:T(8,128)}, u32[]{:S(2)}) %copy-start.2) | copy-done | bytes 2097176
  56.7 5.1 %slices.3.matrix_ref = f32[2,4,128,512]{3,2,1,0:T(8,128)S(1)} custom-call(f32[2,4,128,512]{3,2,1,0:T(8,128)S(1)} %copy-done.2, f32[2,4,128,512]{3,2,1,0:T(8,128)} %collective-permute-done.6.low_ref, f32[2,4,128,512]{3,2,1,0:T(8,128)} %collective-permute-done.7.high_ref, f32[128,128]{1,0:T(8,128)S(1)} %pad.4.coef_ref), custom_call_target="tpu_custom_call" | custom-call | tf_op jit(solution)/shard_map/slices/pallas_call | solution.py:63
  61.8 2.3 %collective-permute-done.5.other_ref = f32[1024,128]{1,0:T(8,128)S(1)} collective-permute-done((f32[1024,128]{1,0:T(8,128)S(1)}, f32[1024,128]{1,0:T(8,128)S(1)}, u32[]{:S(2)}, u32[]{:S(2)}) %collective-permute-start.5) | collective-permute-done | bytes 524320 | tf_op jit(solution)/shard_map/ppermute | solution.py:312
  64.1 3.5 %shared_sums.1 = f32[32,48,128]{2,1,0:T(8,128)S(1)} custom-call(s32[2]{0:T(128)S(1)} %pad_add_fusion.place_ref, f32[1024,128]{1,0:T(8,128)S(1)} %add.86.held_ref, f32[1024,128]{1,0:T(8,128)S(1)} %collective-permute-done.5.other_ref, f32[2,4,128,512]{3,2,1,0:T(8,128)S(1)} %slices.3.matrix_ref), custom_call_target="tpu_custom_call" | custom-call | tf_op jit(solution)/shard_map/shared_sums/pallas_call | solution.py:204
  67.5 33.8 %all_to_all.10 = f32[32,48,128]{2,1,0:T(8,128)} all-to-all(f32[32,48,128]{2,1,0:T(8,128)S(1)} %shared_sums.1), channel_id=1, replica_groups=mesh['row'=32,'col'=16] {'row'}, dimensions={0} | all-to-all | bytes 1572864 | tf_op jit(solution)/shard_map/all_to_all | solution.py:317
  101.3 1.2 reduce_sum.9
  102.5 0.1 broadcast_in_dim.26
  102.6 17.9 %all_to_all.11.sums_ref = f32[32,48,128]{2,1,0:T(8,128)S(1)} all-to-all(f32[32,48,128]{2,1,0:T(8,128)S(1)} %broadcast_in_dim.26), channel_id=1, replica_groups=mesh['row'=32,'col'=16] {'row'}, dimensions={0} | all-to-all | bytes 1572864 | tf_op jit(solution)/shard_map/all_to_all | solution.py:319
  120.4 5.9 %factor_a.1 = (f32[128,128]{1,0:T(8,128)S(1)}, f32[128,128]{1,0:T(8,128)S(1)}, f32[128,128]{1,0:T(8,128)S(1)}) custom-call(f32[32,48,128]{2,1,0:T(8,128)S(1)} %all_to_all.11.sums_ref), custom_call_target="tpu_custom_call" | custom-call | tf_op jit(solution)/shard_map/factor_a/pallas_call | solution.py:163
  126.3 5.8 %factor_b.1.inv_ref = f32[256,256]{1,0:T(8,128)S(1)} custom-call(f32[32,48,128]{2,1,0:T(8,128)S(1)} %all_to_all.11.sums_ref, f32[128,128]{1,0:T(8,128)S(1)} %get-tuple-element.7.rest_ref, f32[128,128]{1,0:T(8,128)S(1)} %get-tuple-element.8.inv0_ref, f32[128,128]{1,0:T(8,128)S(1)} %get-tuple-element.9.cross_ref), custom_call_target="tpu_custom_call" | custom-call | tf_op jit(solution)/shard_map/factor_b/pallas_call | solution.py:163
  132.1 5.3 %finish.1 = (f32[2,4,128,512]{3,2,1,0:T(8,128)}, f32[1,512]{1,0:T(1,128)}) custom-call(s32[2]{0:T(128)S(1)} %pad_add_fusion.place_ref, f32[256,256]{1,0:T(8,128)S(1)} %factor_b.1.inv_ref, f32[32,48,128]{2,1,0:T(8,128)S(1)} %all_to_all.11.sums_ref, f32[1024,128]{1,0:T(8,128)S(1)} %add.86.held_ref, f32[1024,128]{1,0:T(8,128)S(1)} %collective-permute-done.5.other_ref, ...), custom_call_target="tpu_custom_call" | custom-call | tf_op jit(solution)/shard_map/finish/pallas_call | solution.py:256
  (8 shorter events, 0.1 us)
Async XLA Ops:
  0.6 12.2 %copy-start = (s32[4,128,128]{2,1,0:T(8,128)S(1)}, s32[4,128,128]{2,1,0:T(8,128)}, u32[]{:S(2)}) copy-start(s32[4,128,128]{2,1,0:T(8,128)} %param.3) | copy-start | bytes 786436
  1.8 20.9 %copy-start.1 = (f32[2,4,128,512]{3,2,1,0:T(8,128)S(1)}, f32[2,4,128,512]{3,2,1,0:T(8,128)}, u32[]{:S(2)}) copy-start(f32[2,4,128,512]{3,2,1,0:T(8,128)} %vec_ref.1) | copy-start | bytes 6291460
  1.8 11.8 %collective-permute-start.1 = (f32[2,4,128,128]{3,2,1,0:T(8,128)S(1)}, f32[2,4,128,128]{3,2,1,0:T(8,128)S(1)}, u32[]{:S(2)}, u32[]{:S(2)}) collective-permute-start(f32[2,4,128,128]{3,2,1,0:T(8,128)S(1)} %slice.3.vec_ref), channel_id=1, source_target_pairs={{16,0},{17,1},{32,16},{33,17},{48,32},{49,33},{64,48},{65,49},{80,... | collective-permute-start | bytes 1572872 | tf_op jit(solution)/shard_map/ppermute | solution.py:294
  10.7 8.0 %collective-permute-start = (f32[2,4,128,128]{3,2,1,0:T(8,128)S(1)}, f32[2,4,128,128]{3,2,1,0:T(8,128)}, u32[]{:S(2)}, u32[]{:S(2)}) collective-permute-start(f32[2,4,128,128]{3,2,1,0:T(8,128)S(1)} %slice.3.vec_ref), channel_id=1, source_target_pairs={{0,16},{1,17},{16,32},{17,33},{32,48},{33,49},{48,64},{49,65},{64,... | collective-permute-start | bytes 1572872 | tf_op jit(solution)/shard_map/ppermute | solution.py:294
  20.6 11.1 %collective-permute-start.2 = (f32[1024,128]{1,0:T(8,128)S(1)}, f32[1024,128]{1,0:T(8,128)S(1)}, u32[]{:S(2)}, u32[]{:S(2)}) collective-permute-start(f32[1024,128]{1,0:T(8,128)S(1)} %bitcast.10), channel_id=1, source_target_pairs={{0,9},{1,8},{16,25},{17,24},{32,41},{33,40},{48,57},{49,56},{64,73... | collective-permute-start | bytes 1572872 | tf_op jit(solution)/shard_map/ppermute | solution.py:310
  22.7 32.4 %collective-permute-start.6 = (f32[2,4,128,512]{3,2,1,0:T(8,128)S(1)}, f32[2,4,128,512]{3,2,1,0:T(8,128)}, u32[]{:S(2)}, u32[]{:S(2)}) collective-permute-start(f32[2,4,128,512]{3,2,1,0:T(8,128)S(1)} %copy-done.1), channel_id=1, source_target_pairs={{0,16},{1,17},{2,18},{3,19},{4,20},{5,21},{6,22},{7,23},{8,24},{9,... | collective-permute-start | bytes 6291464 | tf_op jit(solution)/shard_map/ppermute | solution.py:294
  26.8 28.3 %collective-permute-start.7 = (f32[2,4,128,512]{3,2,1,0:T(8,128)S(1)}, f32[2,4,128,512]{3,2,1,0:T(8,128)}, u32[]{:S(2)}, u32[]{:S(2)}) collective-permute-start(f32[2,4,128,512]{3,2,1,0:T(8,128)S(1)} %copy-done.1), channel_id=1, source_target_pairs={{16,0},{17,1},{18,2},{19,3},{20,4},{21,5},{22,6},{23,7},{24,8},{25... | collective-permute-start | bytes 6291464 | tf_op jit(solution)/shard_map/ppermute | solution.py:294
  31.7 7.8 %collective-permute-start.3 = (f32[1024,128]{1,0:T(8,128)S(1)}, f32[1024,128]{1,0:T(8,128)S(1)}, u32[]{:S(2)}, u32[]{:S(2)}) collective-permute-start(f32[1024,128]{1,0:T(8,128)S(1)} %bitcast_add_fusion), channel_id=1, source_target_pairs={{0,4},{8,12},{1,13},{9,5},{16,20},{24,28},{17,29},{25,21},{32,36},... | collective-permute-start | bytes 1572872 | tf_op jit(solution)/shard_map/ppermute | solution.py:310
  39.6 7.4 %collective-permute-start.4 = (f32[1024,128]{1,0:T(8,128)S(1)}, f32[1024,128]{1,0:T(8,128)S(1)}, u32[]{:S(2)}, u32[]{:S(2)}) collective-permute-start(f32[1024,128]{1,0:T(8,128)S(1)} %add.85), channel_id=1, source_target_pairs={{1,3},{13,15},{5,7},{9,11},{4,2},{0,14},{8,6},{12,10},{17,19},{29,... | collective-permute-start | bytes 1572872 | tf_op jit(solution)/shard_map/ppermute | solution.py:310
  47.1 17.0 %collective-permute-start.5 = (f32[1024,128]{1,0:T(8,128)S(1)}, f32[1024,128]{1,0:T(8,128)S(1)}, u32[]{:S(2)}, u32[]{:S(2)}) collective-permute-start(f32[1024,128]{1,0:T(8,128)S(1)} %add.86.held_ref), channel_id=1, source_target_pairs={{4,3},{2,1},{0,15},{14,13},{12,11},{10,9},{8,7},{6,5},{3,4},{1,2},... | collective-permute-start | bytes 1572872 | tf_op jit(solution)/shard_map/ppermute | solution.py:312
  55.1 1.6 %copy-start.2 = (f32[2,4,128,512]{3,2,1,0:T(8,128)S(1)}, f32[2,4,128,512]{3,2,1,0:T(8,128)}, u32[]{:S(2)}) copy-start(f32[2,4,128,512]{3,2,1,0:T(8,128)} %vec_ref.1) | copy-start | bytes 6291460
